TPU v7x, 32 devices: a whole 2x2x4 slice. The times are simulated.
32 devices in a mesh: ctx: 8 (over y, x, core), tp: 4 (over z).
Axes of the slice: x: 2, y: 2, z: 4, core: 2. Of those that a mesh axis runs over, the one named last changes fastest.
Arguments:
- inputs: bfloat16 [1024, 2048], P('ctx', 'tp'), may hold values from -6 to 6
- residue: float32 [2048, 16], P('tp'), may hold values from -1.5 to 1.5
- log_rate: float32 [2048, 16], P('tp'), may hold values from -1 to 6.5
- skip: float32 [2048], P('tp'), may hold values from 0.5 to 1.5
- out_weight: bfloat16 [2048, 8192], P('tp'), may hold values from -0.125 to 0.125
- out_grad: bfloat16 [1024, 8192], P(('ctx', 'tp')), may hold values from -6 to 6
Outputs:
- out: bfloat16 [1024, 8192], P(('ctx', 'tp'))
- grad_input: bfloat16 [1024, 2048], P('ctx', 'tp')
- grad_residue: float32 [2048, 16], P('tp')
- grad_log_rate: float32 [2048, 16], P('tp')
- grad_skip: float32 [2048], P('tp')
All inputs are finite; a program needn't handle non-finite values.
Results may differ from a plain program's by a relative error of at most 0.02.
Values may be sent and summed in bfloat16 or wider, within the bound.
No kernel may reach another device: no remote copies, remote signals or barrier semaphores. Data moves between devices by JAX's collectives and lax.ppermute only.
A program may use at most 128 MiB of HBM per device.

v0:
```python
import functools
import math

import jax
import jax.numpy as jnp
from jax import lax
from jax.experimental import pallas as pl
from jax.experimental.pallas import tpu as pltpu
from jax.sharding import PartitionSpec as P

F32 = jnp.float32
BF16 = jnp.bfloat16
STEP = 8
CLEAR_FLOPS = 4_000_000_000
HALVES = 2


def call(body, outs, scratch, args, flops=1024):
    whole = pl.BlockSpec(memory_space=pltpu.VMEM)
    return pl.pallas_call(
        body,
        out_shape=outs,
        in_specs=[whole] * len(args),
        out_specs=[whole] * len(outs),
        scratch_shapes=scratch,
        compiler_params=pltpu.CompilerParams(vmem_limit_bytes=12 << 20),
        cost_estimate=pl.CostEstimate(flops=flops, bytes_accessed=1024, transcendentals=0),
    )(*args)


def row_of(ref, at, like):
    return jnp.broadcast_to(ref[pl.ds(at, 1), :], like.shape)


def part_of(ref, which, modes):
    return ref[pl.ds(which * modes, modes), :]


def clear_body(state_ref):
    state_ref[...] = jnp.zeros_like(state_ref)


def ends_body(seq, x_ref, log_ref, zero_ref, x_f, rate_ref, ends_ref):
    tok = x_ref.shape[0]
    modes = log_ref.shape[0]
    rate = jnp.exp(log_ref[...]) / seq
    a = jnp.exp(-rate)
    rate_ref[...] = rate
    x_f[...] = x_ref[...].astype(F32)

    def steps(block, carry):
        h, q = carry
        for inner in range(STEP):
            ah = a * h
            q = a * q + ah
            h = ah + row_of(x_f, block * STEP + inner, a)
        return h, q

    h, q = lax.fori_loop(0, tok // STEP, steps, (zero_ref[...], zero_ref[...]))
    ends_ref[pl.ds(0, modes), :] = h
    ends_ref[pl.ds(modes, modes), :] = q


def table_body(rate_ref, res_ref, skip_ref, table_ref):
    modes = rate_ref.shape[0]
    rate = rate_ref[...]
    norm = jnp.sqrt(2.0 * rate)
    table_ref[pl.ds(0, modes), :] = rate
    table_ref[pl.ds(modes, modes), :] = norm
    table_ref[pl.ds(2 * modes, modes), :] = res_ref[...] * norm
    table_ref[pl.ds(3 * modes, 8), :] = jnp.broadcast_to(skip_ref[...], (8, rate.shape[1]))


def advance(h, q, a_span, span):
    return a_span * h, a_span * (q + span * h)


def pair_ends_body(tok, modes, rate_ref, own_ref, other_ref, pair_ref):
    second = lax.axis_index("ctx") % 2 == 1
    a_chunk = jnp.exp(-(rate_ref[...] * tok))
    own = part_of(own_ref, 0, modes), part_of(own_ref, 1, modes)
    other = part_of(other_ref, 0, modes), part_of(other_ref, 1, modes)
    early = [jnp.where(second, theirs, ours) for ours, theirs in zip(own, other)]
    late = [jnp.where(second, ours, theirs) for ours, theirs in zip(own, other)]
    h, q = advance(*early, a_chunk, tok)
    pair_ref[pl.ds(0, modes), :] = (h + late[0]).astype(BF16)
    pair_ref[pl.ds(modes, modes), :] = (q + late[1]).astype(BF16)


def merged_body(modes, x_f, table_ref, other_ref, *refs):
    *far_refs, merged_ref, start_ref, y_f = refs
    tok = x_f.shape[0]
    rate = part_of(table_ref, 0, modes)
    c = part_of(table_ref, 2, modes)
    a = jnp.exp(-rate)
    a_chunk = jnp.exp(-(rate * tok))
    index = lax.axis_index("ctx")
    pair = index // 2
    h = jnp.zeros_like(a)
    q = jnp.zeros_like(a)
    for j, far in enumerate(far_refs, 1):
        apart = pair - (pair ^ j)
        since = (jnp.maximum(apart - 1, 0) * (2 * tok)).astype(F32)
        far_h, far_q = part_of(far, 0, modes).astype(F32), part_of(far, 1, modes).astype(F32)
        far_h, far_q = advance(far_h, far_q, jnp.exp(-(rate * since)), since)
        h = h + jnp.where(apart > 0, far_h, 0.0)
        q = q + jnp.where(apart > 0, far_q, 0.0)
    h_late, q_late = advance(h, q, a_chunk, tok)
    second = index % 2 == 1
    h = jnp.where(second, h_late + part_of(other_ref, 0, modes), h)
    q = jnp.where(second, q_late + part_of(other_ref, 1, modes), q)
    start_ref[pl.ds(0, modes), :] = h
    start_ref[pl.ds(modes, modes), :] = q

    def steps(block, h):
        for inner in range(STEP):
            at = block * STEP + inner
            h = a * h + row_of(x_f, at, a)
            y_f[pl.ds(at, 1), :] = jnp.sum(c * h, axis=0, keepdims=True)
        return h

    lax.fori_loop(0, tok // STEP, steps, h)
    merged_ref[...] = (y_f[...] + table_ref[pl.ds(3 * modes, 1), :] * x_f[...]).astype(BF16)


def states_body(modes, x_f, table_ref, start_ref, h_ref, q_ref):
    tok = x_f.shape[0]
    a = jnp.exp(-part_of(table_ref, 0, modes))

    def steps(block, carry):
        h, q = carry
        for inner in range(STEP):
            at = block * STEP + inner
            ah = a * h
            q = a * q + ah
            h = ah + row_of(x_f, at, a)
            to = pl.ds(pl.multiple_of(at * modes, 8), modes)
            h_ref[to, :] = h
            q_ref[to, :] = q
        return h, q

    lax.fori_loop(0, tok // STEP, steps, (part_of(start_ref, 0, modes), part_of(start_ref, 1, modes)))


def grads_body(modes, rows, places_of, x_f, table_ref, h_ref, q_ref, *refs):
    *g_refs, g_f, sums_ref = refs
    tok = x_f.shape[0]
    rate = part_of(table_ref, 0, modes)
    a = jnp.exp(-rate)
    places = places_of()
    slot = 0
    for g_ref in g_refs:
        for at in range(g_ref.shape[0] // rows):
            to = pl.multiple_of(places[slot] * rows, 8)
            g_f[pl.ds(to, rows), :] = g_ref[pl.ds(at * rows, rows), :].astype(BF16).astype(F32)
            slot += 1

    def steps(block, carry):
        power, back, by_res, by_rate = carry
        for inner in range(STEP):
            at = block * STEP + inner
            g = row_of(g_f, at, a)
            to = pl.ds(pl.multiple_of(at * modes, 8), modes)
            back = back + power * g
            power = power * a
            by_res = by_res + g * h_ref[to, :]
            by_rate = by_rate + g * q_ref[to, :]
        return power, back, by_res, by_rate

    zero = jnp.zeros_like(a)
    _, back, by_res, by_rate = lax.fori_loop(0, tok // STEP, steps, (jnp.ones_like(a), zero, zero, zero))
    sums_ref[pl.ds(0, modes), :] = back
    sums_ref[pl.ds(modes, modes), :] = by_res
    sums_ref[pl.ds(2 * modes, modes), :] = 0.5 * by_res - rate * by_rate
    direct = jnp.sum(g_f[...] * x_f[...], axis=0, keepdims=True)
    sums_ref[pl.ds(3 * modes, 8), :] = jnp.broadcast_to(direct, (8, direct.shape[1]))


def pair_sums_body(tok, modes, table_ref, own_ref, other_ref, pair_ref):
    second = lax.axis_index("ctx") % 2 == 1
    a_chunk = jnp.exp(-(part_of(table_ref, 0, modes) * tok))
    own = part_of(own_ref, 0, modes)
    other = part_of(other_ref, 0, modes)
    early = jnp.where(second, other, own)
    late = jnp.where(second, own, other)
    pair_ref[pl.ds(0, modes), :] = (early + a_chunk * late).astype(BF16)
    both = pl.ds(modes, 2 * modes)
    pair_ref[both, :] = (own_ref[both, :] + other_ref[both, :]).astype(BF16)
    direct = own_ref[pl.ds(3 * modes, 1), :] + other_ref[pl.ds(3 * modes, 1), :]
    pair_ref[pl.ds(3 * modes, modes), :] = jnp.broadcast_to(direct, own.shape).astype(BF16)


def input_body(seq, modes, g_f, table_ref, other_ref, pair_ref, *refs):
    *far_refs, grad_ref, by_res_ref, by_log_ref, by_skip_ref, y_f = refs
    tok = g_f.shape[0]
    rate = part_of(table_ref, 0, modes)
    norm = part_of(table_ref, 1, modes)
    c = part_of(table_ref, 2, modes)
    a = jnp.exp(-rate)
    a_chunk = jnp.exp(-(rate * tok))
    index = lax.axis_index("ctx")
    pair = index // 2
    z = jnp.zeros_like(a)
    for j, far in enumerate(far_refs, 1):
        apart = (pair ^ j) - pair
        until = (jnp.maximum(apart - 1, 0) * (2 * tok)).astype(F32)
        decay = jnp.exp(-(rate * until))
        z = z + jnp.where(apart > 0, decay * far[pl.ds(0, modes), :].astype(F32), 0.0)
    z = jnp.where(index % 2 == 0, a_chunk * z + part_of(other_ref, 0, modes), z)

    def steps(block, z):
        for inner in range(STEP):
            at = tok - 1 - (block * STEP + inner)
            z = a * z + row_of(g_f, at, a)
            y_f[pl.ds(at, 1), :] = jnp.sum(c * z, axis=0, keepdims=True)
        return z

    lax.fori_loop(0, tok // STEP, steps, z)
    grad_ref[...] = (y_f[...] + table_ref[pl.ds(3 * modes, 1), :] * g_f[...]).astype(BF16)
    rest = pl.ds(modes, 3 * modes)
    total = pair_ref[rest, :].astype(F32)
    for far in far_refs:
        total = total + far[rest, :].astype(F32)
    scale = 1.0 / math.sqrt(seq)
    by_res_ref[...] = scale * (norm * total[:modes])
    by_log_ref[...] = scale * (c * total[modes:2 * modes])
    by_skip_ref[...] = scale * total[2 * modes:2 * modes + 1]


def from_other_core(array, blocks):
    return lax.ppermute(array, "ctx", [(i, i ^ 1) for i in range(blocks)])


def from_pairs(array, blocks):
    return [lax.ppermute(array, "ctx", [(i, i ^ (2 * j)) for i in range(blocks)]) for j in range(1, blocks // 2)]


def outer(array):
    return lax.ppermute(array, "tp", [(0, 1), (1, 0), (2, 3), (3, 2)])


def inner(array):
    return lax.ppermute(array, "tp", [(1, 2), (2, 1), (0, 0), (3, 3)])


def back_dot(rows_in, weight):
    return lax.dot_general(rows_in, weight, (((1,), (1,)), ((), ())), preferred_element_type=F32)


def at_end():
    index = lax.axis_index("tp")
    return (index == 0) | (index == 3)


def inward(far):
    low = lax.axis_index("tp") < 2
    return jnp.where(low, 3, 0) if far else jnp.where(low, 2, 1)


def share_body(span, merged_ref, weight_ref, share_ref):
    cut = share_ref.shape[1]
    tile = min(cut, 512)
    merged = merged_ref[...]
    for at in range(0, cut, tile):
        weight = weight_ref[:, span.start + at:span.start + at + tile]
        share_ref[:, at:at + tile] = jnp.dot(merged, weight, preferred_element_type=F32).astype(BF16)


def share_rows(share_ref, at, rows):
    return share_ref[pl.ds(pl.multiple_of(at * rows, 16), rows), :]


def send_body(span, far, share_ref, passing_ref, out_ref):
    rows = out_ref.shape[0]
    end = at_end()

    @pl.when(end)
    def _():
        out_ref[...] = share_rows(share_ref, inward(far), rows)

    @pl.when(jnp.logical_not(end))
    def _():
        out_ref[...] = passing_ref[:, span]


def back_tiles(rows_ref, weight_ref, start):
    width = rows_ref.shape[1]
    tile = min(width, 1024)
    total = None
    for at in range(0, width, tile):
        part = back_dot(rows_ref[:, at:at + tile], weight_ref[:, start + at:start + at + tile])
        total = part if total is None else total + part
    return total


def near_body(own_ref, beside_ref, weight_ref, g_ref, rows_ref):
    rows = own_ref.shape[0]
    rows_ref[pl.ds(0, rows), :] = own_ref[...]
    rows_ref[pl.ds(rows, rows), :] = beside_ref[...]
    g_ref[...] = back_tiles(rows_ref, weight_ref, 0)


def far_body(span, second_ref, third_ref, across_ref, far_ref, weight_ref, *refs):
    *before_refs, g_ref, rows_ref = refs
    rows = second_ref.shape[0]
    end = at_end()

    @pl.when(end)
    def _():
        rows_ref[pl.ds(0, rows), :] = second_ref[...]
        rows_ref[pl.ds(rows, rows), :] = third_ref[...]

    @pl.when(jnp.logical_not(end))
    def _():
        rows_ref[pl.ds(0, rows), :] = across_ref[:, span]
        rows_ref[pl.ds(rows, rows), :] = far_ref[...]

    total = back_tiles(rows_ref, weight_ref, span.start)
    for before in before_refs:
        total = total + before[...]
    g_ref[...] = total


def add_body(far, share_ref, got_ref, out_ref):
    rows = out_ref.shape[0]
    block = share_rows(share_ref, inward(far), rows).astype(F32)
    out_ref[...] = (block + got_ref[...].astype(F32)).astype(BF16)


def add_whole_body(spans, *refs):
    *in_refs, out_ref = refs
    rows = out_ref.shape[0]
    for at, span in enumerate(spans):
        share_ref, got_ref = in_refs[2 * at:2 * at + 2]
        block = share_rows(share_ref, inward(False), rows).astype(F32)
        out_ref[:, span] = (block + got_ref[...].astype(F32)).astype(BF16)


def last_body(spans, *refs):
    *done_refs, share_ref, got_ref, out_ref = refs
    rows = share_ref.shape[0] // 4
    end = at_end()
    for done_ref, span in zip(done_refs, spans):
        out_ref[:, span] = done_ref[...]
    block = share_rows(share_ref, lax.axis_index("tp") ^ 1, rows).astype(F32)
    out_ref[:, spans[-1]] = (block + jnp.where(end, 0.0, got_ref[...].astype(F32))).astype(BF16)


def total_body(spans, *refs):
    *share_refs, last_ref, near_ref, out_ref = refs
    rows = out_ref.shape[0]
    end = at_end()
    for share_ref, span in zip(share_refs, spans):
        total = share_rows(share_ref, lax.axis_index("tp"), rows).astype(F32) + last_ref[:, span].astype(F32)
        out_ref[:, span] = (total + jnp.where(end, 0.0, near_ref[:, span].astype(F32))).astype(BF16)


def line_of_four(out_grad, out_weight, merged, x_f, states_of, grads_of):
    rows, width = out_grad.shape
    cut = width // HALVES
    spans = [slice(at * cut, (at + 1) * cut) for at in range(HALVES)]
    piece = [jax.ShapeDtypeStruct((rows, cut), BF16)]
    whole = [jax.ShapeDtypeStruct((rows, width), BF16)]
    pairs_of = lambda ones, twos: [ref for pair in zip(ones, twos) for ref in pair]

    across = inner(out_grad)
    beside = outer(out_grad)

    shares = []
    second = []
    for span in spans:
        (share,) = call(
            functools.partial(share_body, span), [jax.ShapeDtypeStruct((merged.shape[0], cut), BF16)], [],
            [merged, out_weight],
        )
        shares.append(share)
        (part,) = call(functools.partial(send_body, span, True), piece, [], [share, across])
        second.append(outer(part))
        merged = lax.optimization_barrier((merged, part))[0]
    beside = lax.optimization_barrier((beside, part))[0]
    across_far = [inner(beside[:, span]) for span in spans]
    g_rows = [jax.ShapeDtypeStruct((2 * rows, out_weight.shape[0]), F32)]
    (g_near,) = call(near_body, g_rows, [pltpu.VMEM((2 * rows, width), BF16)], [out_grad, beside, out_weight])
    second[0] = lax.optimization_barrier((second[0], g_near))[0]
    third = []
    to_far = []
    for at in range(HALVES):
        (sent,) = call(functools.partial(add_body, True), piece, [], [shares[at], second[at]])
        to_far.append(inner(sent))
        far = lax.optimization_barrier((across_far[at], sent))[0]
        (sent,) = call(functools.partial(send_body, slice(None), False), piece, [], [shares[at], far])
        third.append(outer(sent))
        if at + 1 < HALVES:
            states = states_of(lax.optimization_barrier((x_f, sent))[0])
            second[at + 1] = lax.optimization_barrier((second[at + 1], *states))[0]
    g_far = []
    ready = []
    for at, span in enumerate(spans):
        g_far = call(
            functools.partial(far_body, span), g_rows, [pltpu.VMEM((2 * rows, cut), BF16)],
            [second[at], third[at], across, across_far[at], out_weight, *g_far],
        )
        if at == 0:
            got = lax.optimization_barrier((to_far[0], *g_far))[0]
            ready = call(functools.partial(last_body, [slice(None)]), piece, [], [shares[0], got])
            third[-1] = lax.optimization_barrier((third[-1], *ready))[0]
    ready = call(functools.partial(last_body, spans), whole, [], [*ready, shares[-1], to_far[-1]])[0]
    (near,) = call(functools.partial(add_whole_body, spans), whole, [], pairs_of(shares, third))
    ready, near, *g_far = lax.optimization_barrier((ready, near, *g_far))

    def places():
        at = lax.axis_index("tp")
        return [at, at ^ 1, inward(False), inward(True)]

    g_f, sums = grads_of([g_near, *g_far], places, states)
    last = outer(ready)
    to_near = inner(near)
    (out,) = call(functools.partial(total_body, spans), whole, [], [*shares, last, to_near])
    return out, g_f, sums


def any_axis(out_grad, out_weight, merged, x_f, states_of, grads_of):
    parts = lax.axis_size("tp")
    gathered = lax.all_gather(out_grad, "tp", axis=0, tiled=True)
    share = jnp.dot(merged, out_weight, preferred_element_type=F32).astype(BF16)
    out = lax.psum_scatter(share, "tp", scatter_dimension=0, tiled=True)
    return out, *grads_of([back_dot(gathered, out_weight)], lambda: list(range(parts)), states_of(x_f))


def per_device(inputs, residue, log_rate, skip, out_weight, out_grad):
    blocks = lax.axis_size("ctx")
    parts = lax.axis_size("tp")
    tok, chans = inputs.shape
    seq = blocks * tok
    rows = out_grad.shape[0]
    modes = residue.shape[1]
    lanes = functools.partial(jax.ShapeDtypeStruct, dtype=F32)
    state = lanes((modes, chans))
    token_f = pltpu.VMEM((tok, chans), F32)

    (zero,) = call(clear_body, [state], [], [], flops=CLEAR_FLOPS)
    out_grad = lax.optimization_barrier((out_grad, zero))[0]
    x_f, rate, ends = call(
        functools.partial(ends_body, seq), [lanes((tok, chans)), state, lanes((2 * modes, chans))], [],
        [inputs, log_rate.T, zero],
    )
    (table,) = call(
        table_body, [lanes((3 * modes + 8, chans))], [], [rate, residue.T, skip[None, :]], flops=1_000_000_000
    )
    other_ends = from_other_core(ends, blocks)
    (pair_ends,) = call(
        functools.partial(pair_ends_body, tok, modes), [jax.ShapeDtypeStruct((2 * modes, chans), BF16)], [],
        [rate, ends, other_ends],
    )
    merged, start = call(
        functools.partial(merged_body, modes),
        [jax.ShapeDtypeStruct((tok, chans), BF16), lanes((2 * modes, chans))],
        [token_f], [x_f, table, other_ends, *from_pairs(pair_ends, blocks)],
    )

    def states_of(x_f):
        return call(
            functools.partial(states_body, modes), [lanes((tok * modes, chans))] * 2, [], [x_f, table, start]
        )

    def grads_of(pieces, places, states):
        return call(
            functools.partial(grads_body, modes, rows, places), [lanes((tok, chans)), lanes((3 * modes + 8, chans))], [],
            [x_f, table, *states, *pieces],
        )

    reduce = line_of_four if parts == 4 else any_axis
    out, g_f, sums = reduce(out_grad, out_weight, merged, x_f, states_of, grads_of)
    other_sums = from_other_core(sums, blocks)
    (pair_sums,) = call(
        functools.partial(pair_sums_body, tok, modes), [jax.ShapeDtypeStruct((4 * modes, chans), BF16)], [],
        [table, sums, other_sums],
    )
    grad_input, by_res, by_log, by_skip = call(
        functools.partial(input_body, seq, modes),
        [jax.ShapeDtypeStruct((tok, chans), BF16), state, state, lanes((1, chans))], [token_f],
        [g_f, table, other_sums, pair_sums, *from_pairs(pair_sums, blocks)],
    )
    return out, grad_input, by_res.T, by_log.T, by_skip[0]


def solution(mesh):
    placed = (
        P("ctx", "tp"),
        P("tp", None),
        P("tp", None),
        P("tp"),
        P("tp", None),
        P(("ctx", "tp"), None),
    )
    return jax.shard_map(
        per_device,
        mesh=mesh,
        in_specs=placed,
        out_specs=(P(("ctx", "tp"), None), P("ctx", "tp"), P("tp", None), P("tp", None), P("tp")),
        check_vma=False,
    )
```

profile of v0, /device:TPU:0, one launch (start us, length us, event | category | flops | bytes accessed | tf_op | source)
XLA Modules:
  0.0 61.2 jit_solution(3501345723706840960)
XLA Ops:
  0.7 1.0 %copy-done.1 = bf16[32,8192]{1,0:T(8,128)(2,1)S(1)} copy-done((bf16[32,8192]{1,0:T(8,128)(2,1)S(1)}, bf16[32,8192]{1,0:T(8,128)(2,1)}, u32[]{:S(2)}) %copy-start.1) | copy-done | bytes 524312
  1.7 0.8 %collective-permute-start.4 = (bf16[32,8192]{1,0:T(8,128)(2,1)S(1)}, bf16[32,8192]{1,0:T(8,128)(2,1)S(1)}, u32[]{:S(2)}, u32[]{:S(2)}) collective-permute-start(bf16[32,8192]{1,0:T(8,128)(2,1)S(1)} %copy-done.1), channel_id=1, source_target_pairs={{1,2},{2,1},{0,0},{3,3},{5,6},{6,5},{4,4},{7,7},{9,10},{10,9},{8,8... | collective-permute-start | bytes 1572872 | tf_op jit(solution)/shard_map/ppermute | solution.py:243
  2.5 6.0 %collective-permute-start.6 = (bf16[32,8192]{1,0:T(8,128)(2,1)S(1)}, bf16[32,8192]{1,0:T(8,128)(2,1)S(1)}, u32[]{:S(2)}, u32[]{:S(2)}) collective-permute-start(bf16[32,8192]{1,0:T(8,128)(2,1)S(1)} %copy-done.1), channel_id=1, source_target_pairs={{0,1},{1,0},{2,3},{3,2},{4,5},{5,4},{6,7},{7,6},{8,9},{9,8},{10,11... | collective-permute-start | bytes 1572872 | tf_op jit(solution)/shard_map/ppermute | solution.py:239
  9.2 1.2 %collective-permute-done.other_ref = f32[32,512]{1,0:T(8,128)S(1)} collective-permute-done((f32[32,512]{1,0:T(8,128)S(1)}, f32[32,512]{1,0:T(8,128)S(1)}, u32[]{:S(2)}, u32[]{:S(2)}) %collective-permute-start) | collective-permute-done | bytes 65568 | tf_op jit(solution)/shard_map/ppermute | solution.py:231
  10.5 2.5 %collective-permute-start.3 = (bf16[32,512]{1,0:T(8,128)(2,1)S(1)}, bf16[32,512]{1,0:T(8,128)(2,1)S(1)}, u32[]{:S(2)}, u32[]{:S(2)}) collective-permute-start(bf16[32,512]{1,0:T(8,128)(2,1)S(1)} %shard_map.104), channel_id=1, source_target_pairs={{0,24},{4,28},{8,16},{12,20},{16,8},{20,12},{24,0},{28,4},{1,25},{... | collective-permute-start | bytes 98312 | tf_op jit(solution)/shard_map/ppermute | solution.py:235
  14.1 1.3 %collective-permute-done.3.refs_2_ = bf16[32,512]{1,0:T(8,128)(2,1)S(1)} collective-permute-done((bf16[32,512]{1,0:T(8,128)(2,1)S(1)}, bf16[32,512]{1,0:T(8,128)(2,1)S(1)}, u32[]{:S(2)}, u32[]{:S(2)}) %collective-permute-start.3) | collective-permute-done | bytes 32800 | tf_op jit(solution)/shard_map/ppermute | solution.py:235
  15.4 1.5 %collective-permute-done.2.refs_1_ = bf16[32,512]{1,0:T(8,128)(2,1)S(1)} collective-permute-done((bf16[32,512]{1,0:T(8,128)(2,1)S(1)}, bf16[32,512]{1,0:T(8,128)(2,1)S(1)}, u32[]{:S(2)}, u32[]{:S(2)}) %collective-permute-start.2) | collective-permute-done | bytes 32800 | tf_op jit(solution)/shard_map/ppermute | solution.py:235
  17.4 1.2 %shard_map.105 = (bf16[128,512]{1,0:T(8,128)(2,1)S(1)}, f32[32,512]{1,0:T(8,128)S(1)}) custom-call(f32[128,512]{1,0:T(8,128)S(1)} %get-tuple-element.41.x_f, f32[56,512]{1,0:T(8,128)S(1)} %shard_map.103.table_ref, f32[32,512]{1,0:T(8,128)S(1)} %collective-permute-done.other_ref, bf16[32,512]{1,0:T(8,128)(2,1)S(1)} %collective-permute-done.1.refs_0_, ...), custom_call_target="tpu_custom_call" | custom-call | flops 1024 | bytes 1024 | tf_op jit(solution)/shard_map/pallas_call | solution.py:20
  18.7 0.7 %shard_map.106.share_ref.refs_0_ = bf16[128,4096]{1,0:T(8,128)(2,1)S(1)} custom-call(bf16[128,512]{1,0:T(8,128)(2,1)S(1)} %get-tuple-element.36.merged_ref, bf16[512,8192]{1,0:T(8,128)(2,1)S(1)} %copy-done), custom_call_target="tpu_custom_call" | custom-call | flops 1024 | bytes 1024 | tf_op jit(solution)/shard_map/pallas_call | solution.py:20
  19.4 0.7 %shard_map.108.share_ref.refs_1_.refs_2_ = bf16[128,4096]{1,0:T(8,128)(2,1)S(1)} custom-call(bf16[128,512]{1,0:T(8,128)(2,1)S(1)} %get-tuple-element.36.merged_ref, bf16[512,8192]{1,0:T(8,128)(2,1)S(1)} %copy-done), custom_call_target="tpu_custom_call" | custom-call | flops 1024 | bytes 1024 | tf_op jit(solution)/shard_map/pallas_call | solution.py:20
  20.2 1.2 %collective-permute-start.5 = (bf16[32,4096]{1,0:T(8,128)(2,1)S(1)}, bf16[32,4096]{1,0:T(8,128)(2,1)S(1)}, u32[]{:S(2)}, u32[]{:S(2)}) collective-permute-start(bf16[32,4096]{1,0:T(8,128)(2,1)S(1)} %shard_map.107), channel_id=1, source_target_pairs={{0,1},{1,0},{2,3},{3,2},{4,5},{5,4},{6,7},{7,6},{8,9},{9,8},{10,11... | collective-permute-start | bytes 786440 | tf_op jit(solution)/shard_map/ppermute | solution.py:239
  22.1 2.9 %collective-permute-start.10 = (bf16[32,4096]{1,0:T(8,128)(2,1)S(1)}, bf16[32,4096]{1,0:T(8,128)(2,1)S(1)}, u32[]{:S(2)}, u32[]{:S(2)}) collective-permute-start(bf16[32,4096]{1,0:T(8,128)(2,1)S(1)} %shard_map.109), channel_id=1, source_target_pairs={{0,1},{1,0},{2,3},{3,2},{4,5},{5,4},{6,7},{7,6},{8,9},{9,8},{10,11... | collective-permute-start | bytes 786440 | tf_op jit(solution)/shard_map/ppermute | solution.py:239
  25.7 2.6 %shard_map.110.refs_0_ = f32[64,512]{1,0:T(8,128)S(1)} custom-call(bf16[32,8192]{1,0:T(8,128)(2,1)S(1)} %copy-done.1, bf16[32,8192]{1,0:T(8,128)(2,1)S(1)} %collective-permute-done.6.beside_ref, bf16[512,8192]{1,0:T(8,128)(2,1)S(1)} %copy-done), custom_call_target="tpu_custom_call" | custom-call | flops 1024 | bytes 1024 | tf_op jit(solution)/shard_map/pallas_call | solution.py:20
  28.3 1.2 %collective-permute-done.5.got_ref.second_ref = bf16[32,4096]{1,0:T(8,128)(2,1)S(1)} collective-permute-done((bf16[32,4096]{1,0:T(8,128)(2,1)S(1)}, bf16[32,4096]{1,0:T(8,128)(2,1)S(1)}, u32[]{:S(2)}, u32[]{:S(2)}) %collective-permute-start.5) | collective-permute-done | bytes 262176 | tf_op jit(solution)/shard_map/ppermute | solution.py:239
  29.6 0.7 %collective-permute-start.7 = (bf16[32,4096]{1,0:T(8,128)(2,1)S(1)}, bf16[32,4096]{1,0:T(8,128)(2,1)S(1)}, u32[]{:S(2)}, u32[]{:S(2)}) collective-permute-start(bf16[32,4096]{1,0:T(8,128)(2,1)S(1)} %shard_map.111), channel_id=1, source_target_pairs={{1,2},{2,1},{0,0},{3,3},{5,6},{6,5},{4,4},{7,7},{9,10},{10,9},{8,8... | collective-permute-start | bytes 786440 | tf_op jit(solution)/shard_map/ppermute | solution.py:243
  30.3 4.0 %collective-permute-start.9 = (bf16[32,4096]{1,0:T(8,128)(2,1)S(1)}, bf16[32,4096]{1,0:T(8,128)(2,1)S(1)}, u32[]{:S(2)}, u32[]{:S(2)}) collective-permute-start(bf16[32,4096]{1,0:T(8,128)(2,1)S(1)} %shard_map.112), channel_id=1, source_target_pairs={{0,1},{1,0},{2,3},{3,2},{4,5},{5,4},{6,7},{7,6},{8,9},{9,8},{10,11... | collective-permute-start | bytes 786440 | tf_op jit(solution)/shard_map/ppermute | solution.py:239
  34.3 0.9 %shard_map.115 = (f32[2048,512]{1,0:T(8,128)S(1)}, f32[2048,512]{1,0:T(8,128)S(1)}) custom-call(f32[128,512]{1,0:T(8,128)S(1)} %get-tuple-element.41.x_f, f32[56,512]{1,0:T(8,128)S(1)} %shard_map.103.table_ref, f32[32,512]{1,0:T(8,128)S(1)} %get-tuple-element.42.start_ref), custom_call_target="tpu_custom_call" | custom-call | flops 1024 | bytes 1024 | tf_op jit(solution)/shard_map/pallas_call | solution.py:20
  35.3 3.8 %collective-permute-start.13 = (bf16[32,4096]{1,0:T(8,128)(2,1)S(1)}, bf16[32,4096]{1,0:T(8,128)(2,1)S(1)}, u32[]{:S(2)}, u32[]{:S(2)}) collective-permute-start(bf16[32,4096]{1,0:T(8,128)(2,1)S(1)} %shard_map.118), channel_id=1, source_target_pairs={{0,1},{1,0},{2,3},{3,2},{4,5},{5,4},{6,7},{7,6},{8,9},{9,8},{10,11... | collective-permute-start | bytes 786440 | tf_op jit(solution)/shard_map/ppermute | solution.py:239
  39.9 1.4 %collective-permute-done.9.third_ref.refs_1_ = bf16[32,4096]{1,0:T(8,128)(2,1)S(1)} collective-permute-done((bf16[32,4096]{1,0:T(8,128)(2,1)S(1)}, bf16[32,4096]{1,0:T(8,128)(2,1)S(1)}, u32[]{:S(2)}, u32[]{:S(2)}) %collective-permute-start.9) | collective-permute-done | bytes 262176 | tf_op jit(solution)/shard_map/ppermute | solution.py:239
  41.2 1.4 %shard_map.113.refs_0_ = f32[64,512]{1,0:T(8,128)S(1)} custom-call(bf16[32,4096]{1,0:T(8,128)(2,1)S(1)} %collective-permute-done.5.got_ref.second_ref, bf16[32,4096]{1,0:T(8,128)(2,1)S(1)} %collective-permute-done.9.third_ref.refs_1_, bf16[32,8192]{1,0:T(8,128)(2,1)S(1)} %collective-permute-done.4.passing_ref.across_ref, ...), custom_call_target="tpu_custom_call" | custom-call | flops 1024 | bytes 1024 | tf_op jit(solution)/shard_map/pallas_call | solution.py:20
  42.8 1.3 %collective-permute-done.13.refs_3_.third_ref = bf16[32,4096]{1,0:T(8,128)(2,1)S(1)} collective-permute-done((bf16[32,4096]{1,0:T(8,128)(2,1)S(1)}, bf16[32,4096]{1,0:T(8,128)(2,1)S(1)}, u32[]{:S(2)}, u32[]{:S(2)}) %collective-permute-start.13) | collective-permute-done | bytes 262176 | tf_op jit(solution)/shard_map/ppermute | solution.py:239
  44.0 1.4 %shard_map.120.refs_1_ = f32[64,512]{1,0:T(8,128)S(1)} custom-call(bf16[32,4096]{1,0:T(8,128)(2,1)S(1)} %collective-permute-done.10.got_ref.second_ref, bf16[32,4096]{1,0:T(8,128)(2,1)S(1)} %collective-permute-done.13.refs_3_.third_ref, bf16[32,8192]{1,0:T(8,128)(2,1)S(1)} %collective-permute-done.4.passing_ref.across_ref, ...), custom_call_target="tpu_custom_call" | custom-call | flops 1024 | bytes 1024 | tf_op jit(solution)/shard_map/pallas_call | solution.py:20
  45.7 2.2 %collective-permute-start.14 = (bf16[32,8192]{1,0:T(8,128)(2,1)S(1)}, bf16[32,8192]{1,0:T(8,128)(2,1)S(1)}, u32[]{:S(2)}, u32[]{:S(2)}) collective-permute-start(bf16[32,8192]{1,0:T(8,128)(2,1)S(1)} %shard_map.117), channel_id=1, source_target_pairs={{0,1},{1,0},{2,3},{3,2},{4,5},{5,4},{6,7},{7,6},{8,9},{9,8},{10,11... | collective-permute-start | bytes 1572872 | tf_op jit(solution)/shard_map/ppermute | solution.py:239
  47.9 0.7 %collective-permute-start.15 = (bf16[32,8192]{1,0:T(8,128)(2,1)S(1)}, bf16[32,8192]{1,0:T(8,128)(2,1)S(1)}, u32[]{:S(2)}, u32[]{:S(2)}) collective-permute-start(bf16[32,8192]{1,0:T(8,128)(2,1)S(1)} %shard_map.119), channel_id=1, source_target_pairs={{1,2},{2,1},{0,0},{3,3},{5,6},{6,5},{4,4},{7,7},{9,10},{10,9},{8,8... | collective-permute-start | bytes 1572872 | tf_op jit(solution)/shard_map/ppermute | solution.py:243
  48.6 1.2 %shard_map.122 = (f32[128,512]{1,0:T(8,128)S(1)}, f32[56,512]{1,0:T(8,128)S(1)}) custom-call(f32[128,512]{1,0:T(8,128)S(1)} %get-tuple-element.41.x_f, f32[56,512]{1,0:T(8,128)S(1)} %shard_map.103.table_ref, f32[2048,512]{1,0:T(8,128)S(1)} %get-tuple-element.43.h_ref, f32[2048,512]{1,0:T(8,128)S(1)} %get-tuple-element.44.q_ref, ...), custom_call_target="tpu_custom_call" | custom-call | flops 1024 | bytes 1024 | tf_op jit(solution)/shard_map/pallas_call | solution.py:20
  49.9 1.3 %collective-permute-done.16.other_ref = f32[56,512]{1,0:T(8,128)S(1)} collective-permute-done((f32[56,512]{1,0:T(8,128)S(1)}, f32[56,512]{1,0:T(8,128)S(1)}, u32[]{:S(2)}, u32[]{:S(2)}) %collective-permute-start.16) | collective-permute-done | bytes 114720 | tf_op jit(solution)/shard_map/ppermute | solution.py:231
  51.2 2.3 %collective-permute-start.19 = (bf16[64,512]{1,0:T(8,128)(2,1)S(1)}, bf16[64,512]{1,0:T(8,128)(2,1)S(1)}, u32[]{:S(2)}, u32[]{:S(2)}) collective-permute-start(bf16[64,512]{1,0:T(8,128)(2,1)S(1)} %shard_map.123.pair_ref), channel_id=1, source_target_pairs={{0,24},{4,28},{8,16},{12,20},{16,8},{20,12},{24,0},{28,4},{1,25},{... | collective-permute-start | bytes 196616 | tf_op jit(solution)/shard_map/ppermute | solution.py:235
  54.0 0.8 %collective-permute-start.17 = (bf16[64,512]{1,0:T(8,128)(2,1)S(1)}, bf16[64,512]{1,0:T(8,128)(2,1)S(1)}, u32[]{:S(2)}, u32[]{:S(2)}) collective-permute-start(bf16[64,512]{1,0:T(8,128)(2,1)S(1)} %shard_map.123.pair_ref), channel_id=1, source_target_pairs={{0,8},{4,12},{8,0},{12,4},{16,24},{20,28},{24,16},{28,20},{1,9},{5... | collective-permute-start | bytes 196616 | tf_op jit(solution)/shard_map/ppermute | solution.py:235
  54.8 1.7 %collective-permute-done.19.refs_2_ = bf16[64,512]{1,0:T(8,128)(2,1)S(1)} collective-permute-done((bf16[64,512]{1,0:T(8,128)(2,1)S(1)}, bf16[64,512]{1,0:T(8,128)(2,1)S(1)}, u32[]{:S(2)}, u32[]{:S(2)}) %collective-permute-start.19) | collective-permute-done | bytes 65568 | tf_op jit(solution)/shard_map/ppermute | solution.py:235
  56.5 1.4 %collective-permute-done.18.refs_1_ = bf16[64,512]{1,0:T(8,128)(2,1)S(1)} collective-permute-done((bf16[64,512]{1,0:T(8,128)(2,1)S(1)}, bf16[64,512]{1,0:T(8,128)(2,1)S(1)}, u32[]{:S(2)}, u32[]{:S(2)}) %collective-permute-start.18) | collective-permute-done | bytes 65568 | tf_op jit(solution)/shard_map/ppermute | solution.py:235
  58.3 1.9 %shard_map.124 = (bf16[128,512]{1,0:T(8,128)(2,1)}, f32[16,512]{1,0:T(8,128)}, f32[16,512]{1,0:T(8,128)}, f32[1,512]{1,0:T(1,128)}) custom-call(f32[128,512]{1,0:T(8,128)S(1)} %get-tuple-element.51.g_f, f32[56,512]{1,0:T(8,128)S(1)} %shard_map.103.table_ref, f32[56,512]{1,0:T(8,128)S(1)} %collective-permute-done.16.other_ref, ...), custom_call_target="tpu_custom_call" | custom-call | flops 1024 | bytes 1024 | tf_op jit(solution)/shard_map/pallas_call | solution.py:20
  60.2 1.0 %shard_map.121 = bf16[32,8192]{1,0:T(8,128)(2,1)} custom-call(bf16[128,4096]{1,0:T(8,128)(2,1)S(1)} %shard_map.106.share_ref.refs_0_, bf16[128,4096]{1,0:T(8,128)(2,1)S(1)} %shard_map.108.share_ref.refs_1_.refs_2_, bf16[32,8192]{1,0:T(8,128)(2,1)S(1)} %collective-permute-done.14.refs_2_, bf16[32,8192]{1,0:T(8,128)(2,1)S(1)} %collective-permute-done.15.refs_3_), custom_call_target="tpu_custom_call" | custom-call | flops 1024 | bytes 1024 | tf_op jit(solution)/shard_map/pallas_call | solution.py:20
  (45 shorter events, 6.0 us)
Async XLA Ops:
  0.6 1.0 %copy-start.1 = (bf16[32,8192]{1,0:T(8,128)(2,1)S(1)}, bf16[32,8192]{1,0:T(8,128)(2,1)}, u32[]{:S(2)}) copy-start(bf16[32,8192]{1,0:T(8,128)(2,1)} %own_ref) | copy-start | bytes 1572868
  0.6 7.9 %copy-start.3 = (f32[512,16]{0,1:T(8,128)S(1)}, f32[512,16]{0,1:T(8,128)}, u32[]{:S(2)}) copy-start(f32[512,16]{0,1:T(8,128)} %param.8) | copy-start | bytes 98308
  0.7 7.9 %copy-start.2 = (bf16[128,512]{1,0:T(8,128)(2,1)S(1)}, bf16[128,512]{1,0:T(8,128)(2,1)}, u32[]{:S(2)}) copy-start(bf16[128,512]{1,0:T(8,128)(2,1)} %x_ref.1) | copy-start | bytes 393220
  0.7 13.4 %copy-start.5 = (f32[512]{0:T(512)S(1)}, f32[512]{0:T(512)}, u32[]{:S(2)}) copy-start(f32[512]{0:T(512)} %param.9) | copy-start | bytes 6148
  0.7 13.4 %copy-start.4 = (f32[512,16]{0,1:T(8,128)S(1)}, f32[512,16]{0,1:T(8,128)}, u32[]{:S(2)}) copy-start(f32[512,16]{0,1:T(8,128)} %param.7) | copy-start | bytes 98308
  0.7 18.0 %copy-start = (bf16[512,8192]{1,0:T(8,128)(2,1)S(1)}, bf16[512,8192]{1,0:T(8,128)(2,1)}, u32[]{:S(2)}) copy-start(bf16[512,8192]{1,0:T(8,128)(2,1)} %weight_ref.9) | copy-start | bytes 25165828
  1.7 17.7 %collective-permute-start.4 = (bf16[32,8192]{1,0:T(8,128)(2,1)S(1)}, bf16[32,8192]{1,0:T(8,128)(2,1)S(1)}, u32[]{:S(2)}, u32[]{:S(2)}) collective-permute-start(bf16[32,8192]{1,0:T(8,128)(2,1)S(1)} %copy-done.1), channel_id=1, source_target_pairs={{1,2},{2,1},{0,0},{3,3},{5,6},{6,5},{4,4},{7,7},{9,10},{10,9},{8,8... | collective-permute-start | bytes 1572872 | tf_op jit(solution)/shard_map/ppermute | solution.py:243
  2.5 18.9 %collective-permute-start.6 = (bf16[32,8192]{1,0:T(8,128)(2,1)S(1)}, bf16[32,8192]{1,0:T(8,128)(2,1)S(1)}, u32[]{:S(2)}, u32[]{:S(2)}) collective-permute-start(bf16[32,8192]{1,0:T(8,128)(2,1)S(1)} %copy-done.1), channel_id=1, source_target_pairs={{0,1},{1,0},{2,3},{3,2},{4,5},{5,4},{6,7},{7,6},{8,9},{9,8},{10,11... | collective-permute-start | bytes 1572872 | tf_op jit(solution)/shard_map/ppermute | solution.py:239
  9.1 1.3 %collective-permute-start = (f32[32,512]{1,0:T(8,128)S(1)}, f32[32,512]{1,0:T(8,128)S(1)}, u32[]{:S(2)}, u32[]{:S(2)}) collective-permute-start(f32[32,512]{1,0:T(8,128)S(1)} %get-tuple-element.33.own_ref), channel_id=1, source_target_pairs={{0,4},{4,0},{8,12},{12,8},{16,20},{20,16},{24,28},{28,24},{1,5},{5... | collective-permute-start | bytes 196616 | tf_op jit(solution)/shard_map/ppermute | solution.py:231
  10.5 4.9 %collective-permute-start.3 = (bf16[32,512]{1,0:T(8,128)(2,1)S(1)}, bf16[32,512]{1,0:T(8,128)(2,1)S(1)}, u32[]{:S(2)}, u32[]{:S(2)}) collective-permute-start(bf16[32,512]{1,0:T(8,128)(2,1)S(1)} %shard_map.104), channel_id=1, source_target_pairs={{0,24},{4,28},{8,16},{12,20},{16,8},{20,12},{24,0},{28,4},{1,25},{... | collective-permute-start | bytes 98312 | tf_op jit(solution)/shard_map/ppermute | solution.py:235
  13.0 3.9 %collective-permute-start.2 = (bf16[32,512]{1,0:T(8,128)(2,1)S(1)}, bf16[32,512]{1,0:T(8,128)(2,1)S(1)}, u32[]{:S(2)}, u32[]{:S(2)}) collective-permute-start(bf16[32,512]{1,0:T(8,128)(2,1)S(1)} %shard_map.104), channel_id=1, source_target_pairs={{0,16},{4,20},{8,24},{12,28},{16,0},{20,4},{24,8},{28,12},{1,17},{... | collective-permute-start | bytes 98312 | tf_op jit(solution)/shard_map/ppermute | solution.py:235
  13.5 3.9 %collective-permute-start.1 = (bf16[32,512]{1,0:T(8,128)(2,1)S(1)}, bf16[32,512]{1,0:T(8,128)(2,1)S(1)}, u32[]{:S(2)}, u32[]{:S(2)}) collective-permute-start(bf16[32,512]{1,0:T(8,128)(2,1)S(1)} %shard_map.104), channel_id=1, source_target_pairs={{0,8},{4,12},{8,0},{12,4},{16,24},{20,28},{24,16},{28,20},{1,9},{5... | collective-permute-start | bytes 98312 | tf_op jit(solution)/shard_map/ppermute | solution.py:235
  20.2 9.3 %collective-permute-start.5 = (bf16[32,4096]{1,0:T(8,128)(2,1)S(1)}, bf16[32,4096]{1,0:T(8,128)(2,1)S(1)}, u32[]{:S(2)}, u32[]{:S(2)}) collective-permute-start(bf16[32,4096]{1,0:T(8,128)(2,1)S(1)} %shard_map.107), channel_id=1, source_target_pairs={{0,1},{1,0},{2,3},{3,2},{4,5},{5,4},{6,7},{7,6},{8,9},{9,8},{10,11... | collective-permute-start | bytes 786440 | tf_op jit(solution)/shard_map/ppermute | solution.py:239
  21.4 8.8 %collective-permute-start.8 = (bf16[32,4096]{1,0:T(8,128)(2,1)S(1)}, bf16[32,4096]{1,0:T(8,128)(2,1)S(1)}, u32[]{:S(2)}, u32[]{:S(2)}) collective-permute-start(bf16[32,4096]{1,0:T(8,128)(2,1)S(1)} %get-tuple-element.58), channel_id=1, source_target_pairs={{1,2},{2,1},{0,0},{3,3},{5,6},{6,5},{4,4},{7,7},{9,10},{10,9},{8,8... | collective-permute-start | bytes 786440 | tf_op jit(solution)/shard_map/ppermute | solution.py:243
  22.1 13.1 %collective-permute-start.10 = (bf16[32,4096]{1,0:T(8,128)(2,1)S(1)}, bf16[32,4096]{1,0:T(8,128)(2,1)S(1)}, u32[]{:S(2)}, u32[]{:S(2)}) collective-permute-start(bf16[32,4096]{1,0:T(8,128)(2,1)S(1)} %shard_map.109), channel_id=1, source_target_pairs={{0,1},{1,0},{2,3},{3,2},{4,5},{5,4},{6,7},{7,6},{8,9},{9,8},{10,11... | collective-permute-start | bytes 786440 | tf_op jit(solution)/shard_map/ppermute | solution.py:239
  25.0 10.3 %collective-permute-start.12 = (bf16[32,4096]{1,0:T(8,128)(2,1)S(1)}, bf16[32,4096]{1,0:T(8,128)(2,1)S(1)}, u32[]{:S(2)}, u32[]{:S(2)}) collective-permute-start(bf16[32,4096]{1,0:T(8,128)(2,1)S(1)} %get-tuple-element.57), channel_id=1, source_target_pairs={{1,2},{2,1},{0,0},{3,3},{5,6},{6,5},{4,4},{7,7},{9,10},{10,9},{8,8... | collective-permute-start | bytes 786440 | tf_op jit(solution)/shard_map/ppermute | solution.py:243
  29.6 13.1 %collective-permute-start.7 = (bf16[32,4096]{1,0:T(8,128)(2,1)S(1)}, bf16[32,4096]{1,0:T(8,128)(2,1)S(1)}, u32[]{:S(2)}, u32[]{:S(2)}) collective-permute-start(bf16[32,4096]{1,0:T(8,128)(2,1)S(1)} %shard_map.111), channel_id=1, source_target_pairs={{1,2},{2,1},{0,0},{3,3},{5,6},{6,5},{4,4},{7,7},{9,10},{10,9},{8,8... | collective-permute-start | bytes 786440 | tf_op jit(solution)/shard_map/ppermute | solution.py:243
  30.3 10.9 %collective-permute-start.9 = (bf16[32,4096]{1,0:T(8,128)(2,1)S(1)}, bf16[32,4096]{1,0:T(8,128)(2,1)S(1)}, u32[]{:S(2)}, u32[]{:S(2)}) collective-permute-start(bf16[32,4096]{1,0:T(8,128)(2,1)S(1)} %shard_map.112), channel_id=1, source_target_pairs={{0,1},{1,0},{2,3},{3,2},{4,5},{5,4},{6,7},{7,6},{8,9},{9,8},{10,11... | collective-permute-start | bytes 786440 | tf_op jit(solution)/shard_map/ppermute | solution.py:239
  35.3 8.7 %collective-permute-start.13 = (bf16[32,4096]{1,0:T(8,128)(2,1)S(1)}, bf16[32,4096]{1,0:T(8,128)(2,1)S(1)}, u32[]{:S(2)}, u32[]{:S(2)}) collective-permute-start(bf16[32,4096]{1,0:T(8,128)(2,1)S(1)} %shard_map.118), channel_id=1, source_target_pairs={{0,1},{1,0},{2,3},{3,2},{4,5},{5,4},{6,7},{7,6},{8,9},{9,8},{10,11... | collective-permute-start | bytes 786440 | tf_op jit(solution)/shard_map/ppermute | solution.py:239
  39.2 6.4 %collective-permute-start.11 = (bf16[32,4096]{1,0:T(8,128)(2,1)S(1)}, bf16[32,4096]{1,0:T(8,128)(2,1)S(1)}, u32[]{:S(2)}, u32[]{:S(2)}) collective-permute-start(bf16[32,4096]{1,0:T(8,128)(2,1)S(1)} %shard_map.116), channel_id=1, source_target_pairs={{1,2},{2,1},{0,0},{3,3},{5,6},{6,5},{4,4},{7,7},{9,10},{10,9},{8,8... | collective-permute-start | bytes 786440 | tf_op jit(solution)/shard_map/ppermute | solution.py:243
  45.7 14.5 %collective-permute-start.14 = (bf16[32,8192]{1,0:T(8,128)(2,1)S(1)}, bf16[32,8192]{1,0:T(8,128)(2,1)S(1)}, u32[]{:S(2)}, u32[]{:S(2)}) collective-permute-start(bf16[32,8192]{1,0:T(8,128)(2,1)S(1)} %shard_map.117), channel_id=1, source_target_pairs={{0,1},{1,0},{2,3},{3,2},{4,5},{5,4},{6,7},{7,6},{8,9},{9,8},{10,11... | collective-permute-start | bytes 1572872 | tf_op jit(solution)/shard_map/ppermute | solution.py:239
  47.9 12.3 %collective-permute-start.15 = (bf16[32,8192]{1,0:T(8,128)(2,1)S(1)}, bf16[32,8192]{1,0:T(8,128)(2,1)S(1)}, u32[]{:S(2)}, u32[]{:S(2)}) collective-permute-start(bf16[32,8192]{1,0:T(8,128)(2,1)S(1)} %shard_map.119), channel_id=1, source_target_pairs={{1,2},{2,1},{0,0},{3,3},{5,6},{6,5},{4,4},{7,7},{9,10},{10,9},{8,8... | collective-permute-start | bytes 1572872 | tf_op jit(solution)/shard_map/ppermute | solution.py:243
  49.8 1.4 %collective-permute-start.16 = (f32[56,512]{1,0:T(8,128)S(1)}, f32[56,512]{1,0:T(8,128)S(1)}, u32[]{:S(2)}, u32[]{:S(2)}) collective-permute-start(f32[56,512]{1,0:T(8,128)S(1)} %get-tuple-element.52.own_ref), channel_id=1, source_target_pairs={{0,4},{4,0},{8,12},{12,8},{16,20},{20,16},{24,28},{28,24},{1,5},{5... | collective-permute-start | bytes 344072 | tf_op jit(solution)/shard_map/ppermute | solution.py:231
  51.2 5.3 %collective-permute-start.19 = (bf16[64,512]{1,0:T(8,128)(2,1)S(1)}, bf16[64,512]{1,0:T(8,128)(2,1)S(1)}, u32[]{:S(2)}, u32[]{:S(2)}) collective-permute-start(bf16[64,512]{1,0:T(8,128)(2,1)S(1)} %shard_map.123.pair_ref), channel_id=1, source_target_pairs={{0,24},{4,28},{8,16},{12,20},{16,8},{20,12},{24,0},{28,4},{1,25},{... | collective-permute-start | bytes 196616 | tf_op jit(solution)/shard_map/ppermute | solution.py:235
  53.5 4.3 %collective-permute-start.18 = (bf16[64,512]{1,0:T(8,128)(2,1)S(1)}, bf16[64,512]{1,0:T(8,128)(2,1)S(1)}, u32[]{:S(2)}, u32[]{:S(2)}) collective-permute-start(bf16[64,512]{1,0:T(8,128)(2,1)S(1)} %shard_map.123.pair_ref), channel_id=1, source_target_pairs={{0,16},{4,20},{8,24},{12,28},{16,0},{20,4},{24,8},{28,12},{1,17},{... | collective-permute-start | bytes 196616 | tf_op jit(solution)/shard_map/ppermute | solution.py:235
  54.0 4.3 %collective-permute-start.17 = (bf16[64,512]{1,0:T(8,128)(2,1)S(1)}, bf16[64,512]{1,0:T(8,128)(2,1)S(1)}, u32[]{:S(2)}, u32[]{:S(2)}) collective-permute-start(bf16[64,512]{1,0:T(8,128)(2,1)S(1)} %shard_map.123.pair_ref), channel_id=1, source_target_pairs={{0,8},{4,12},{8,0},{12,4},{16,24},{20,28},{24,16},{28,20},{1,9},{5... | collective-permute-start | bytes 196616 | tf_op jit(solution)/shard_map/ppermute | solution.py:235
where the time goes:
time: 61.4 us; the launch traced here: 61.2 us
  starting transfers between devices  31.5 us (51%)
  Pallas kernels  14.4 us (23%)
  waiting for transfers between devices  13.3 us (22%)
  local copies, waits for them, and re-layouts  1.03 us (2%)
  between operations  0.96 us (2%)
    ppermute x6, starting transfers between devices, outer(): return lax.ppermute(array, 'tp', [(0, 1), (1, 0), (2, 3), (3, 2)])  20.1 us
    pallas_call x24, Pallas kernels, call(): pl.pallas_call(body, out_shape=outs, in_specs=[whole] * len(args), out_sp...  14.4 us
    ppermute x6, starting transfers between devices, from_pairs(): lax.ppermute(array, 'ctx', [(i, i ^ 2 * j) for i in range(blocks)])  7.11 us
    ppermute x6, waiting for transfers between devices, from_pairs(): lax.ppermute(array, 'ctx', [(i, i ^ 2 * j) for i in range(blocks)])  6.86 us
    ppermute x6, starting transfers between devices, inner(): return lax.ppermute(array, 'tp', [(1, 2), (2, 1), (0, 0), (3, 3)])  4.18 us
    ppermute x6, waiting for transfers between devices, outer(): return lax.ppermute(array, 'tp', [(0, 1), (1, 0), (2, 3), (3, 2)])  3.84 us
    ppermute x2, waiting for transfers between devices, from_other_core(): return lax.ppermute(array, 'ctx', [(i, i ^ 1) for i in range(blocks)])  2.55 us
  transfers between devices with their start and end apart: 20, of which 11 were waited for; matrix products, arithmetic and copies ran while one was open for 0% of the time, Pallas kernels for 22%

commit v1 on v0

--- a/solution.py
+++ b/solution.py
@@ -227,6 +227,13 @@
     by_skip_ref[...] = scale * total[2 * modes:2 * modes + 1]
 
 
+def final_body(count, total, rest, *refs):
+    total_refs, refs = refs[:count], refs[count:]
+    out_ref = refs[-6]
+    total(*total_refs, out_ref)
+    rest(*refs[:-6], *refs[-5:])
+
+
 def from_other_core(array, blocks):
     return lax.ppermute(array, "ctx", [(i, i ^ 1) for i in range(blocks)])
 
@@ -382,41 +389,45 @@
     g_rows = [jax.ShapeDtypeStruct((2 * rows, out_weight.shape[0]), F32)]
     (g_near,) = call(near_body, g_rows, [pltpu.VMEM((2 * rows, width), BF16)], [out_grad, beside, out_weight])
     second[0] = lax.optimization_barrier((second[0], g_near))[0]
+
+    def far(at, before):
+        return call(
+            functools.partial(far_body, spans[at]), g_rows, [pltpu.VMEM((2 * rows, cut), BF16)],
+            [second[at], third[at], across, across_far[at], out_weight, *before],
+        )
+
     third = []
     to_far = []
     for at in range(HALVES):
         (sent,) = call(functools.partial(add_body, True), piece, [], [shares[at], second[at]])
         to_far.append(inner(sent))
-        far = lax.optimization_barrier((across_far[at], sent))[0]
-        (sent,) = call(functools.partial(send_body, slice(None), False), piece, [], [shares[at], far])
+        passing = lax.optimization_barrier((across_far[at], sent))[0]
+        (sent,) = call(functools.partial(send_body, slice(None), False), piece, [], [shares[at], passing])
         third.append(outer(sent))
         if at + 1 < HALVES:
             states = states_of(lax.optimization_barrier((x_f, sent))[0])
             second[at + 1] = lax.optimization_barrier((second[at + 1], *states))[0]
-    g_far = []
-    ready = []
-    for at, span in enumerate(spans):
-        g_far = call(
-            functools.partial(far_body, span), g_rows, [pltpu.VMEM((2 * rows, cut), BF16)],
-            [second[at], third[at], across, across_far[at], out_weight, *g_far],
-        )
-        if at == 0:
-            got = lax.optimization_barrier((to_far[0], *g_far))[0]
-            ready = call(functools.partial(last_body, [slice(None)]), piece, [], [shares[0], got])
-            third[-1] = lax.optimization_barrier((third[-1], *ready))[0]
-    ready = call(functools.partial(last_body, spans), whole, [], [*ready, shares[-1], to_far[-1]])[0]
+    g_far = far(0, [])
+    got = lax.optimization_barrier((to_far[0], *g_far))[0]
+    ready = call(functools.partial(last_body, [slice(None)]), piece, [], [shares[0], got])
     (near,) = call(functools.partial(add_whole_body, spans), whole, [], pairs_of(shares, third))
-    ready, near, *g_far = lax.optimization_barrier((ready, near, *g_far))
+    got = lax.optimization_barrier((to_far[-1], near))[0]
+    (ready,) = call(functools.partial(last_body, spans), whole, [], [*ready, shares[-1], got])
+    third[-1] = lax.optimization_barrier((third[-1], ready))[0]
+    g_far = far(1, g_far)
+    last = outer(ready)
+    to_near = inner(near)
 
     def places():
         at = lax.axis_index("tp")
         return [at, at ^ 1, inward(False), inward(True)]
 
     g_f, sums = grads_of([g_near, *g_far], places, states)
-    last = outer(ready)
-    to_near = inner(near)
-    (out,) = call(functools.partial(total_body, spans), whole, [], [*shares, last, to_near])
-    return out, g_f, sums
+    return (functools.partial(total_body, spans), whole, [*shares, last, to_near]), g_f, sums
+
+
+def whole_body(total_ref, out_ref):
+    out_ref[...] = total_ref[...]
 
 
 def any_axis(out_grad, out_weight, merged, x_f, states_of, grads_of):
@@ -424,7 +435,7 @@
     gathered = lax.all_gather(out_grad, "tp", axis=0, tiled=True)
     share = jnp.dot(merged, out_weight, preferred_element_type=F32).astype(BF16)
     out = lax.psum_scatter(share, "tp", scatter_dimension=0, tiled=True)
-    return out, *grads_of([back_dot(gathered, out_weight)], lambda: list(range(parts)), states_of(x_f))
+    return (whole_body, [jax.ShapeDtypeStruct(out.shape, out.dtype)], [out]), *grads_of([back_dot(gathered, out_weight)], lambda: list(range(parts)), states_of(x_f))
 
 
 def per_device(inputs, residue, log_rate, skip, out_weight, out_grad):
@@ -438,11 +449,9 @@
     state = lanes((modes, chans))
     token_f = pltpu.VMEM((tok, chans), F32)
 
-    (zero,) = call(clear_body, [state], [], [], flops=CLEAR_FLOPS)
-    out_grad = lax.optimization_barrier((out_grad, zero))[0]
     x_f, rate, ends = call(
         functools.partial(ends_body, seq), [lanes((tok, chans)), state, lanes((2 * modes, chans))], [],
-        [inputs, log_rate.T, zero],
+        [inputs, log_rate.T, *call(clear_body, [state], [], [], flops=CLEAR_FLOPS)], flops=2_000_000_000,
     )
     (table,) = call(
         table_body, [lanes((3 * modes + 8, chans))], [], [rate, residue.T, skip[None, :]], flops=1_000_000_000
@@ -470,16 +479,18 @@
         )
 
     reduce = line_of_four if parts == 4 else any_axis
-    out, g_f, sums = reduce(out_grad, out_weight, merged, x_f, states_of, grads_of)
+    (total, out_shape, total_args), g_f, sums = reduce(out_grad, out_weight, merged, x_f, states_of, grads_of)
     other_sums = from_other_core(sums, blocks)
     (pair_sums,) = call(
         functools.partial(pair_sums_body, tok, modes), [jax.ShapeDtypeStruct((4 * modes, chans), BF16)], [],
         [table, sums, other_sums],
     )
-    grad_input, by_res, by_log, by_skip = call(
-        functools.partial(input_body, seq, modes),
-        [jax.ShapeDtypeStruct((tok, chans), BF16), state, state, lanes((1, chans))], [token_f],
-        [g_f, table, other_sums, pair_sums, *from_pairs(pair_sums, blocks)],
+    far_sums = from_pairs(pair_sums, blocks)
+    far_sums[0] = lax.optimization_barrier((far_sums[0], total_args[-1]))[0]
+    out, grad_input, by_res, by_log, by_skip = call(
+        functools.partial(final_body, len(total_args), total, functools.partial(input_body, seq, modes)),
+        [*out_shape, jax.ShapeDtypeStruct((tok, chans), BF16), state, state, lanes((1, chans))], [token_f],
+        [*total_args, g_f, table, other_sums, pair_sums, *far_sums],
     )
     return out, grad_input, by_res.T, by_log.T, by_skip[0]
 

time: 61.4 us -> 62.6 us (1.020)
  starting transfers between devices: 31.5 us -> 33.6 us
  local copies, waits for them, and re-layouts: 1.03 us -> 0.06 us
  Pallas kernels: 14.4 us -> 13.7 us
  waiting for transfers between devices: 13.3 us -> 14 us
    ppermute x6, starting transfers between devices: 20.1 us -> 21.2 us  [outer(): return lax.ppermute(array, 'tp', [(0, 1), (1, 0), (2, 3), (3, 2)])]
    ppermute x6, starting transfers between devices: 4.18 us -> 5.21 us  [inner(): return lax.ppermute(array, 'tp', [(1, 2), (2, 1), (0, 0), (3, 3)])]
    unnamed x12, local copies, waits for them, and re-layouts: 0.99 us -> 0.03 us
    ppermute x6, waiting for transfers between devices: 6.86 us -> 7.67 us  [from_pairs(): lax.ppermute(array, 'ctx', [(i, i ^ 2 * j) for i in range(blocks)])]
    pallas_call x24 -> x23, Pallas kernels: 14.4 us -> 13.7 us  [call(): pl.pallas_call(body, out_shape=outs, in_specs=[whole] * len(args), out_sp...]
  transfers between devices with their start and end apart: 20 -> 20, of which waited for: 11 -> 11; matrix products, arithmetic and copies ran while one was open for 0% -> 0% of each run, Pallas kernels for 22% -> 18%
where the time goes in v1:
time: 62.6 us; the launch traced here: 62.4 us
  starting transfers between devices  33.6 us (54%)
  waiting for transfers between devices  14 us (22%)
  Pallas kernels  13.7 us (22%)
  between operations  0.94 us (2%)
    ppermute x6, starting transfers between devices, outer(): return lax.ppermute(array, 'tp', [(0, 1), (1, 0), (2, 3), (3, 2)])  21.2 us
    pallas_call x23, Pallas kernels, call(): pl.pallas_call(body, out_shape=outs, in_specs=[whole] * len(args), out_sp...  13.7 us
    ppermute x6, waiting for transfers between devices, from_pairs(): lax.ppermute(array, 'ctx', [(i, i ^ 2 * j) for i in range(blocks)])  7.67 us
    ppermute x6, starting transfers between devices, from_pairs(): lax.ppermute(array, 'ctx', [(i, i ^ 2 * j) for i in range(blocks)])  7.11 us
    ppermute x6, starting transfers between devices, inner(): return lax.ppermute(array, 'tp', [(1, 2), (2, 1), (0, 0), (3, 3)])  5.21 us
    ppermute x6, waiting for transfers between devices, outer(): return lax.ppermute(array, 'tp', [(0, 1), (1, 0), (2, 3), (3, 2)])  3.75 us
    ppermute x2, waiting for transfers between devices, from_other_core(): return lax.ppermute(array, 'ctx', [(i, i ^ 1) for i in range(blocks)])  2.55 us
  transfers between devices with their start and end apart: 20, of which 11 were waited for; matrix products, arithmetic and copies ran while one was open for 0% of the time, Pallas kernels for 18%

profile of v1, /device:TPU:0, one launch (start us, length us, event | category | flops | bytes accessed | tf_op | source)
XLA Modules:
  0.0 62.4 jit_solution(8398875942928107934)
XLA Ops:
  0.7 1.8 %collective-permute-start.4 = (bf16[32,8192]{1,0:T(8,128)(2,1)}, bf16[32,8192]{1,0:T(8,128)(2,1)S(1)}, u32[]{:S(2)}, u32[]{:S(2)}) collective-permute-start(bf16[32,8192]{1,0:T(8,128)(2,1)} %own_ref.1), channel_id=1, source_target_pairs={{1,2},{2,1},{0,0},{3,3},{5,6},{6,5},{4,4},{7,7},{9,10},{10,9},{8,8... | collective-permute-start | bytes 1572872 | tf_op jit(solution)/shard_map/ppermute | solution.py:250
  2.5 4.9 %collective-permute-start.6 = (bf16[32,8192]{1,0:T(8,128)(2,1)}, bf16[32,8192]{1,0:T(8,128)(2,1)S(1)}, u32[]{:S(2)}, u32[]{:S(2)}) collective-permute-start(bf16[32,8192]{1,0:T(8,128)(2,1)} %own_ref.1), channel_id=1, source_target_pairs={{0,1},{1,0},{2,3},{3,2},{4,5},{5,4},{6,7},{7,6},{8,9},{9,8},{10,11... | collective-permute-start | bytes 1572872 | tf_op jit(solution)/shard_map/ppermute | solution.py:246
  8.1 1.2 %collective-permute-done.other_ref = f32[32,512]{1,0:T(8,128)S(1)} collective-permute-done((f32[32,512]{1,0:T(8,128)S(1)}, f32[32,512]{1,0:T(8,128)S(1)}, u32[]{:S(2)}, u32[]{:S(2)}) %collective-permute-start) | collective-permute-done | bytes 65568 | tf_op jit(solution)/shard_map/ppermute | solution.py:238
  9.4 2.5 %collective-permute-start.3 = (bf16[32,512]{1,0:T(8,128)(2,1)S(1)}, bf16[32,512]{1,0:T(8,128)(2,1)S(1)}, u32[]{:S(2)}, u32[]{:S(2)}) collective-permute-start(bf16[32,512]{1,0:T(8,128)(2,1)S(1)} %shard_map.104), channel_id=1, source_target_pairs={{0,24},{4,28},{8,16},{12,20},{16,8},{20,12},{24,0},{28,4},{1,25},{... | collective-permute-start | bytes 98312 | tf_op jit(solution)/shard_map/ppermute | solution.py:242
  12.9 1.3 %collective-permute-done.3.refs_2_ = bf16[32,512]{1,0:T(8,128)(2,1)S(1)} collective-permute-done((bf16[32,512]{1,0:T(8,128)(2,1)S(1)}, bf16[32,512]{1,0:T(8,128)(2,1)S(1)}, u32[]{:S(2)}, u32[]{:S(2)}) %collective-permute-start.3) | collective-permute-done | bytes 32800 | tf_op jit(solution)/shard_map/ppermute | solution.py:242
  14.2 1.5 %collective-permute-done.2.refs_1_ = bf16[32,512]{1,0:T(8,128)(2,1)S(1)} collective-permute-done((bf16[32,512]{1,0:T(8,128)(2,1)S(1)}, bf16[32,512]{1,0:T(8,128)(2,1)S(1)}, u32[]{:S(2)}, u32[]{:S(2)}) %collective-permute-start.2) | collective-permute-done | bytes 32800 | tf_op jit(solution)/shard_map/ppermute | solution.py:242
  16.3 1.2 %shard_map.105 = (bf16[128,512]{1,0:T(8,128)(2,1)S(1)}, f32[32,512]{1,0:T(8,128)S(1)}) custom-call(f32[128,512]{1,0:T(8,128)S(1)} %get-tuple-element.39.x_f, f32[56,512]{1,0:T(8,128)S(1)} %shard_map.103.table_ref.refs_5_, f32[32,512]{1,0:T(8,128)S(1)} %collective-permute-done.other_ref, bf16[32,512]{1,0:T(8,128)(2,1)S(1)} %collective-permute-done.1.refs_0_, ...), custom_call_target="tpu_custom_call" | custom-call | flops 1024 | bytes 1024 | tf_op jit(solution)/shard_map/pallas_call | solution.py:20
  17.5 0.7 %shard_map.106.share_ref.refs_0_ = bf16[128,4096]{1,0:T(8,128)(2,1)S(1)} custom-call(bf16[128,512]{1,0:T(8,128)(2,1)S(1)} %get-tuple-element.34.merged_ref, bf16[512,8192]{1,0:T(8,128)(2,1)S(1)} %copy-done), custom_call_target="tpu_custom_call" | custom-call | flops 1024 | bytes 1024 | tf_op jit(solution)/shard_map/pallas_call | solution.py:20
  18.3 0.7 %shard_map.108.share_ref.refs_2_.refs_1_ = bf16[128,4096]{1,0:T(8,128)(2,1)S(1)} custom-call(bf16[128,512]{1,0:T(8,128)(2,1)S(1)} %get-tuple-element.34.merged_ref, bf16[512,8192]{1,0:T(8,128)(2,1)S(1)} %copy-done), custom_call_target="tpu_custom_call" | custom-call | flops 1024 | bytes 1024 | tf_op jit(solution)/shard_map/pallas_call | solution.py:20
  19.1 1.3 %collective-permute-start.5 = (bf16[32,4096]{1,0:T(8,128)(2,1)S(1)}, bf16[32,4096]{1,0:T(8,128)(2,1)S(1)}, u32[]{:S(2)}, u32[]{:S(2)}) collective-permute-start(bf16[32,4096]{1,0:T(8,128)(2,1)S(1)} %shard_map.107), channel_id=1, source_target_pairs={{0,1},{1,0},{2,3},{3,2},{4,5},{5,4},{6,7},{7,6},{8,9},{9,8},{10,11... | collective-permute-start | bytes 786440 | tf_op jit(solution)/shard_map/ppermute | solution.py:246
  20.5 0.7 %collective-permute-start.8 = (bf16[32,4096]{1,0:T(8,128)(2,1)S(1)}, bf16[32,4096]{1,0:T(8,128)(2,1)S(1)}, u32[]{:S(2)}, u32[]{:S(2)}) collective-permute-start(bf16[32,4096]{1,0:T(8,128)(2,1)S(1)} %get-tuple-element.56), channel_id=1, source_target_pairs={{1,2},{2,1},{0,0},{3,3},{5,6},{6,5},{4,4},{7,7},{9,10},{10,9},{8,8... | collective-permute-start | bytes 786440 | tf_op jit(solution)/shard_map/ppermute | solution.py:250
  21.2 2.9 %collective-permute-start.10 = (bf16[32,4096]{1,0:T(8,128)(2,1)S(1)}, bf16[32,4096]{1,0:T(8,128)(2,1)S(1)}, u32[]{:S(2)}, u32[]{:S(2)}) collective-permute-start(bf16[32,4096]{1,0:T(8,128)(2,1)S(1)} %shard_map.109), channel_id=1, source_target_pairs={{0,1},{1,0},{2,3},{3,2},{4,5},{5,4},{6,7},{7,6},{8,9},{9,8},{10,11... | collective-permute-start | bytes 786440 | tf_op jit(solution)/shard_map/ppermute | solution.py:246
  24.8 2.6 %shard_map.110.refs_0_ = f32[64,512]{1,0:T(8,128)S(1)} custom-call(bf16[32,8192]{1,0:T(8,128)(2,1)S(1)} %copy-done.1, bf16[32,8192]{1,0:T(8,128)(2,1)S(1)} %collective-permute-done.6.beside_ref, bf16[512,8192]{1,0:T(8,128)(2,1)S(1)} %copy-done), custom_call_target="tpu_custom_call" | custom-call | flops 1024 | bytes 1024 | tf_op jit(solution)/shard_map/pallas_call | solution.py:20
  27.4 1.0 %collective-permute-done.5.got_ref.second_ref = bf16[32,4096]{1,0:T(8,128)(2,1)S(1)} collective-permute-done((bf16[32,4096]{1,0:T(8,128)(2,1)S(1)}, bf16[32,4096]{1,0:T(8,128)(2,1)S(1)}, u32[]{:S(2)}, u32[]{:S(2)}) %collective-permute-start.5) | collective-permute-done | bytes 262176 | tf_op jit(solution)/shard_map/ppermute | solution.py:246
  28.5 0.7 %collective-permute-start.7 = (bf16[32,4096]{1,0:T(8,128)(2,1)S(1)}, bf16[32,4096]{1,0:T(8,128)(2,1)S(1)}, u32[]{:S(2)}, u32[]{:S(2)}) collective-permute-start(bf16[32,4096]{1,0:T(8,128)(2,1)S(1)} %shard_map.111), channel_id=1, source_target_pairs={{1,2},{2,1},{0,0},{3,3},{5,6},{6,5},{4,4},{7,7},{9,10},{10,9},{8,8... | collective-permute-start | bytes 786440 | tf_op jit(solution)/shard_map/ppermute | solution.py:250
  29.2 4.1 %collective-permute-start.9 = (bf16[32,4096]{1,0:T(8,128)(2,1)S(1)}, bf16[32,4096]{1,0:T(8,128)(2,1)S(1)}, u32[]{:S(2)}, u32[]{:S(2)}) collective-permute-start(bf16[32,4096]{1,0:T(8,128)(2,1)S(1)} %shard_map.112), channel_id=1, source_target_pairs={{0,1},{1,0},{2,3},{3,2},{4,5},{5,4},{6,7},{7,6},{8,9},{9,8},{10,11... | collective-permute-start | bytes 786440 | tf_op jit(solution)/shard_map/ppermute | solution.py:246
  33.3 0.9 %shard_map.115 = (f32[2048,512]{1,0:T(8,128)S(1)}, f32[2048,512]{1,0:T(8,128)S(1)}) custom-call(f32[128,512]{1,0:T(8,128)S(1)} %get-tuple-element.39.x_f, f32[56,512]{1,0:T(8,128)S(1)} %shard_map.103.table_ref.refs_5_, f32[32,512]{1,0:T(8,128)S(1)} %get-tuple-element.40.start_ref), custom_call_target="tpu_custom_call" | custom-call | flops 1024 | bytes 1024 | tf_op jit(solution)/shard_map/pallas_call | solution.py:20
  34.4 3.6 %collective-permute-start.13 = (bf16[32,4096]{1,0:T(8,128)(2,1)S(1)}, bf16[32,4096]{1,0:T(8,128)(2,1)S(1)}, u32[]{:S(2)}, u32[]{:S(2)}) collective-permute-start(bf16[32,4096]{1,0:T(8,128)(2,1)S(1)} %shard_map.117), channel_id=1, source_target_pairs={{0,1},{1,0},{2,3},{3,2},{4,5},{5,4},{6,7},{7,6},{8,9},{9,8},{10,11... | collective-permute-start | bytes 786440 | tf_op jit(solution)/shard_map/ppermute | solution.py:246
  38.7 1.5 %collective-permute-done.9.third_ref.refs_1_ = bf16[32,4096]{1,0:T(8,128)(2,1)S(1)} collective-permute-done((bf16[32,4096]{1,0:T(8,128)(2,1)S(1)}, bf16[32,4096]{1,0:T(8,128)(2,1)S(1)}, u32[]{:S(2)}, u32[]{:S(2)}) %collective-permute-start.9) | collective-permute-done | bytes 262176 | tf_op jit(solution)/shard_map/ppermute | solution.py:246
  40.2 1.4 %shard_map.113.refs_0_ = f32[64,512]{1,0:T(8,128)S(1)} custom-call(bf16[32,4096]{1,0:T(8,128)(2,1)S(1)} %collective-permute-done.5.got_ref.second_ref, bf16[32,4096]{1,0:T(8,128)(2,1)S(1)} %collective-permute-done.9.third_ref.refs_1_, bf16[32,8192]{1,0:T(8,128)(2,1)S(1)} %collective-permute-done.4.passing_ref.across_ref, ...), custom_call_target="tpu_custom_call" | custom-call | flops 1024 | bytes 1024 | tf_op jit(solution)/shard_map/pallas_call | solution.py:20
  41.7 1.3 %collective-permute-done.13.refs_3_.third_ref = bf16[32,4096]{1,0:T(8,128)(2,1)S(1)} collective-permute-done((bf16[32,4096]{1,0:T(8,128)(2,1)S(1)}, bf16[32,4096]{1,0:T(8,128)(2,1)S(1)}, u32[]{:S(2)}, u32[]{:S(2)}) %collective-permute-start.13) | collective-permute-done | bytes 262176 | tf_op jit(solution)/shard_map/ppermute | solution.py:246
  43.1 0.7 %collective-permute-start.15 = (bf16[32,8192]{1,0:T(8,128)(2,1)S(1)}, bf16[32,8192]{1,0:T(8,128)(2,1)S(1)}, u32[]{:S(2)}, u32[]{:S(2)}) collective-permute-start(bf16[32,8192]{1,0:T(8,128)(2,1)S(1)} %shard_map.118), channel_id=1, source_target_pairs={{1,2},{2,1},{0,0},{3,3},{5,6},{6,5},{4,4},{7,7},{9,10},{10,9},{8,8... | collective-permute-start | bytes 1572872 | tf_op jit(solution)/shard_map/ppermute | solution.py:250
  44.0 4.3 %collective-permute-start.14 = (bf16[32,8192]{1,0:T(8,128)(2,1)S(1)}, bf16[32,8192]{1,0:T(8,128)(2,1)S(1)}, u32[]{:S(2)}, u32[]{:S(2)}) collective-permute-start(bf16[32,8192]{1,0:T(8,128)(2,1)S(1)} %shard_map.119), channel_id=1, source_target_pairs={{0,1},{1,0},{2,3},{3,2},{4,5},{5,4},{6,7},{7,6},{8,9},{9,8},{10,11... | collective-permute-start | bytes 1572872 | tf_op jit(solution)/shard_map/ppermute | solution.py:246
  48.2 1.4 %shard_map.120.refs_1_ = f32[64,512]{1,0:T(8,128)S(1)} custom-call(bf16[32,4096]{1,0:T(8,128)(2,1)S(1)} %collective-permute-done.10.got_ref.second_ref, bf16[32,4096]{1,0:T(8,128)(2,1)S(1)} %collective-permute-done.13.refs_3_.third_ref, bf16[32,8192]{1,0:T(8,128)(2,1)S(1)} %collective-permute-done.4.passing_ref.across_ref, ...), custom_call_target="tpu_custom_call" | custom-call | flops 1024 | bytes 1024 | tf_op jit(solution)/shard_map/pallas_call | solution.py:20
  49.7 1.2 %shard_map.121 = (f32[128,512]{1,0:T(8,128)S(1)}, f32[56,512]{1,0:T(8,128)S(1)}) custom-call(f32[128,512]{1,0:T(8,128)S(1)} %get-tuple-element.39.x_f, f32[56,512]{1,0:T(8,128)S(1)} %shard_map.103.table_ref.refs_5_, f32[2048,512]{1,0:T(8,128)S(1)} %get-tuple-element.41.h_ref, f32[2048,512]{1,0:T(8,128)S(1)} %get-tuple-element.42.q_ref, ...), custom_call_target="tpu_custom_call" | custom-call | flops 1024 | bytes 1024 | tf_op jit(solution)/shard_map/pallas_call | solution.py:20
  50.9 1.3 %collective-permute-done.16.other_ref.refs_6_ = f32[56,512]{1,0:T(8,128)S(1)} collective-permute-done((f32[56,512]{1,0:T(8,128)S(1)}, f32[56,512]{1,0:T(8,128)S(1)}, u32[]{:S(2)}, u32[]{:S(2)}) %collective-permute-start.16) | collective-permute-done | bytes 114720 | tf_op jit(solution)/shard_map/ppermute | solution.py:238
  52.3 1.6 %collective-permute-start.17 = (bf16[64,512]{1,0:T(8,128)(2,1)S(1)}, bf16[64,512]{1,0:T(8,128)(2,1)S(1)}, u32[]{:S(2)}, u32[]{:S(2)}) collective-permute-start(bf16[64,512]{1,0:T(8,128)(2,1)S(1)} %shard_map.122.refs_7_), channel_id=1, source_target_pairs={{0,8},{4,12},{8,0},{12,4},{16,24},{20,28},{24,16},{28,20},{1,9},{5... | collective-permute-start | bytes 196616 | tf_op jit(solution)/shard_map/ppermute | solution.py:242
  53.8 1.5 %collective-permute-start.19 = (bf16[64,512]{1,0:T(8,128)(2,1)S(1)}, bf16[64,512]{1,0:T(8,128)(2,1)S(1)}, u32[]{:S(2)}, u32[]{:S(2)}) collective-permute-start(bf16[64,512]{1,0:T(8,128)(2,1)S(1)} %shard_map.122.refs_7_), channel_id=1, source_target_pairs={{0,24},{4,28},{8,16},{12,20},{16,8},{20,12},{24,0},{28,4},{1,25},{... | collective-permute-start | bytes 196616 | tf_op jit(solution)/shard_map/ppermute | solution.py:242
  55.8 0.8 %collective-permute-done.17.refs_8_ = bf16[64,512]{1,0:T(8,128)(2,1)S(1)} collective-permute-done((bf16[64,512]{1,0:T(8,128)(2,1)S(1)}, bf16[64,512]{1,0:T(8,128)(2,1)S(1)}, u32[]{:S(2)}, u32[]{:S(2)}) %collective-permute-start.17) | collective-permute-done | bytes 65568 | tf_op jit(solution)/shard_map/ppermute | solution.py:242
  56.6 2.5 %collective-permute-done.19.refs_10_ = bf16[64,512]{1,0:T(8,128)(2,1)S(1)} collective-permute-done((bf16[64,512]{1,0:T(8,128)(2,1)S(1)}, bf16[64,512]{1,0:T(8,128)(2,1)S(1)}, u32[]{:S(2)}, u32[]{:S(2)}) %collective-permute-start.19) | collective-permute-done | bytes 65568 | tf_op jit(solution)/shard_map/ppermute | solution.py:242
  59.1 1.1 %collective-permute-done.18.refs_9_ = bf16[64,512]{1,0:T(8,128)(2,1)S(1)} collective-permute-done((bf16[64,512]{1,0:T(8,128)(2,1)S(1)}, bf16[64,512]{1,0:T(8,128)(2,1)S(1)}, u32[]{:S(2)}, u32[]{:S(2)}) %collective-permute-start.18) | collective-permute-done | bytes 65568 | tf_op jit(solution)/shard_map/ppermute | solution.py:242
  60.1 2.2 %shard_map.123 = (bf16[32,8192]{1,0:T(8,128)(2,1)}, bf16[128,512]{1,0:T(8,128)(2,1)}, f32[16,512]{1,0:T(8,128)}, f32[16,512]{1,0:T(8,128)}, f32[1,512]{1,0:T(1,128)}) custom-call(bf16[128,4096]{1,0:T(8,128)(2,1)S(1)} %shard_map.106.share_ref.refs_0_, bf16[128,4096]{1,0:T(8,128)(2,1)S(1)} %shard_map.108.share_ref.refs_2_.refs_1_, ...), custom_call_target="tpu_custom_call" | custom-call | flops 1024 | bytes 1024 | tf_op jit(solution)/shard_map/pallas_call | solution.py:20
  (44 shorter events, 4.9 us)
Async XLA Ops:
  0.6 6.7 %copy-start.3 = (f32[512,16]{0,1:T(8,128)S(1)}, f32[512,16]{0,1:T(8,128)}, u32[]{:S(2)}) copy-start(f32[512,16]{0,1:T(8,128)} %param.8) | copy-start | bytes 98308
  0.6 6.7 %copy-start.2 = (bf16[128,512]{1,0:T(8,128)(2,1)S(1)}, bf16[128,512]{1,0:T(8,128)(2,1)}, u32[]{:S(2)}) copy-start(bf16[128,512]{1,0:T(8,128)(2,1)} %x_ref.1) | copy-start | bytes 393220
  0.7 17.6 %collective-permute-start.4 = (bf16[32,8192]{1,0:T(8,128)(2,1)}, bf16[32,8192]{1,0:T(8,128)(2,1)S(1)}, u32[]{:S(2)}, u32[]{:S(2)}) collective-permute-start(bf16[32,8192]{1,0:T(8,128)(2,1)} %own_ref.1), channel_id=1, source_target_pairs={{1,2},{2,1},{0,0},{3,3},{5,6},{6,5},{4,4},{7,7},{9,10},{10,9},{8,8... | collective-permute-start | bytes 1572872 | tf_op jit(solution)/shard_map/ppermute | solution.py:250
  2.5 17.9 %collective-permute-start.6 = (bf16[32,8192]{1,0:T(8,128)(2,1)}, bf16[32,8192]{1,0:T(8,128)(2,1)S(1)}, u32[]{:S(2)}, u32[]{:S(2)}) collective-permute-start(bf16[32,8192]{1,0:T(8,128)(2,1)} %own_ref.1), channel_id=1, source_target_pairs={{0,1},{1,0},{2,3},{3,2},{4,5},{5,4},{6,7},{7,6},{8,9},{9,8},{10,11... | collective-permute-start | bytes 1572872 | tf_op jit(solution)/shard_map/ppermute | solution.py:246
  7.4 5.6 %copy-start.4 = (f32[512,16]{0,1:T(8,128)S(1)}, f32[512,16]{0,1:T(8,128)}, u32[]{:S(2)}) copy-start(f32[512,16]{0,1:T(8,128)} %param.7) | copy-start | bytes 98308
  7.4 5.6 %copy-start.5 = (f32[512]{0:T(512)S(1)}, f32[512]{0:T(512)}, u32[]{:S(2)}) copy-start(f32[512]{0:T(512)} %param.9) | copy-start | bytes 6148
  7.4 10.2 %copy-start = (bf16[512,8192]{1,0:T(8,128)(2,1)S(1)}, bf16[512,8192]{1,0:T(8,128)(2,1)}, u32[]{:S(2)}) copy-start(bf16[512,8192]{1,0:T(8,128)(2,1)} %weight_ref.9) | copy-start | bytes 25165828
  8.0 1.3 %collective-permute-start = (f32[32,512]{1,0:T(8,128)S(1)}, f32[32,512]{1,0:T(8,128)S(1)}, u32[]{:S(2)}, u32[]{:S(2)}) collective-permute-start(f32[32,512]{1,0:T(8,128)S(1)} %get-tuple-element.32.own_ref), channel_id=1, source_target_pairs={{0,4},{4,0},{8,12},{12,8},{16,20},{20,16},{24,28},{28,24},{1,5},{5... | collective-permute-start | bytes 196616 | tf_op jit(solution)/shard_map/ppermute | solution.py:238
  9.4 4.9 %collective-permute-start.3 = (bf16[32,512]{1,0:T(8,128)(2,1)S(1)}, bf16[32,512]{1,0:T(8,128)(2,1)S(1)}, u32[]{:S(2)}, u32[]{:S(2)}) collective-permute-start(bf16[32,512]{1,0:T(8,128)(2,1)S(1)} %shard_map.104), channel_id=1, source_target_pairs={{0,24},{4,28},{8,16},{12,20},{16,8},{20,12},{24,0},{28,4},{1,25},{... | collective-permute-start | bytes 98312 | tf_op jit(solution)/shard_map/ppermute | solution.py:242
  11.9 3.9 %collective-permute-start.2 = (bf16[32,512]{1,0:T(8,128)(2,1)S(1)}, bf16[32,512]{1,0:T(8,128)(2,1)S(1)}, u32[]{:S(2)}, u32[]{:S(2)}) collective-permute-start(bf16[32,512]{1,0:T(8,128)(2,1)S(1)} %shard_map.104), channel_id=1, source_target_pairs={{0,16},{4,20},{8,24},{12,28},{16,0},{20,4},{24,8},{28,12},{1,17},{... | collective-permute-start | bytes 98312 | tf_op jit(solution)/shard_map/ppermute | solution.py:242
  12.4 3.9 %collective-permute-start.1 = (bf16[32,512]{1,0:T(8,128)(2,1)S(1)}, bf16[32,512]{1,0:T(8,128)(2,1)S(1)}, u32[]{:S(2)}, u32[]{:S(2)}) collective-permute-start(bf16[32,512]{1,0:T(8,128)(2,1)S(1)} %shard_map.104), channel_id=1, source_target_pairs={{0,8},{4,12},{8,0},{12,4},{16,24},{20,28},{24,16},{28,20},{1,9},{5... | collective-permute-start | bytes 98312 | tf_op jit(solution)/shard_map/ppermute | solution.py:242
  18.3 6.4 %copy-start.1 = (bf16[32,8192]{1,0:T(8,128)(2,1)S(1)}, bf16[32,8192]{1,0:T(8,128)(2,1)}, u32[]{:S(2)}) copy-start(bf16[32,8192]{1,0:T(8,128)(2,1)} %own_ref.1) | copy-start | bytes 1572868
  19.1 9.3 %collective-permute-start.5 = (bf16[32,4096]{1,0:T(8,128)(2,1)S(1)}, bf16[32,4096]{1,0:T(8,128)(2,1)S(1)}, u32[]{:S(2)}, u32[]{:S(2)}) collective-permute-start(bf16[32,4096]{1,0:T(8,128)(2,1)S(1)} %shard_map.107), channel_id=1, source_target_pairs={{0,1},{1,0},{2,3},{3,2},{4,5},{5,4},{6,7},{7,6},{8,9},{9,8},{10,11... | collective-permute-start | bytes 786440 | tf_op jit(solution)/shard_map/ppermute | solution.py:246
  20.5 8.7 %collective-permute-start.8 = (bf16[32,4096]{1,0:T(8,128)(2,1)S(1)}, bf16[32,4096]{1,0:T(8,128)(2,1)S(1)}, u32[]{:S(2)}, u32[]{:S(2)}) collective-permute-start(bf16[32,4096]{1,0:T(8,128)(2,1)S(1)} %get-tuple-element.56), channel_id=1, source_target_pairs={{1,2},{2,1},{0,0},{3,3},{5,6},{6,5},{4,4},{7,7},{9,10},{10,9},{8,8... | collective-permute-start | bytes 786440 | tf_op jit(solution)/shard_map/ppermute | solution.py:250
  21.2 13.1 %collective-permute-start.10 = (bf16[32,4096]{1,0:T(8,128)(2,1)S(1)}, bf16[32,4096]{1,0:T(8,128)(2,1)S(1)}, u32[]{:S(2)}, u32[]{:S(2)}) collective-permute-start(bf16[32,4096]{1,0:T(8,128)(2,1)S(1)} %shard_map.109), channel_id=1, source_target_pairs={{0,1},{1,0},{2,3},{3,2},{4,5},{5,4},{6,7},{7,6},{8,9},{9,8},{10,11... | collective-permute-start | bytes 786440 | tf_op jit(solution)/shard_map/ppermute | solution.py:246
  24.1 10.3 %collective-permute-start.12 = (bf16[32,4096]{1,0:T(8,128)(2,1)S(1)}, bf16[32,4096]{1,0:T(8,128)(2,1)S(1)}, u32[]{:S(2)}, u32[]{:S(2)}) collective-permute-start(bf16[32,4096]{1,0:T(8,128)(2,1)S(1)} %get-tuple-element.55), channel_id=1, source_target_pairs={{1,2},{2,1},{0,0},{3,3},{5,6},{6,5},{4,4},{7,7},{9,10},{10,9},{8,8... | collective-permute-start | bytes 786440 | tf_op jit(solution)/shard_map/ppermute | solution.py:250
  28.5 13.2 %collective-permute-start.7 = (bf16[32,4096]{1,0:T(8,128)(2,1)S(1)}, bf16[32,4096]{1,0:T(8,128)(2,1)S(1)}, u32[]{:S(2)}, u32[]{:S(2)}) collective-permute-start(bf16[32,4096]{1,0:T(8,128)(2,1)S(1)} %shard_map.111), channel_id=1, source_target_pairs={{1,2},{2,1},{0,0},{3,3},{5,6},{6,5},{4,4},{7,7},{9,10},{10,9},{8,8... | collective-permute-start | bytes 786440 | tf_op jit(solution)/shard_map/ppermute | solution.py:250
  29.2 11.0 %collective-permute-start.9 = (bf16[32,4096]{1,0:T(8,128)(2,1)S(1)}, bf16[32,4096]{1,0:T(8,128)(2,1)S(1)}, u32[]{:S(2)}, u32[]{:S(2)}) collective-permute-start(bf16[32,4096]{1,0:T(8,128)(2,1)S(1)} %shard_map.112), channel_id=1, source_target_pairs={{0,1},{1,0},{2,3},{3,2},{4,5},{5,4},{6,7},{7,6},{8,9},{9,8},{10,11... | collective-permute-start | bytes 786440 | tf_op jit(solution)/shard_map/ppermute | solution.py:246
  34.4 8.6 %collective-permute-start.13 = (bf16[32,4096]{1,0:T(8,128)(2,1)S(1)}, bf16[32,4096]{1,0:T(8,128)(2,1)S(1)}, u32[]{:S(2)}, u32[]{:S(2)}) collective-permute-start(bf16[32,4096]{1,0:T(8,128)(2,1)S(1)} %shard_map.117), channel_id=1, source_target_pairs={{0,1},{1,0},{2,3},{3,2},{4,5},{5,4},{6,7},{7,6},{8,9},{9,8},{10,11... | collective-permute-start | bytes 786440 | tf_op jit(solution)/shard_map/ppermute | solution.py:246
  38.1 5.8 %collective-permute-start.11 = (bf16[32,4096]{1,0:T(8,128)(2,1)S(1)}, bf16[32,4096]{1,0:T(8,128)(2,1)S(1)}, u32[]{:S(2)}, u32[]{:S(2)}) collective-permute-start(bf16[32,4096]{1,0:T(8,128)(2,1)S(1)} %shard_map.116), channel_id=1, source_target_pairs={{1,2},{2,1},{0,0},{3,3},{5,6},{6,5},{4,4},{7,7},{9,10},{10,9},{8,8... | collective-permute-start | bytes 786440 | tf_op jit(solution)/shard_map/ppermute | solution.py:250
  43.1 13.4 %collective-permute-start.15 = (bf16[32,8192]{1,0:T(8,128)(2,1)S(1)}, bf16[32,8192]{1,0:T(8,128)(2,1)S(1)}, u32[]{:S(2)}, u32[]{:S(2)}) collective-permute-start(bf16[32,8192]{1,0:T(8,128)(2,1)S(1)} %shard_map.118), channel_id=1, source_target_pairs={{1,2},{2,1},{0,0},{3,3},{5,6},{6,5},{4,4},{7,7},{9,10},{10,9},{8,8... | collective-permute-start | bytes 1572872 | tf_op jit(solution)/shard_map/ppermute | solution.py:250
  44.0 16.2 %collective-permute-start.14 = (bf16[32,8192]{1,0:T(8,128)(2,1)S(1)}, bf16[32,8192]{1,0:T(8,128)(2,1)S(1)}, u32[]{:S(2)}, u32[]{:S(2)}) collective-permute-start(bf16[32,8192]{1,0:T(8,128)(2,1)S(1)} %shard_map.119), channel_id=1, source_target_pairs={{0,1},{1,0},{2,3},{3,2},{4,5},{5,4},{6,7},{7,6},{8,9},{9,8},{10,11... | collective-permute-start | bytes 1572872 | tf_op jit(solution)/shard_map/ppermute | solution.py:246
  50.8 1.4 %collective-permute-start.16 = (f32[56,512]{1,0:T(8,128)S(1)}, f32[56,512]{1,0:T(8,128)S(1)}, u32[]{:S(2)}, u32[]{:S(2)}) collective-permute-start(f32[56,512]{1,0:T(8,128)S(1)} %get-tuple-element.48.own_ref), channel_id=1, source_target_pairs={{0,4},{4,0},{8,12},{12,8},{16,20},{20,16},{24,28},{28,24},{1,5},{5... | collective-permute-start | bytes 344072 | tf_op jit(solution)/shard_map/ppermute | solution.py:238
  52.3 4.3 %collective-permute-start.17 = (bf16[64,512]{1,0:T(8,128)(2,1)S(1)}, bf16[64,512]{1,0:T(8,128)(2,1)S(1)}, u32[]{:S(2)}, u32[]{:S(2)}) collective-permute-start(bf16[64,512]{1,0:T(8,128)(2,1)S(1)} %shard_map.122.refs_7_), channel_id=1, source_target_pairs={{0,8},{4,12},{8,0},{12,4},{16,24},{20,28},{24,16},{28,20},{1,9},{5... | collective-permute-start | bytes 196616 | tf_op jit(solution)/shard_map/ppermute | solution.py:242
  53.8 5.2 %collective-permute-start.19 = (bf16[64,512]{1,0:T(8,128)(2,1)S(1)}, bf16[64,512]{1,0:T(8,128)(2,1)S(1)}, u32[]{:S(2)}, u32[]{:S(2)}) collective-permute-start(bf16[64,512]{1,0:T(8,128)(2,1)S(1)} %shard_map.122.refs_7_), channel_id=1, source_target_pairs={{0,24},{4,28},{8,16},{12,20},{16,8},{20,12},{24,0},{28,4},{1,25},{... | collective-permute-start | bytes 196616 | tf_op jit(solution)/shard_map/ppermute | solution.py:242
  55.3 4.8 %collective-permute-start.18 = (bf16[64,512]{1,0:T(8,128)(2,1)S(1)}, bf16[64,512]{1,0:T(8,128)(2,1)S(1)}, u32[]{:S(2)}, u32[]{:S(2)}) collective-permute-start(bf16[64,512]{1,0:T(8,128)(2,1)S(1)} %shard_map.122.refs_7_), channel_id=1, source_target_pairs={{0,16},{4,20},{8,24},{12,28},{16,0},{20,4},{24,8},{28,12},{1,17},{... | collective-permute-start | bytes 196616 | tf_op jit(solution)/shard_map/ppermute | solution.py:242

commit v2 on v0

--- a/solution.py
+++ b/solution.py
@@ -11,17 +11,18 @@
 F32 = jnp.float32
 BF16 = jnp.bfloat16
 STEP = 8
+LOCAL_FLOPS = 1_000_000_000
 CLEAR_FLOPS = 4_000_000_000
 HALVES = 2
 
 
-def call(body, outs, scratch, args, flops=1024):
+def call(body, outs, scratch, args, flops=1024, place=pltpu.VMEM):
     whole = pl.BlockSpec(memory_space=pltpu.VMEM)
     return pl.pallas_call(
         body,
         out_shape=outs,
         in_specs=[whole] * len(args),
-        out_specs=[whole] * len(outs),
+        out_specs=[pl.BlockSpec(memory_space=place)] * len(outs),
         scratch_shapes=scratch,
         compiler_params=pltpu.CompilerParams(vmem_limit_bytes=12 << 20),
         cost_estimate=pl.CostEstimate(flops=flops, bytes_accessed=1024, transcendentals=0),
@@ -96,17 +97,17 @@
     a_chunk = jnp.exp(-(rate * tok))
     index = lax.axis_index("ctx")
     pair = index // 2
+    second = index % 2 == 1
     h = jnp.zeros_like(a)
     q = jnp.zeros_like(a)
-    for j, far in enumerate(far_refs, 1):
+    both = [chosen_from(far_refs, second, pl.ds(at * modes, modes)) for at in range(2)]
+    for j, (far_h, far_q) in enumerate(zip(*both), 1):
         apart = pair - (pair ^ j)
         since = (jnp.maximum(apart - 1, 0) * (2 * tok)).astype(F32)
-        far_h, far_q = part_of(far, 0, modes).astype(F32), part_of(far, 1, modes).astype(F32)
         far_h, far_q = advance(far_h, far_q, jnp.exp(-(rate * since)), since)
         h = h + jnp.where(apart > 0, far_h, 0.0)
         q = q + jnp.where(apart > 0, far_q, 0.0)
     h_late, q_late = advance(h, q, a_chunk, tok)
-    second = index % 2 == 1
     h = jnp.where(second, h_late + part_of(other_ref, 0, modes), h)
     q = jnp.where(second, q_late + part_of(other_ref, 1, modes), q)
     start_ref[pl.ds(0, modes), :] = h
@@ -190,9 +191,25 @@
     pair_ref[pl.ds(3 * modes, modes), :] = jnp.broadcast_to(direct, own.shape).astype(BF16)
 
 
-def input_body(seq, modes, g_f, table_ref, other_ref, pair_ref, *refs):
+def local_body(modes, g_f, table_ref, y_f):
+    tok = g_f.shape[0]
+    c = part_of(table_ref, 2, modes)
+    a = jnp.exp(-part_of(table_ref, 0, modes))
+
+    def steps(block, z):
+        for inner in range(STEP):
+            at = tok - 1 - (block * STEP + inner)
+            z = a * z + row_of(g_f, at, a)
+            y_f[pl.ds(at, 1), :] = jnp.sum(c * z, axis=0, keepdims=True)
+        return z
+
+    lax.fori_loop(0, tok // STEP, steps, jnp.zeros_like(a))
+    y_f[...] = y_f[...] + table_ref[pl.ds(3 * modes, 1), :] * g_f[...]
+
+
+def input_body(seq, modes, own_f, table_ref, other_ref, pair_ref, *refs):
     *far_refs, grad_ref, by_res_ref, by_log_ref, by_skip_ref, y_f = refs
-    tok = g_f.shape[0]
+    tok = own_f.shape[0]
     rate = part_of(table_ref, 0, modes)
     norm = part_of(table_ref, 1, modes)
     c = part_of(table_ref, 2, modes)
@@ -200,27 +217,26 @@
     a_chunk = jnp.exp(-(rate * tok))
     index = lax.axis_index("ctx")
     pair = index // 2
+    second = index % 2 == 1
     z = jnp.zeros_like(a)
-    for j, far in enumerate(far_refs, 1):
+    for j, far_z in enumerate(chosen_from(far_refs, second, pl.ds(0, modes)), 1):
         apart = (pair ^ j) - pair
         until = (jnp.maximum(apart - 1, 0) * (2 * tok)).astype(F32)
-        decay = jnp.exp(-(rate * until))
-        z = z + jnp.where(apart > 0, decay * far[pl.ds(0, modes), :].astype(F32), 0.0)
+        z = z + jnp.where(apart > 0, jnp.exp(-(rate * until)) * far_z, 0.0)
     z = jnp.where(index % 2 == 0, a_chunk * z + part_of(other_ref, 0, modes), z)
 
-    def steps(block, z):
+    def steps(block, w):
         for inner in range(STEP):
-            at = tok - 1 - (block * STEP + inner)
-            z = a * z + row_of(g_f, at, a)
-            y_f[pl.ds(at, 1), :] = jnp.sum(c * z, axis=0, keepdims=True)
-        return z
-
-    lax.fori_loop(0, tok // STEP, steps, z)
-    grad_ref[...] = (y_f[...] + table_ref[pl.ds(3 * modes, 1), :] * g_f[...]).astype(BF16)
+            w = a * w
+            y_f[pl.ds(tok - 1 - (block * STEP + inner), 1), :] = jnp.sum(w, axis=0, keepdims=True)
+        return w
+
+    lax.fori_loop(0, tok // STEP, steps, c * z)
+    grad_ref[...] = (own_f[...] + y_f[...]).astype(BF16)
     rest = pl.ds(modes, 3 * modes)
     total = pair_ref[rest, :].astype(F32)
-    for far in far_refs:
-        total = total + far[rest, :].astype(F32)
+    for far in chosen_from(far_refs, second, rest):
+        total = total + far
     scale = 1.0 / math.sqrt(seq)
     by_res_ref[...] = scale * (norm * total[:modes])
     by_log_ref[...] = scale * (c * total[modes:2 * modes])
@@ -232,7 +248,18 @@
 
 
 def from_pairs(array, blocks):
-    return [lax.ppermute(array, "ctx", [(i, i ^ (2 * j)) for i in range(blocks)]) for j in range(1, blocks // 2)]
+    if blocks != 8:
+        return [lax.ppermute(array, "ctx", [(i, i ^ (2 * j)) for i in range(blocks)]) for j in range(1, blocks // 2)]
+    side = lax.ppermute(array, "ctx", [(i, i ^ (4 if i % 2 else 2)) for i in range(blocks)])
+    corner = lax.ppermute(array, "ctx", [(i, i ^ 6) for i in range(blocks)])
+    return [side, from_other_core(side, blocks), corner]
+
+
+def chosen_from(refs, second, at):
+    if len(refs) != 3:
+        return [ref[at, :].astype(F32) for ref in refs]
+    mine, swapped, corner = (ref[at, :].astype(F32) for ref in refs)
+    return [jnp.where(second, swapped, mine), jnp.where(second, mine, swapped), corner]
 
 
 def outer(array):
@@ -347,12 +374,17 @@
 
 
 def total_body(spans, *refs):
-    *share_refs, last_ref, near_ref, out_ref = refs
+    *share_refs, last_ref, near_ref, out_far, out_ref, sems = refs
     rows = out_ref.shape[0]
     end = at_end()
-    for share_ref, span in zip(share_refs, spans):
+    copies = []
+    for at, (share_ref, span) in enumerate(zip(share_refs, spans)):
         total = share_rows(share_ref, lax.axis_index("tp"), rows).astype(F32) + last_ref[:, span].astype(F32)
         out_ref[:, span] = (total + jnp.where(end, 0.0, near_ref[:, span].astype(F32))).astype(BF16)
+        copies.append(pltpu.make_async_copy(out_ref.at[:, span], out_far.at[:, span], sems.at[at]))
+        copies[-1].start()
+    for copy in copies:
+        copy.wait()
 
 
 def line_of_four(out_grad, out_weight, merged, x_f, states_of, grads_of):
@@ -415,7 +447,11 @@
     g_f, sums = grads_of([g_near, *g_far], places, states)
     last = outer(ready)
     to_near = inner(near)
-    (out,) = call(functools.partial(total_body, spans), whole, [], [*shares, last, to_near])
+    (out,) = call(
+        functools.partial(total_body, spans), whole,
+        [pltpu.VMEM((rows, width), BF16), pltpu.SemaphoreType.DMA((len(spans),))],
+        [*shares, last, to_near], place=pl.ANY,
+    )
     return out, g_f, sums
 
 
@@ -438,11 +474,9 @@
     state = lanes((modes, chans))
     token_f = pltpu.VMEM((tok, chans), F32)
 
-    (zero,) = call(clear_body, [state], [], [], flops=CLEAR_FLOPS)
-    out_grad = lax.optimization_barrier((out_grad, zero))[0]
     x_f, rate, ends = call(
         functools.partial(ends_body, seq), [lanes((tok, chans)), state, lanes((2 * modes, chans))], [],
-        [inputs, log_rate.T, zero],
+        [inputs, log_rate.T, *call(clear_body, [state], [], [], flops=CLEAR_FLOPS)], flops=2_000_000_000,
     )
     (table,) = call(
         table_body, [lanes((3 * modes + 8, chans))], [], [rate, residue.T, skip[None, :]], flops=1_000_000_000
@@ -471,6 +505,7 @@
 
     reduce = line_of_four if parts == 4 else any_axis
     out, g_f, sums = reduce(out_grad, out_weight, merged, x_f, states_of, grads_of)
+    (own_grad,) = call(functools.partial(local_body, modes), [lanes((tok, chans))], [], [g_f, table], flops=LOCAL_FLOPS)
     other_sums = from_other_core(sums, blocks)
     (pair_sums,) = call(
         functools.partial(pair_sums_body, tok, modes), [jax.ShapeDtypeStruct((4 * modes, chans), BF16)], [],
@@ -479,7 +514,7 @@
     grad_input, by_res, by_log, by_skip = call(
         functools.partial(input_body, seq, modes),
         [jax.ShapeDtypeStruct((tok, chans), BF16), state, state, lanes((1, chans))], [token_f],
-        [g_f, table, other_sums, pair_sums, *from_pairs(pair_sums, blocks)],
+        [own_grad, table, other_sums, pair_sums, *from_pairs(pair_sums, blocks)],
     )
     return out, grad_input, by_res.T, by_log.T, by_skip[0]
 

time: 61.4 us -> 59.6 us (0.971)
  waiting for transfers between devices: 13.3 us -> 11.8 us
  local copies, waits for them, and re-layouts: 1.03 us -> 0.06 us
  Pallas kernels: 14.4 us -> 15.2 us
    ppermute x6 -> x4, waiting for transfers between devices: 6.86 us -> 5.82 us  [the longest x2 3.17 us: from_pairs(): corner = lax.ppermute(array, 'ctx', [(i, i ^ 6) for i in range(blocks)])]
    ppermute x6, starting transfers between devices: 4.18 us -> 5.2 us  [inner(): return lax.ppermute(array, 'tp', [(1, 2), (2, 1), (0, 0), (3, 3)])]
    ppermute x6 -> x4, starting transfers between devices: 7.11 us -> 6.09 us  [the longest x2 3.17 us: from_pairs(): lax.ppermute(array, 'ctx', [(i, i ^ (4 if i % 2 else 2)) for i in range(b...]
    unnamed x12, local copies, waits for them, and re-layouts: 0.99 us -> 0.03 us
    pallas_call x24 -> x25, Pallas kernels: 14.4 us -> 15.2 us  [call(): pl.pallas_call(body, out_shape=outs, in_specs=[whole] * len(args), out_sp...]
    ppermute x2 -> x4, waiting for transfers between devices: 2.55 us -> 2.56 us  [from_other_core(): return lax.ppermute(array, 'ctx', [(i, i ^ 1) for i in range(blocks)])]
  transfers between devices with their start and end apart: 20 -> 20, of which waited for: 11 -> 9; matrix products, arithmetic and copies ran while one was open for 0% -> 0% of each run, Pallas kernels for 22% -> 24%
where the time goes in v2:
time: 59.6 us; the launch traced here: 59.4 us
  starting transfers between devices  31.3 us (53%)
  Pallas kernels  15.2 us (26%)
  waiting for transfers between devices  11.8 us (20%)
  between operations  0.96 us (2%)
    ppermute x6, starting transfers between devices, outer(): return lax.ppermute(array, 'tp', [(0, 1), (1, 0), (2, 3), (3, 2)])  19.9 us
    pallas_call x25, Pallas kernels, call(): pl.pallas_call(body, out_shape=outs, in_specs=[whole] * len(args), out_sp...  15.2 us
    ppermute x6, starting transfers between devices, inner(): return lax.ppermute(array, 'tp', [(1, 2), (2, 1), (0, 0), (3, 3)])  5.2 us
    ppermute x6, waiting for transfers between devices, outer(): return lax.ppermute(array, 'tp', [(0, 1), (1, 0), (2, 3), (3, 2)])  3.41 us
    ppermute x2, waiting for transfers between devices, from_pairs(): corner = lax.ppermute(array, 'ctx', [(i, i ^ 6) for i in range(blocks)])  3.17 us
    ppermute x2, starting transfers between devices, from_pairs(): lax.ppermute(array, 'ctx', [(i, i ^ (4 if i % 2 else 2)) for i in range(b...  3.17 us
    ppermute x2, starting transfers between devices, from_pairs(): corner = lax.ppermute(array, 'ctx', [(i, i ^ 6) for i in range(blocks)])  2.93 us
    ppermute x2, waiting for transfers between devices, from_pairs(): lax.ppermute(array, 'ctx', [(i, i ^ (4 if i % 2 else 2)) for i in range(b...  2.64 us
  transfers between devices with their start and end apart: 20, of which 9 were waited for; matrix products, arithmetic and copies ran while one was open for 0% of the time, Pallas kernels for 24%

profile of v2, /device:TPU:0, one launch (start us, length us, event | category | flops | bytes accessed | tf_op | source)
XLA Modules:
  0.0 59.4 jit_solution(15407224576460554102)
XLA Ops:
  0.7 1.8 %collective-permute-start.4 = (bf16[32,8192]{1,0:T(8,128)(2,1)}, bf16[32,8192]{1,0:T(8,128)(2,1)S(1)}, u32[]{:S(2)}, u32[]{:S(2)}) collective-permute-start(bf16[32,8192]{1,0:T(8,128)(2,1)} %own_ref.1), channel_id=1, source_target_pairs={{1,2},{2,1},{0,0},{3,3},{5,6},{6,5},{4,4},{7,7},{9,10},{10,9},{8,8... | collective-permute-start | bytes 1572872 | tf_op jit(solution)/shard_map/ppermute | solution.py:270
  2.5 4.9 %collective-permute-start.6 = (bf16[32,8192]{1,0:T(8,128)(2,1)}, bf16[32,8192]{1,0:T(8,128)(2,1)S(1)}, u32[]{:S(2)}, u32[]{:S(2)}) collective-permute-start(bf16[32,8192]{1,0:T(8,128)(2,1)} %own_ref.1), channel_id=1, source_target_pairs={{0,1},{1,0},{2,3},{3,2},{4,5},{5,4},{6,7},{7,6},{8,9},{9,8},{10,11... | collective-permute-start | bytes 1572872 | tf_op jit(solution)/shard_map/ppermute | solution.py:266
  8.1 1.2 %collective-permute-done.other_ref = f32[32,512]{1,0:T(8,128)S(1)} collective-permute-done((f32[32,512]{1,0:T(8,128)S(1)}, f32[32,512]{1,0:T(8,128)S(1)}, u32[]{:S(2)}, u32[]{:S(2)}) %collective-permute-start) | collective-permute-done | bytes 65568 | tf_op jit(solution)/shard_map/ppermute | solution.py:247
  9.4 1.6 %collective-permute-start.1 = (bf16[32,512]{1,0:T(8,128)(2,1)S(1)}, bf16[32,512]{1,0:T(8,128)(2,1)S(1)}, u32[]{:S(2)}, u32[]{:S(2)}) collective-permute-start(bf16[32,512]{1,0:T(8,128)(2,1)S(1)} %shard_map.104), channel_id=1, source_target_pairs={{0,8},{4,20},{8,0},{12,28},{16,24},{20,4},{24,16},{28,12},{1,9},{5... | collective-permute-start | bytes 98312 | tf_op jit(solution)/shard_map/ppermute | solution.py:253
  10.9 1.5 %collective-permute-start.3 = (bf16[32,512]{1,0:T(8,128)(2,1)S(1)}, bf16[32,512]{1,0:T(8,128)(2,1)S(1)}, u32[]{:S(2)}, u32[]{:S(2)}) collective-permute-start(bf16[32,512]{1,0:T(8,128)(2,1)S(1)} %shard_map.104), channel_id=1, source_target_pairs={{0,24},{4,28},{8,16},{12,20},{16,8},{20,12},{24,0},{28,4},{1,25},{... | collective-permute-start | bytes 98312 | tf_op jit(solution)/shard_map/ppermute | solution.py:254
  12.4 0.9 %collective-permute-done.1.refs_0_ = bf16[32,512]{1,0:T(8,128)(2,1)S(1)} collective-permute-done((bf16[32,512]{1,0:T(8,128)(2,1)S(1)}, bf16[32,512]{1,0:T(8,128)(2,1)S(1)}, u32[]{:S(2)}, u32[]{:S(2)}) %collective-permute-start.1) | collective-permute-done | bytes 32800 | tf_op jit(solution)/shard_map/ppermute | solution.py:253
  13.4 2.4 %collective-permute-done.3.refs_2_ = bf16[32,512]{1,0:T(8,128)(2,1)S(1)} collective-permute-done((bf16[32,512]{1,0:T(8,128)(2,1)S(1)}, bf16[32,512]{1,0:T(8,128)(2,1)S(1)}, u32[]{:S(2)}, u32[]{:S(2)}) %collective-permute-start.3) | collective-permute-done | bytes 32800 | tf_op jit(solution)/shard_map/ppermute | solution.py:254
  15.7 1.2 %shard_map.105 = (bf16[128,512]{1,0:T(8,128)(2,1)S(1)}, f32[32,512]{1,0:T(8,128)S(1)}) custom-call(f32[128,512]{1,0:T(8,128)S(1)} %get-tuple-element.39.x_f, f32[56,512]{1,0:T(8,128)S(1)} %shard_map.103.table_ref, f32[32,512]{1,0:T(8,128)S(1)} %collective-permute-done.other_ref, bf16[32,512]{1,0:T(8,128)(2,1)S(1)} %collective-permute-done.1.refs_0_, ...), custom_call_target="tpu_custom_call" | custom-call | flops 1024 | bytes 1024 | tf_op jit(solution)/shard_map/pallas_call | solution.py:21
  17.0 0.7 %shard_map.106.share_ref.refs_0_ = bf16[128,4096]{1,0:T(8,128)(2,1)S(1)} custom-call(bf16[128,512]{1,0:T(8,128)(2,1)S(1)} %get-tuple-element.34.merged_ref, bf16[512,8192]{1,0:T(8,128)(2,1)S(1)} %copy-done), custom_call_target="tpu_custom_call" | custom-call | flops 1024 | bytes 1024 | tf_op jit(solution)/shard_map/pallas_call | solution.py:21
  17.8 0.7 %shard_map.108.share_ref.refs_1_.refs_2_ = bf16[128,4096]{1,0:T(8,128)(2,1)S(1)} custom-call(bf16[128,512]{1,0:T(8,128)(2,1)S(1)} %get-tuple-element.34.merged_ref, bf16[512,8192]{1,0:T(8,128)(2,1)S(1)} %copy-done), custom_call_target="tpu_custom_call" | custom-call | flops 1024 | bytes 1024 | tf_op jit(solution)/shard_map/pallas_call | solution.py:21
  18.5 1.9 %collective-permute-start.5 = (bf16[32,4096]{1,0:T(8,128)(2,1)S(1)}, bf16[32,4096]{1,0:T(8,128)(2,1)S(1)}, u32[]{:S(2)}, u32[]{:S(2)}) collective-permute-start(bf16[32,4096]{1,0:T(8,128)(2,1)S(1)} %shard_map.107), channel_id=1, source_target_pairs={{0,1},{1,0},{2,3},{3,2},{4,5},{5,4},{6,7},{7,6},{8,9},{9,8},{10,11... | collective-permute-start | bytes 786440 | tf_op jit(solution)/shard_map/ppermute | solution.py:266
  20.5 0.7 %collective-permute-start.8 = (bf16[32,4096]{1,0:T(8,128)(2,1)S(1)}, bf16[32,4096]{1,0:T(8,128)(2,1)S(1)}, u32[]{:S(2)}, u32[]{:S(2)}) collective-permute-start(bf16[32,4096]{1,0:T(8,128)(2,1)S(1)} %get-tuple-element.56), channel_id=1, source_target_pairs={{1,2},{2,1},{0,0},{3,3},{5,6},{6,5},{4,4},{7,7},{9,10},{10,9},{8,8... | collective-permute-start | bytes 786440 | tf_op jit(solution)/shard_map/ppermute | solution.py:270
  21.2 2.9 %collective-permute-start.10 = (bf16[32,4096]{1,0:T(8,128)(2,1)S(1)}, bf16[32,4096]{1,0:T(8,128)(2,1)S(1)}, u32[]{:S(2)}, u32[]{:S(2)}) collective-permute-start(bf16[32,4096]{1,0:T(8,128)(2,1)S(1)} %shard_map.109), channel_id=1, source_target_pairs={{0,1},{1,0},{2,3},{3,2},{4,5},{5,4},{6,7},{7,6},{8,9},{9,8},{10,11... | collective-permute-start | bytes 786440 | tf_op jit(solution)/shard_map/ppermute | solution.py:266
  24.8 2.6 %shard_map.110.refs_0_ = f32[64,512]{1,0:T(8,128)S(1)} custom-call(bf16[32,8192]{1,0:T(8,128)(2,1)S(1)} %copy-done.1, bf16[32,8192]{1,0:T(8,128)(2,1)S(1)} %collective-permute-done.6.beside_ref, bf16[512,8192]{1,0:T(8,128)(2,1)S(1)} %copy-done), custom_call_target="tpu_custom_call" | custom-call | flops 1024 | bytes 1024 | tf_op jit(solution)/shard_map/pallas_call | solution.py:21
  28.6 4.7 %collective-permute-start.9 = (bf16[32,4096]{1,0:T(8,128)(2,1)S(1)}, bf16[32,4096]{1,0:T(8,128)(2,1)S(1)}, u32[]{:S(2)}, u32[]{:S(2)}) collective-permute-start(bf16[32,4096]{1,0:T(8,128)(2,1)S(1)} %shard_map.112), channel_id=1, source_target_pairs={{0,1},{1,0},{2,3},{3,2},{4,5},{5,4},{6,7},{7,6},{8,9},{9,8},{10,11... | collective-permute-start | bytes 786440 | tf_op jit(solution)/shard_map/ppermute | solution.py:266
  33.3 0.9 %shard_map.115 = (f32[2048,512]{1,0:T(8,128)S(1)}, f32[2048,512]{1,0:T(8,128)S(1)}) custom-call(f32[128,512]{1,0:T(8,128)S(1)} %get-tuple-element.39.x_f, f32[56,512]{1,0:T(8,128)S(1)} %shard_map.103.table_ref, f32[32,512]{1,0:T(8,128)S(1)} %get-tuple-element.40.start_ref), custom_call_target="tpu_custom_call" | custom-call | flops 1024 | bytes 1024 | tf_op jit(solution)/shard_map/pallas_call | solution.py:21
  34.4 3.4 %collective-permute-start.13 = (bf16[32,4096]{1,0:T(8,128)(2,1)S(1)}, bf16[32,4096]{1,0:T(8,128)(2,1)S(1)}, u32[]{:S(2)}, u32[]{:S(2)}) collective-permute-start(bf16[32,4096]{1,0:T(8,128)(2,1)S(1)} %shard_map.118), channel_id=1, source_target_pairs={{0,1},{1,0},{2,3},{3,2},{4,5},{5,4},{6,7},{7,6},{8,9},{9,8},{10,11... | collective-permute-start | bytes 786440 | tf_op jit(solution)/shard_map/ppermute | solution.py:266
  38.5 1.7 %collective-permute-done.9.third_ref.refs_1_ = bf16[32,4096]{1,0:T(8,128)(2,1)S(1)} collective-permute-done((bf16[32,4096]{1,0:T(8,128)(2,1)S(1)}, bf16[32,4096]{1,0:T(8,128)(2,1)S(1)}, u32[]{:S(2)}, u32[]{:S(2)}) %collective-permute-start.9) | collective-permute-done | bytes 262176 | tf_op jit(solution)/shard_map/ppermute | solution.py:266
  40.2 1.4 %shard_map.113.refs_0_ = f32[64,512]{1,0:T(8,128)S(1)} custom-call(bf16[32,4096]{1,0:T(8,128)(2,1)S(1)} %collective-permute-done.5.got_ref.second_ref, bf16[32,4096]{1,0:T(8,128)(2,1)S(1)} %collective-permute-done.9.third_ref.refs_1_, bf16[32,8192]{1,0:T(8,128)(2,1)S(1)} %collective-permute-done.4.passing_ref.across_ref, ...), custom_call_target="tpu_custom_call" | custom-call | flops 1024 | bytes 1024 | tf_op jit(solution)/shard_map/pallas_call | solution.py:21
  41.7 1.3 %collective-permute-done.13.refs_3_.third_ref = bf16[32,4096]{1,0:T(8,128)(2,1)S(1)} collective-permute-done((bf16[32,4096]{1,0:T(8,128)(2,1)S(1)}, bf16[32,4096]{1,0:T(8,128)(2,1)S(1)}, u32[]{:S(2)}, u32[]{:S(2)}) %collective-permute-start.13) | collective-permute-done | bytes 262176 | tf_op jit(solution)/shard_map/ppermute | solution.py:266
  43.0 1.4 %shard_map.120.refs_1_ = f32[64,512]{1,0:T(8,128)S(1)} custom-call(bf16[32,4096]{1,0:T(8,128)(2,1)S(1)} %collective-permute-done.10.got_ref.second_ref, bf16[32,4096]{1,0:T(8,128)(2,1)S(1)} %collective-permute-done.13.refs_3_.third_ref, bf16[32,8192]{1,0:T(8,128)(2,1)S(1)} %collective-permute-done.4.passing_ref.across_ref, ...), custom_call_target="tpu_custom_call" | custom-call | flops 1024 | bytes 1024 | tf_op jit(solution)/shard_map/pallas_call | solution.py:21
  44.7 2.1 %collective-permute-start.14 = (bf16[32,8192]{1,0:T(8,128)(2,1)S(1)}, bf16[32,8192]{1,0:T(8,128)(2,1)S(1)}, u32[]{:S(2)}, u32[]{:S(2)}) collective-permute-start(bf16[32,8192]{1,0:T(8,128)(2,1)S(1)} %shard_map.117), channel_id=1, source_target_pairs={{0,1},{1,0},{2,3},{3,2},{4,5},{5,4},{6,7},{7,6},{8,9},{9,8},{10,11... | collective-permute-start | bytes 1572872 | tf_op jit(solution)/shard_map/ppermute | solution.py:266
  46.8 0.7 %collective-permute-start.15 = (bf16[32,8192]{1,0:T(8,128)(2,1)S(1)}, bf16[32,8192]{1,0:T(8,128)(2,1)S(1)}, u32[]{:S(2)}, u32[]{:S(2)}) collective-permute-start(bf16[32,8192]{1,0:T(8,128)(2,1)S(1)} %shard_map.119), channel_id=1, source_target_pairs={{1,2},{2,1},{0,0},{3,3},{5,6},{6,5},{4,4},{7,7},{9,10},{10,9},{8,8... | collective-permute-start | bytes 1572872 | tf_op jit(solution)/shard_map/ppermute | solution.py:270
  47.5 1.2 %shard_map.122 = (f32[128,512]{1,0:T(8,128)S(1)}, f32[56,512]{1,0:T(8,128)S(1)}) custom-call(f32[128,512]{1,0:T(8,128)S(1)} %get-tuple-element.39.x_f, f32[56,512]{1,0:T(8,128)S(1)} %shard_map.103.table_ref, f32[2048,512]{1,0:T(8,128)S(1)} %get-tuple-element.41.h_ref, f32[2048,512]{1,0:T(8,128)S(1)} %get-tuple-element.42.q_ref, ...), custom_call_target="tpu_custom_call" | custom-call | flops 1024 | bytes 1024 | tf_op jit(solution)/shard_map/pallas_call | solution.py:21
  48.7 1.3 %collective-permute-done.16.other_ref = f32[56,512]{1,0:T(8,128)S(1)} collective-permute-done((f32[56,512]{1,0:T(8,128)S(1)}, f32[56,512]{1,0:T(8,128)S(1)}, u32[]{:S(2)}, u32[]{:S(2)}) %collective-permute-start.16) | collective-permute-done | bytes 114720 | tf_op jit(solution)/shard_map/ppermute | solution.py:247
  50.1 1.6 %collective-permute-start.17 = (bf16[64,512]{1,0:T(8,128)(2,1)S(1)}, bf16[64,512]{1,0:T(8,128)(2,1)S(1)}, u32[]{:S(2)}, u32[]{:S(2)}) collective-permute-start(bf16[64,512]{1,0:T(8,128)(2,1)S(1)} %shard_map.124.pair_ref), channel_id=1, source_target_pairs={{0,8},{4,20},{8,0},{12,28},{16,24},{20,4},{24,16},{28,12},{1,9},{5... | collective-permute-start | bytes 196616 | tf_op jit(solution)/shard_map/ppermute | solution.py:253
  51.7 1.4 %collective-permute-start.19 = (bf16[64,512]{1,0:T(8,128)(2,1)S(1)}, bf16[64,512]{1,0:T(8,128)(2,1)S(1)}, u32[]{:S(2)}, u32[]{:S(2)}) collective-permute-start(bf16[64,512]{1,0:T(8,128)(2,1)S(1)} %shard_map.124.pair_ref), channel_id=1, source_target_pairs={{0,24},{4,28},{8,16},{12,20},{16,8},{20,12},{24,0},{28,4},{1,25},{... | collective-permute-start | bytes 196616 | tf_op jit(solution)/shard_map/ppermute | solution.py:254
  53.1 1.7 %collective-permute-done.17.refs_0_ = bf16[64,512]{1,0:T(8,128)(2,1)S(1)} collective-permute-done((bf16[64,512]{1,0:T(8,128)(2,1)S(1)}, bf16[64,512]{1,0:T(8,128)(2,1)S(1)}, u32[]{:S(2)}, u32[]{:S(2)}) %collective-permute-start.17) | collective-permute-done | bytes 65568 | tf_op jit(solution)/shard_map/ppermute | solution.py:253
  54.8 1.2 %shard_map.123.own_f = f32[128,512]{1,0:T(8,128)S(1)} custom-call(f32[128,512]{1,0:T(8,128)S(1)} %get-tuple-element.49.g_f, f32[56,512]{1,0:T(8,128)S(1)} %shard_map.103.table_ref), custom_call_target="tpu_custom_call" | custom-call | flops 1000000000 | bytes 1024 | tf_op jit(solution)/shard_map/pallas_call | solution.py:21
  56.0 0.8 %collective-permute-done.19.refs_2_ = bf16[64,512]{1,0:T(8,128)(2,1)S(1)} collective-permute-done((bf16[64,512]{1,0:T(8,128)(2,1)S(1)}, bf16[64,512]{1,0:T(8,128)(2,1)S(1)}, u32[]{:S(2)}, u32[]{:S(2)}) %collective-permute-start.19) | collective-permute-done | bytes 65568 | tf_op jit(solution)/shard_map/ppermute | solution.py:254
  56.8 1.6 %shard_map.125 = (bf16[128,512]{1,0:T(8,128)(2,1)}, f32[16,512]{1,0:T(8,128)}, f32[16,512]{1,0:T(8,128)}, f32[1,512]{1,0:T(1,128)}) custom-call(f32[128,512]{1,0:T(8,128)S(1)} %shard_map.123.own_f, f32[56,512]{1,0:T(8,128)S(1)} %shard_map.103.table_ref, f32[56,512]{1,0:T(8,128)S(1)} %collective-permute-done.16.other_ref, ...), custom_call_target="tpu_custom_call" | custom-call | flops 1024 | bytes 1024 | tf_op jit(solution)/shard_map/pallas_call | solution.py:21
  58.4 1.0 %shard_map.121 = bf16[32,8192]{1,0:T(8,128)(2,1)} custom-call(bf16[128,4096]{1,0:T(8,128)(2,1)S(1)} %shard_map.106.share_ref.refs_0_, bf16[128,4096]{1,0:T(8,128)(2,1)S(1)} %shard_map.108.share_ref.refs_1_.refs_2_, bf16[32,8192]{1,0:T(8,128)(2,1)S(1)} %collective-permute-done.14.refs_2_, bf16[32,8192]{1,0:T(8,128)(2,1)S(1)} %collective-permute-done.15.refs_3_), custom_call_target="tpu_custom_call" | custom-call | flops 1024 | bytes 1024 | tf_op jit(solution)/shard_map/pallas_call | solution.py:21
  (46 shorter events, 3.9 us)
Async XLA Ops:
  0.6 6.7 %copy-start.3 = (f32[512,16]{0,1:T(8,128)S(1)}, f32[512,16]{0,1:T(8,128)}, u32[]{:S(2)}) copy-start(f32[512,16]{0,1:T(8,128)} %param.8) | copy-start | bytes 98308
  0.6 6.7 %copy-start.2 = (bf16[128,512]{1,0:T(8,128)(2,1)S(1)}, bf16[128,512]{1,0:T(8,128)(2,1)}, u32[]{:S(2)}) copy-start(bf16[128,512]{1,0:T(8,128)(2,1)} %x_ref.1) | copy-start | bytes 393220
  0.7 17.1 %collective-permute-start.4 = (bf16[32,8192]{1,0:T(8,128)(2,1)}, bf16[32,8192]{1,0:T(8,128)(2,1)S(1)}, u32[]{:S(2)}, u32[]{:S(2)}) collective-permute-start(bf16[32,8192]{1,0:T(8,128)(2,1)} %own_ref.1), channel_id=1, source_target_pairs={{1,2},{2,1},{0,0},{3,3},{5,6},{6,5},{4,4},{7,7},{9,10},{10,9},{8,8... | collective-permute-start | bytes 1572872 | tf_op jit(solution)/shard_map/ppermute | solution.py:270
  2.5 17.9 %collective-permute-start.6 = (bf16[32,8192]{1,0:T(8,128)(2,1)}, bf16[32,8192]{1,0:T(8,128)(2,1)S(1)}, u32[]{:S(2)}, u32[]{:S(2)}) collective-permute-start(bf16[32,8192]{1,0:T(8,128)(2,1)} %own_ref.1), channel_id=1, source_target_pairs={{0,1},{1,0},{2,3},{3,2},{4,5},{5,4},{6,7},{7,6},{8,9},{9,8},{10,11... | collective-permute-start | bytes 1572872 | tf_op jit(solution)/shard_map/ppermute | solution.py:266
  7.4 6.0 %copy-start.4 = (f32[512,16]{0,1:T(8,128)S(1)}, f32[512,16]{0,1:T(8,128)}, u32[]{:S(2)}) copy-start(f32[512,16]{0,1:T(8,128)} %param.7) | copy-start | bytes 98308
  7.4 6.0 %copy-start.5 = (f32[512]{0:T(512)S(1)}, f32[512]{0:T(512)}, u32[]{:S(2)}) copy-start(f32[512]{0:T(512)} %param.9) | copy-start | bytes 6148
  7.4 9.6 %copy-start = (bf16[512,8192]{1,0:T(8,128)(2,1)S(1)}, bf16[512,8192]{1,0:T(8,128)(2,1)}, u32[]{:S(2)}) copy-start(bf16[512,8192]{1,0:T(8,128)(2,1)} %weight_ref.9) | copy-start | bytes 25165828
  8.0 1.3 %collective-permute-start = (f32[32,512]{1,0:T(8,128)S(1)}, f32[32,512]{1,0:T(8,128)S(1)}, u32[]{:S(2)}, u32[]{:S(2)}) collective-permute-start(f32[32,512]{1,0:T(8,128)S(1)} %get-tuple-element.32.own_ref), channel_id=1, source_target_pairs={{0,4},{4,0},{8,12},{12,8},{16,20},{20,16},{24,28},{28,24},{1,5},{5... | collective-permute-start | bytes 196616 | tf_op jit(solution)/shard_map/ppermute | solution.py:247
  9.4 4.0 %collective-permute-start.1 = (bf16[32,512]{1,0:T(8,128)(2,1)S(1)}, bf16[32,512]{1,0:T(8,128)(2,1)S(1)}, u32[]{:S(2)}, u32[]{:S(2)}) collective-permute-start(bf16[32,512]{1,0:T(8,128)(2,1)S(1)} %shard_map.104), channel_id=1, source_target_pairs={{0,8},{4,20},{8,0},{12,28},{16,24},{20,4},{24,16},{28,12},{1,9},{5... | collective-permute-start | bytes 98312 | tf_op jit(solution)/shard_map/ppermute | solution.py:253
  10.9 4.8 %collective-permute-start.3 = (bf16[32,512]{1,0:T(8,128)(2,1)S(1)}, bf16[32,512]{1,0:T(8,128)(2,1)S(1)}, u32[]{:S(2)}, u32[]{:S(2)}) collective-permute-start(bf16[32,512]{1,0:T(8,128)(2,1)S(1)} %shard_map.104), channel_id=1, source_target_pairs={{0,24},{4,28},{8,16},{12,20},{16,8},{20,12},{24,0},{28,4},{1,25},{... | collective-permute-start | bytes 98312 | tf_op jit(solution)/shard_map/ppermute | solution.py:254
  13.3 2.4 %collective-permute-start.2 = (bf16[32,512]{1,0:T(8,128)(2,1)S(1)}, bf16[32,512]{1,0:T(8,128)(2,1)S(1)}, u32[]{:S(2)}, u32[]{:S(2)}) collective-permute-start(bf16[32,512]{1,0:T(8,128)(2,1)S(1)} %collective-permute-done.1.refs_0_), channel_id=1, source_target_pairs={{0,4},{4,0},{8,12},{12,8},{16,20},{20,16},{24,28},{28,24},{1,5},{5... | collective-permute-start | bytes 98312 | tf_op jit(solution)/shard_map/ppermute | solution.py:247
  17.8 7.0 %copy-start.1 = (bf16[32,8192]{1,0:T(8,128)(2,1)S(1)}, bf16[32,8192]{1,0:T(8,128)(2,1)}, u32[]{:S(2)}) copy-start(bf16[32,8192]{1,0:T(8,128)(2,1)} %own_ref.1) | copy-start | bytes 1572868
  18.5 9.3 %collective-permute-start.5 = (bf16[32,4096]{1,0:T(8,128)(2,1)S(1)}, bf16[32,4096]{1,0:T(8,128)(2,1)S(1)}, u32[]{:S(2)}, u32[]{:S(2)}) collective-permute-start(bf16[32,4096]{1,0:T(8,128)(2,1)S(1)} %shard_map.107), channel_id=1, source_target_pairs={{0,1},{1,0},{2,3},{3,2},{4,5},{5,4},{6,7},{7,6},{8,9},{9,8},{10,11... | collective-permute-start | bytes 786440 | tf_op jit(solution)/shard_map/ppermute | solution.py:266
  20.5 8.1 %collective-permute-start.8 = (bf16[32,4096]{1,0:T(8,128)(2,1)S(1)}, bf16[32,4096]{1,0:T(8,128)(2,1)S(1)}, u32[]{:S(2)}, u32[]{:S(2)}) collective-permute-start(bf16[32,4096]{1,0:T(8,128)(2,1)S(1)} %get-tuple-element.56), channel_id=1, source_target_pairs={{1,2},{2,1},{0,0},{3,3},{5,6},{6,5},{4,4},{7,7},{9,10},{10,9},{8,8... | collective-permute-start | bytes 786440 | tf_op jit(solution)/shard_map/ppermute | solution.py:270
  21.2 13.1 %collective-permute-start.10 = (bf16[32,4096]{1,0:T(8,128)(2,1)S(1)}, bf16[32,4096]{1,0:T(8,128)(2,1)S(1)}, u32[]{:S(2)}, u32[]{:S(2)}) collective-permute-start(bf16[32,4096]{1,0:T(8,128)(2,1)S(1)} %shard_map.109), channel_id=1, source_target_pairs={{0,1},{1,0},{2,3},{3,2},{4,5},{5,4},{6,7},{7,6},{8,9},{9,8},{10,11... | collective-permute-start | bytes 786440 | tf_op jit(solution)/shard_map/ppermute | solution.py:266
  24.1 10.3 %collective-permute-start.12 = (bf16[32,4096]{1,0:T(8,128)(2,1)S(1)}, bf16[32,4096]{1,0:T(8,128)(2,1)S(1)}, u32[]{:S(2)}, u32[]{:S(2)}) collective-permute-start(bf16[32,4096]{1,0:T(8,128)(2,1)S(1)} %get-tuple-element.55), channel_id=1, source_target_pairs={{1,2},{2,1},{0,0},{3,3},{5,6},{6,5},{4,4},{7,7},{9,10},{10,9},{8,8... | collective-permute-start | bytes 786440 | tf_op jit(solution)/shard_map/ppermute | solution.py:270
  27.9 13.7 %collective-permute-start.7 = (bf16[32,4096]{1,0:T(8,128)(2,1)S(1)}, bf16[32,4096]{1,0:T(8,128)(2,1)S(1)}, u32[]{:S(2)}, u32[]{:S(2)}) collective-permute-start(bf16[32,4096]{1,0:T(8,128)(2,1)S(1)} %shard_map.111), channel_id=1, source_target_pairs={{1,2},{2,1},{0,0},{3,3},{5,6},{6,5},{4,4},{7,7},{9,10},{10,9},{8,8... | collective-permute-start | bytes 786440 | tf_op jit(solution)/shard_map/ppermute | solution.py:270
  28.6 11.6 %collective-permute-start.9 = (bf16[32,4096]{1,0:T(8,128)(2,1)S(1)}, bf16[32,4096]{1,0:T(8,128)(2,1)S(1)}, u32[]{:S(2)}, u32[]{:S(2)}) collective-permute-start(bf16[32,4096]{1,0:T(8,128)(2,1)S(1)} %shard_map.112), channel_id=1, source_target_pairs={{0,1},{1,0},{2,3},{3,2},{4,5},{5,4},{6,7},{7,6},{8,9},{9,8},{10,11... | collective-permute-start | bytes 786440 | tf_op jit(solution)/shard_map/ppermute | solution.py:266
  34.4 8.6 %collective-permute-start.13 = (bf16[32,4096]{1,0:T(8,128)(2,1)S(1)}, bf16[32,4096]{1,0:T(8,128)(2,1)S(1)}, u32[]{:S(2)}, u32[]{:S(2)}) collective-permute-start(bf16[32,4096]{1,0:T(8,128)(2,1)S(1)} %shard_map.118), channel_id=1, source_target_pairs={{0,1},{1,0},{2,3},{3,2},{4,5},{5,4},{6,7},{7,6},{8,9},{9,8},{10,11... | collective-permute-start | bytes 786440 | tf_op jit(solution)/shard_map/ppermute | solution.py:266
  37.8 6.7 %collective-permute-start.11 = (bf16[32,4096]{1,0:T(8,128)(2,1)S(1)}, bf16[32,4096]{1,0:T(8,128)(2,1)S(1)}, u32[]{:S(2)}, u32[]{:S(2)}) collective-permute-start(bf16[32,4096]{1,0:T(8,128)(2,1)S(1)} %shard_map.116), channel_id=1, source_target_pairs={{1,2},{2,1},{0,0},{3,3},{5,6},{6,5},{4,4},{7,7},{9,10},{10,9},{8,8... | collective-permute-start | bytes 786440 | tf_op jit(solution)/shard_map/ppermute | solution.py:270
  44.7 13.7 %collective-permute-start.14 = (bf16[32,8192]{1,0:T(8,128)(2,1)S(1)}, bf16[32,8192]{1,0:T(8,128)(2,1)S(1)}, u32[]{:S(2)}, u32[]{:S(2)}) collective-permute-start(bf16[32,8192]{1,0:T(8,128)(2,1)S(1)} %shard_map.117), channel_id=1, source_target_pairs={{0,1},{1,0},{2,3},{3,2},{4,5},{5,4},{6,7},{7,6},{8,9},{9,8},{10,11... | collective-permute-start | bytes 1572872 | tf_op jit(solution)/shard_map/ppermute | solution.py:266
  46.8 11.6 %collective-permute-start.15 = (bf16[32,8192]{1,0:T(8,128)(2,1)S(1)}, bf16[32,8192]{1,0:T(8,128)(2,1)S(1)}, u32[]{:S(2)}, u32[]{:S(2)}) collective-permute-start(bf16[32,8192]{1,0:T(8,128)(2,1)S(1)} %shard_map.119), channel_id=1, source_target_pairs={{1,2},{2,1},{0,0},{3,3},{5,6},{6,5},{4,4},{7,7},{9,10},{10,9},{8,8... | collective-permute-start | bytes 1572872 | tf_op jit(solution)/shard_map/ppermute | solution.py:270
  48.6 1.4 %collective-permute-start.16 = (f32[56,512]{1,0:T(8,128)S(1)}, f32[56,512]{1,0:T(8,128)S(1)}, u32[]{:S(2)}, u32[]{:S(2)}) collective-permute-start(f32[56,512]{1,0:T(8,128)S(1)} %get-tuple-element.50.own_ref), channel_id=1, source_target_pairs={{0,4},{4,0},{8,12},{12,8},{16,20},{20,16},{24,28},{28,24},{1,5},{5... | collective-permute-start | bytes 344072 | tf_op jit(solution)/shard_map/ppermute | solution.py:247
  50.1 4.8 %collective-permute-start.17 = (bf16[64,512]{1,0:T(8,128)(2,1)S(1)}, bf16[64,512]{1,0:T(8,128)(2,1)S(1)}, u32[]{:S(2)}, u32[]{:S(2)}) collective-permute-start(bf16[64,512]{1,0:T(8,128)(2,1)S(1)} %shard_map.124.pair_ref), channel_id=1, source_target_pairs={{0,8},{4,20},{8,0},{12,28},{16,24},{20,4},{24,16},{28,12},{1,9},{5... | collective-permute-start | bytes 196616 | tf_op jit(solution)/shard_map/ppermute | solution.py:253
  51.7 5.2 %collective-permute-start.19 = (bf16[64,512]{1,0:T(8,128)(2,1)S(1)}, bf16[64,512]{1,0:T(8,128)(2,1)S(1)}, u32[]{:S(2)}, u32[]{:S(2)}) collective-permute-start(bf16[64,512]{1,0:T(8,128)(2,1)S(1)} %shard_map.124.pair_ref), channel_id=1, source_target_pairs={{0,24},{4,28},{8,16},{12,20},{16,8},{20,12},{24,0},{28,4},{1,25},{... | collective-permute-start | bytes 196616 | tf_op jit(solution)/shard_map/ppermute | solution.py:254
  54.8 2.0 %collective-permute-start.18 = (bf16[64,512]{1,0:T(8,128)(2,1)S(1)}, bf16[64,512]{1,0:T(8,128)(2,1)S(1)}, u32[]{:S(2)}, u32[]{:S(2)}) collective-permute-start(bf16[64,512]{1,0:T(8,128)(2,1)S(1)} %collective-permute-done.17.refs_0_), channel_id=1, source_target_pairs={{0,4},{4,0},{8,12},{12,8},{16,20},{20,16},{24,28},{28,24},{1,5},{5... | collective-permute-start | bytes 196616 | tf_op jit(solution)/shard_map/ppermute | solution.py:247

commit v3 on v2

--- a/solution.py
+++ b/solution.py
@@ -191,8 +191,12 @@
     pair_ref[pl.ds(3 * modes, modes), :] = jnp.broadcast_to(direct, own.shape).astype(BF16)
 
 
-def local_body(modes, g_f, table_ref, y_f):
+def local_body(modes, g_f, table_ref, y_f, powers_ref):
     tok = g_f.shape[0]
+    ahead = 8 - lax.broadcasted_iota(jnp.int32, (8, g_f.shape[1]), 0)
+    for mode in range(modes):
+        rate = jnp.broadcast_to(table_ref[pl.ds(mode, 1), :], ahead.shape)
+        powers_ref[pl.ds(8 * mode, 8), :] = jnp.exp(-(rate * ahead.astype(F32)))
     c = part_of(table_ref, 2, modes)
     a = jnp.exp(-part_of(table_ref, 0, modes))
 
@@ -207,31 +211,36 @@
     y_f[...] = y_f[...] + table_ref[pl.ds(3 * modes, 1), :] * g_f[...]
 
 
-def input_body(seq, modes, own_f, table_ref, other_ref, pair_ref, *refs):
-    *far_refs, grad_ref, by_res_ref, by_log_ref, by_skip_ref, y_f = refs
+def input_body(seq, modes, own_f, powers_ref, table_ref, other_ref, pair_ref, *refs):
+    *far_refs, grad_ref, by_res_ref, by_log_ref, by_skip_ref, y_f, w_ref = refs
     tok = own_f.shape[0]
     rate = part_of(table_ref, 0, modes)
     norm = part_of(table_ref, 1, modes)
     c = part_of(table_ref, 2, modes)
-    a = jnp.exp(-rate)
     a_chunk = jnp.exp(-(rate * tok))
+    a_block = jnp.exp(-(rate * 8.0))
     index = lax.axis_index("ctx")
     pair = index // 2
     second = index % 2 == 1
-    z = jnp.zeros_like(a)
+    z = jnp.zeros_like(rate)
     for j, far_z in enumerate(chosen_from(far_refs, second, pl.ds(0, modes)), 1):
         apart = (pair ^ j) - pair
         until = (jnp.maximum(apart - 1, 0) * (2 * tok)).astype(F32)
         z = z + jnp.where(apart > 0, jnp.exp(-(rate * until)) * far_z, 0.0)
     z = jnp.where(index % 2 == 0, a_chunk * z + part_of(other_ref, 0, modes), z)
 
-    def steps(block, w):
-        for inner in range(STEP):
-            w = a * w
-            y_f[pl.ds(tok - 1 - (block * STEP + inner), 1), :] = jnp.sum(w, axis=0, keepdims=True)
-        return w
-
-    lax.fori_loop(0, tok // STEP, steps, c * z)
+    w_ref[...] = c * z
+
+    def steps(block, carry):
+        total = None
+        for mode in range(modes):
+            part = row_of(w_ref, mode, powers_ref[pl.ds(0, 8), :]) * powers_ref[pl.ds(8 * mode, 8), :]
+            total = part if total is None else total + part
+        y_f[pl.ds(pl.multiple_of(tok - 8 * (block + 1), 8), 8), :] = total
+        w_ref[...] = a_block * w_ref[...]
+        return carry
+
+    lax.fori_loop(0, tok // 8, steps, 0)
     grad_ref[...] = (own_f[...] + y_f[...]).astype(BF16)
     rest = pl.ds(modes, 3 * modes)
     total = pair_ref[rest, :].astype(F32)
@@ -505,7 +514,10 @@
 
     reduce = line_of_four if parts == 4 else any_axis
     out, g_f, sums = reduce(out_grad, out_weight, merged, x_f, states_of, grads_of)
-    (own_grad,) = call(functools.partial(local_body, modes), [lanes((tok, chans))], [], [g_f, table], flops=LOCAL_FLOPS)
+    own_grad, powers = call(
+        functools.partial(local_body, modes), [lanes((tok, chans)), lanes((8 * modes, chans))], [], [g_f, table],
+        flops=LOCAL_FLOPS,
+    )
     other_sums = from_other_core(sums, blocks)
     (pair_sums,) = call(
         functools.partial(pair_sums_body, tok, modes), [jax.ShapeDtypeStruct((4 * modes, chans), BF16)], [],
@@ -513,8 +525,8 @@
     )
     grad_input, by_res, by_log, by_skip = call(
         functools.partial(input_body, seq, modes),
-        [jax.ShapeDtypeStruct((tok, chans), BF16), state, state, lanes((1, chans))], [token_f],
-        [own_grad, table, other_sums, pair_sums, *from_pairs(pair_sums, blocks)],
+        [jax.ShapeDtypeStruct((tok, chans), BF16), state, state, lanes((1, chans))], [token_f, pltpu.VMEM((modes, chans), F32)],
+        [own_grad, powers, table, other_sums, pair_sums, *from_pairs(pair_sums, blocks)],
     )
     return out, grad_input, by_res.T, by_log.T, by_skip[0]
 

time: 59.6 us -> 59.4 us (level)
  no operation moved by 1% of the time
where the time goes in v3:
time: 59.4 us; the launch traced here: 59.1 us
  starting transfers between devices  31.3 us (53%)
  Pallas kernels  15 us (25%)
  waiting for transfers between devices  11.8 us (20%)
  between operations  0.96 us (2%)
    ppermute x6, starting transfers between devices, outer(): return lax.ppermute(array, 'tp', [(0, 1), (1, 0), (2, 3), (3, 2)])  19.9 us
    pallas_call x25, Pallas kernels, call(): pl.pallas_call(body, out_shape=outs, in_specs=[whole] * len(args), out_sp...  15 us
    ppermute x6, starting transfers between devices, inner(): return lax.ppermute(array, 'tp', [(1, 2), (2, 1), (0, 0), (3, 3)])  5.2 us
    ppermute x6, waiting for transfers between devices, outer(): return lax.ppermute(array, 'tp', [(0, 1), (1, 0), (2, 3), (3, 2)])  3.41 us
    ppermute x2, starting transfers between devices, from_pairs(): lax.ppermute(array, 'ctx', [(i, i ^ (4 if i % 2 else 2)) for i in range(b...  3.17 us
    ppermute x2, waiting for transfers between devices, from_pairs(): corner = lax.ppermute(array, 'ctx', [(i, i ^ 6) for i in range(blocks)])  3.14 us
    ppermute x2, starting transfers between devices, from_pairs(): corner = lax.ppermute(array, 'ctx', [(i, i ^ 6) for i in range(blocks)])  2.93 us
    ppermute x2, waiting for transfers between devices, from_pairs(): lax.ppermute(array, 'ctx', [(i, i ^ (4 if i % 2 else 2)) for i in range(b...  2.64 us
  transfers between devices with their start and end apart: 20, of which 9 were waited for; matrix products, arithmetic and copies ran while one was open for 0% of the time, Pallas kernels for 24%

profile of v3, /device:TPU:0, one launch (start us, length us, event | category | flops | bytes accessed | tf_op | source)
XLA Modules:
  0.0 59.1 jit_solution(15831908272528173837)
XLA Ops:
  0.7 1.8 %collective-permute-start.4 = (bf16[32,8192]{1,0:T(8,128)(2,1)}, bf16[32,8192]{1,0:T(8,128)(2,1)S(1)}, u32[]{:S(2)}, u32[]{:S(2)}) collective-permute-start(bf16[32,8192]{1,0:T(8,128)(2,1)} %own_ref.1), channel_id=1, source_target_pairs={{1,2},{2,1},{0,0},{3,3},{5,6},{6,5},{4,4},{7,7},{9,10},{10,9},{8,8... | collective-permute-start | bytes 1572872 | tf_op jit(solution)/shard_map/ppermute | solution.py:279
  2.5 4.9 %collective-permute-start.6 = (bf16[32,8192]{1,0:T(8,128)(2,1)}, bf16[32,8192]{1,0:T(8,128)(2,1)S(1)}, u32[]{:S(2)}, u32[]{:S(2)}) collective-permute-start(bf16[32,8192]{1,0:T(8,128)(2,1)} %own_ref.1), channel_id=1, source_target_pairs={{0,1},{1,0},{2,3},{3,2},{4,5},{5,4},{6,7},{7,6},{8,9},{9,8},{10,11... | collective-permute-start | bytes 1572872 | tf_op jit(solution)/shard_map/ppermute | solution.py:275
  8.1 1.2 %collective-permute-done.other_ref = f32[32,512]{1,0:T(8,128)S(1)} collective-permute-done((f32[32,512]{1,0:T(8,128)S(1)}, f32[32,512]{1,0:T(8,128)S(1)}, u32[]{:S(2)}, u32[]{:S(2)}) %collective-permute-start) | collective-permute-done | bytes 65568 | tf_op jit(solution)/shard_map/ppermute | solution.py:256
  9.4 1.6 %collective-permute-start.1 = (bf16[32,512]{1,0:T(8,128)(2,1)S(1)}, bf16[32,512]{1,0:T(8,128)(2,1)S(1)}, u32[]{:S(2)}, u32[]{:S(2)}) collective-permute-start(bf16[32,512]{1,0:T(8,128)(2,1)S(1)} %shard_map.104), channel_id=1, source_target_pairs={{0,8},{4,20},{8,0},{12,28},{16,24},{20,4},{24,16},{28,12},{1,9},{5... | collective-permute-start | bytes 98312 | tf_op jit(solution)/shard_map/ppermute | solution.py:262
  10.9 1.5 %collective-permute-start.3 = (bf16[32,512]{1,0:T(8,128)(2,1)S(1)}, bf16[32,512]{1,0:T(8,128)(2,1)S(1)}, u32[]{:S(2)}, u32[]{:S(2)}) collective-permute-start(bf16[32,512]{1,0:T(8,128)(2,1)S(1)} %shard_map.104), channel_id=1, source_target_pairs={{0,24},{4,28},{8,16},{12,20},{16,8},{20,12},{24,0},{28,4},{1,25},{... | collective-permute-start | bytes 98312 | tf_op jit(solution)/shard_map/ppermute | solution.py:263
  12.4 0.9 %collective-permute-done.1.refs_0_ = bf16[32,512]{1,0:T(8,128)(2,1)S(1)} collective-permute-done((bf16[32,512]{1,0:T(8,128)(2,1)S(1)}, bf16[32,512]{1,0:T(8,128)(2,1)S(1)}, u32[]{:S(2)}, u32[]{:S(2)}) %collective-permute-start.1) | collective-permute-done | bytes 32800 | tf_op jit(solution)/shard_map/ppermute | solution.py:262
  13.4 2.4 %collective-permute-done.3.refs_2_ = bf16[32,512]{1,0:T(8,128)(2,1)S(1)} collective-permute-done((bf16[32,512]{1,0:T(8,128)(2,1)S(1)}, bf16[32,512]{1,0:T(8,128)(2,1)S(1)}, u32[]{:S(2)}, u32[]{:S(2)}) %collective-permute-start.3) | collective-permute-done | bytes 32800 | tf_op jit(solution)/shard_map/ppermute | solution.py:263
  15.7 1.2 %shard_map.105 = (bf16[128,512]{1,0:T(8,128)(2,1)S(1)}, f32[32,512]{1,0:T(8,128)S(1)}) custom-call(f32[128,512]{1,0:T(8,128)S(1)} %get-tuple-element.41.x_f, f32[56,512]{1,0:T(8,128)S(1)} %shard_map.103.table_ref, f32[32,512]{1,0:T(8,128)S(1)} %collective-permute-done.other_ref, bf16[32,512]{1,0:T(8,128)(2,1)S(1)} %collective-permute-done.1.refs_0_, ...), custom_call_target="tpu_custom_call" | custom-call | flops 1024 | bytes 1024 | tf_op jit(solution)/shard_map/pallas_call | solution.py:21
  17.0 0.7 %shard_map.106.share_ref.refs_0_ = bf16[128,4096]{1,0:T(8,128)(2,1)S(1)} custom-call(bf16[128,512]{1,0:T(8,128)(2,1)S(1)} %get-tuple-element.36.merged_ref, bf16[512,8192]{1,0:T(8,128)(2,1)S(1)} %copy-done), custom_call_target="tpu_custom_call" | custom-call | flops 1024 | bytes 1024 | tf_op jit(solution)/shard_map/pallas_call | solution.py:21
  17.8 0.7 %shard_map.108.share_ref.refs_1_.refs_2_ = bf16[128,4096]{1,0:T(8,128)(2,1)S(1)} custom-call(bf16[128,512]{1,0:T(8,128)(2,1)S(1)} %get-tuple-element.36.merged_ref, bf16[512,8192]{1,0:T(8,128)(2,1)S(1)} %copy-done), custom_call_target="tpu_custom_call" | custom-call | flops 1024 | bytes 1024 | tf_op jit(solution)/shard_map/pallas_call | solution.py:21
  18.5 1.9 %collective-permute-start.5 = (bf16[32,4096]{1,0:T(8,128)(2,1)S(1)}, bf16[32,4096]{1,0:T(8,128)(2,1)S(1)}, u32[]{:S(2)}, u32[]{:S(2)}) collective-permute-start(bf16[32,4096]{1,0:T(8,128)(2,1)S(1)} %shard_map.107), channel_id=1, source_target_pairs={{0,1},{1,0},{2,3},{3,2},{4,5},{5,4},{6,7},{7,6},{8,9},{9,8},{10,11... | collective-permute-start | bytes 786440 | tf_op jit(solution)/shard_map/ppermute | solution.py:275
  20.5 0.7 %collective-permute-start.8 = (bf16[32,4096]{1,0:T(8,128)(2,1)S(1)}, bf16[32,4096]{1,0:T(8,128)(2,1)S(1)}, u32[]{:S(2)}, u32[]{:S(2)}) collective-permute-start(bf16[32,4096]{1,0:T(8,128)(2,1)S(1)} %get-tuple-element.60), channel_id=1, source_target_pairs={{1,2},{2,1},{0,0},{3,3},{5,6},{6,5},{4,4},{7,7},{9,10},{10,9},{8,8... | collective-permute-start | bytes 786440 | tf_op jit(solution)/shard_map/ppermute | solution.py:279
  21.2 2.9 %collective-permute-start.10 = (bf16[32,4096]{1,0:T(8,128)(2,1)S(1)}, bf16[32,4096]{1,0:T(8,128)(2,1)S(1)}, u32[]{:S(2)}, u32[]{:S(2)}) collective-permute-start(bf16[32,4096]{1,0:T(8,128)(2,1)S(1)} %shard_map.109), channel_id=1, source_target_pairs={{0,1},{1,0},{2,3},{3,2},{4,5},{5,4},{6,7},{7,6},{8,9},{9,8},{10,11... | collective-permute-start | bytes 786440 | tf_op jit(solution)/shard_map/ppermute | solution.py:275
  24.8 2.6 %shard_map.110.refs_0_ = f32[64,512]{1,0:T(8,128)S(1)} custom-call(bf16[32,8192]{1,0:T(8,128)(2,1)S(1)} %copy-done.1, bf16[32,8192]{1,0:T(8,128)(2,1)S(1)} %collective-permute-done.6.beside_ref, bf16[512,8192]{1,0:T(8,128)(2,1)S(1)} %copy-done), custom_call_target="tpu_custom_call" | custom-call | flops 1024 | bytes 1024 | tf_op jit(solution)/shard_map/pallas_call | solution.py:21
  28.6 4.7 %collective-permute-start.9 = (bf16[32,4096]{1,0:T(8,128)(2,1)S(1)}, bf16[32,4096]{1,0:T(8,128)(2,1)S(1)}, u32[]{:S(2)}, u32[]{:S(2)}) collective-permute-start(bf16[32,4096]{1,0:T(8,128)(2,1)S(1)} %shard_map.112), channel_id=1, source_target_pairs={{0,1},{1,0},{2,3},{3,2},{4,5},{5,4},{6,7},{7,6},{8,9},{9,8},{10,11... | collective-permute-start | bytes 786440 | tf_op jit(solution)/shard_map/ppermute | solution.py:275
  33.3 0.9 %shard_map.115 = (f32[2048,512]{1,0:T(8,128)S(1)}, f32[2048,512]{1,0:T(8,128)S(1)}) custom-call(f32[128,512]{1,0:T(8,128)S(1)} %get-tuple-element.41.x_f, f32[56,512]{1,0:T(8,128)S(1)} %shard_map.103.table_ref, f32[32,512]{1,0:T(8,128)S(1)} %get-tuple-element.42.start_ref), custom_call_target="tpu_custom_call" | custom-call | flops 1024 | bytes 1024 | tf_op jit(solution)/shard_map/pallas_call | solution.py:21
  34.4 3.4 %collective-permute-start.13 = (bf16[32,4096]{1,0:T(8,128)(2,1)S(1)}, bf16[32,4096]{1,0:T(8,128)(2,1)S(1)}, u32[]{:S(2)}, u32[]{:S(2)}) collective-permute-start(bf16[32,4096]{1,0:T(8,128)(2,1)S(1)} %shard_map.118), channel_id=1, source_target_pairs={{0,1},{1,0},{2,3},{3,2},{4,5},{5,4},{6,7},{7,6},{8,9},{9,8},{10,11... | collective-permute-start | bytes 786440 | tf_op jit(solution)/shard_map/ppermute | solution.py:275
  38.5 1.7 %collective-permute-done.9.third_ref.refs_1_ = bf16[32,4096]{1,0:T(8,128)(2,1)S(1)} collective-permute-done((bf16[32,4096]{1,0:T(8,128)(2,1)S(1)}, bf16[32,4096]{1,0:T(8,128)(2,1)S(1)}, u32[]{:S(2)}, u32[]{:S(2)}) %collective-permute-start.9) | collective-permute-done | bytes 262176 | tf_op jit(solution)/shard_map/ppermute | solution.py:275
  40.2 1.4 %shard_map.113.refs_0_ = f32[64,512]{1,0:T(8,128)S(1)} custom-call(bf16[32,4096]{1,0:T(8,128)(2,1)S(1)} %collective-permute-done.5.got_ref.second_ref, bf16[32,4096]{1,0:T(8,128)(2,1)S(1)} %collective-permute-done.9.third_ref.refs_1_, bf16[32,8192]{1,0:T(8,128)(2,1)S(1)} %collective-permute-done.4.passing_ref.across_ref, ...), custom_call_target="tpu_custom_call" | custom-call | flops 1024 | bytes 1024 | tf_op jit(solution)/shard_map/pallas_call | solution.py:21
  41.7 1.3 %collective-permute-done.13.refs_3_.third_ref = bf16[32,4096]{1,0:T(8,128)(2,1)S(1)} collective-permute-done((bf16[32,4096]{1,0:T(8,128)(2,1)S(1)}, bf16[32,4096]{1,0:T(8,128)(2,1)S(1)}, u32[]{:S(2)}, u32[]{:S(2)}) %collective-permute-start.13) | collective-permute-done | bytes 262176 | tf_op jit(solution)/shard_map/ppermute | solution.py:275
  43.0 1.4 %shard_map.120.refs_1_ = f32[64,512]{1,0:T(8,128)S(1)} custom-call(bf16[32,4096]{1,0:T(8,128)(2,1)S(1)} %collective-permute-done.10.got_ref.second_ref, bf16[32,4096]{1,0:T(8,128)(2,1)S(1)} %collective-permute-done.13.refs_3_.third_ref, bf16[32,8192]{1,0:T(8,128)(2,1)S(1)} %collective-permute-done.4.passing_ref.across_ref, ...), custom_call_target="tpu_custom_call" | custom-call | flops 1024 | bytes 1024 | tf_op jit(solution)/shard_map/pallas_call | solution.py:21
  44.7 2.1 %collective-permute-start.14 = (bf16[32,8192]{1,0:T(8,128)(2,1)S(1)}, bf16[32,8192]{1,0:T(8,128)(2,1)S(1)}, u32[]{:S(2)}, u32[]{:S(2)}) collective-permute-start(bf16[32,8192]{1,0:T(8,128)(2,1)S(1)} %shard_map.117), channel_id=1, source_target_pairs={{0,1},{1,0},{2,3},{3,2},{4,5},{5,4},{6,7},{7,6},{8,9},{9,8},{10,11... | collective-permute-start | bytes 1572872 | tf_op jit(solution)/shard_map/ppermute | solution.py:275
  46.8 0.7 %collective-permute-start.15 = (bf16[32,8192]{1,0:T(8,128)(2,1)S(1)}, bf16[32,8192]{1,0:T(8,128)(2,1)S(1)}, u32[]{:S(2)}, u32[]{:S(2)}) collective-permute-start(bf16[32,8192]{1,0:T(8,128)(2,1)S(1)} %shard_map.119), channel_id=1, source_target_pairs={{1,2},{2,1},{0,0},{3,3},{5,6},{6,5},{4,4},{7,7},{9,10},{10,9},{8,8... | collective-permute-start | bytes 1572872 | tf_op jit(solution)/shard_map/ppermute | solution.py:279
  47.5 1.2 %shard_map.122 = (f32[128,512]{1,0:T(8,128)S(1)}, f32[56,512]{1,0:T(8,128)S(1)}) custom-call(f32[128,512]{1,0:T(8,128)S(1)} %get-tuple-element.41.x_f, f32[56,512]{1,0:T(8,128)S(1)} %shard_map.103.table_ref, f32[2048,512]{1,0:T(8,128)S(1)} %get-tuple-element.43.h_ref, f32[2048,512]{1,0:T(8,128)S(1)} %get-tuple-element.44.q_ref, ...), custom_call_target="tpu_custom_call" | custom-call | flops 1024 | bytes 1024 | tf_op jit(solution)/shard_map/pallas_call | solution.py:21
  48.7 1.3 %collective-permute-done.16.other_ref = f32[56,512]{1,0:T(8,128)S(1)} collective-permute-done((f32[56,512]{1,0:T(8,128)S(1)}, f32[56,512]{1,0:T(8,128)S(1)}, u32[]{:S(2)}, u32[]{:S(2)}) %collective-permute-start.16) | collective-permute-done | bytes 114720 | tf_op jit(solution)/shard_map/ppermute | solution.py:256
  50.1 1.6 %collective-permute-start.17 = (bf16[64,512]{1,0:T(8,128)(2,1)S(1)}, bf16[64,512]{1,0:T(8,128)(2,1)S(1)}, u32[]{:S(2)}, u32[]{:S(2)}) collective-permute-start(bf16[64,512]{1,0:T(8,128)(2,1)S(1)} %shard_map.124.pair_ref), channel_id=1, source_target_pairs={{0,8},{4,20},{8,0},{12,28},{16,24},{20,4},{24,16},{28,12},{1,9},{5... | collective-permute-start | bytes 196616 | tf_op jit(solution)/shard_map/ppermute | solution.py:262
  51.7 1.4 %collective-permute-start.19 = (bf16[64,512]{1,0:T(8,128)(2,1)S(1)}, bf16[64,512]{1,0:T(8,128)(2,1)S(1)}, u32[]{:S(2)}, u32[]{:S(2)}) collective-permute-start(bf16[64,512]{1,0:T(8,128)(2,1)S(1)} %shard_map.124.pair_ref), channel_id=1, source_target_pairs={{0,24},{4,28},{8,16},{12,20},{16,8},{20,12},{24,0},{28,4},{1,25},{... | collective-permute-start | bytes 196616 | tf_op jit(solution)/shard_map/ppermute | solution.py:263
  53.1 1.7 %collective-permute-done.17.refs_0_ = bf16[64,512]{1,0:T(8,128)(2,1)S(1)} collective-permute-done((bf16[64,512]{1,0:T(8,128)(2,1)S(1)}, bf16[64,512]{1,0:T(8,128)(2,1)S(1)}, u32[]{:S(2)}, u32[]{:S(2)}) %collective-permute-start.17) | collective-permute-done | bytes 65568 | tf_op jit(solution)/shard_map/ppermute | solution.py:262
  54.8 1.2 %shard_map.123 = (f32[128,512]{1,0:T(8,128)S(1)}, f32[128,512]{1,0:T(8,128)S(1)}) custom-call(f32[128,512]{1,0:T(8,128)S(1)} %get-tuple-element.51.g_f, f32[56,512]{1,0:T(8,128)S(1)} %shard_map.103.table_ref), custom_call_target="tpu_custom_call" | custom-call | flops 1000000000 | bytes 1024 | tf_op jit(solution)/shard_map/pallas_call | solution.py:21
  56.0 0.8 %collective-permute-done.19.refs_2_ = bf16[64,512]{1,0:T(8,128)(2,1)S(1)} collective-permute-done((bf16[64,512]{1,0:T(8,128)(2,1)S(1)}, bf16[64,512]{1,0:T(8,128)(2,1)S(1)}, u32[]{:S(2)}, u32[]{:S(2)}) %collective-permute-start.19) | collective-permute-done | bytes 65568 | tf_op jit(solution)/shard_map/ppermute | solution.py:263
  56.8 1.3 %shard_map.125 = (bf16[128,512]{1,0:T(8,128)(2,1)}, f32[16,512]{1,0:T(8,128)}, f32[16,512]{1,0:T(8,128)}, f32[1,512]{1,0:T(1,128)}) custom-call(f32[128,512]{1,0:T(8,128)S(1)} %get-tuple-element.52.own_f, f32[128,512]{1,0:T(8,128)S(1)} %get-tuple-element.53.powers_ref, f32[56,512]{1,0:T(8,128)S(1)} %shard_map.103.table_ref, ...), custom_call_target="tpu_custom_call" | custom-call | flops 1024 | bytes 1024 | tf_op jit(solution)/shard_map/pallas_call | solution.py:21
  58.2 1.0 %shard_map.121 = bf16[32,8192]{1,0:T(8,128)(2,1)} custom-call(bf16[128,4096]{1,0:T(8,128)(2,1)S(1)} %shard_map.106.share_ref.refs_0_, bf16[128,4096]{1,0:T(8,128)(2,1)S(1)} %shard_map.108.share_ref.refs_1_.refs_2_, bf16[32,8192]{1,0:T(8,128)(2,1)S(1)} %collective-permute-done.14.refs_2_, bf16[32,8192]{1,0:T(8,128)(2,1)S(1)} %collective-permute-done.15.refs_3_), custom_call_target="tpu_custom_call" | custom-call | flops 1024 | bytes 1024 | tf_op jit(solution)/shard_map/pallas_call | solution.py:21
  (46 shorter events, 3.9 us)
Async XLA Ops:
  0.6 6.7 %copy-start.3 = (f32[512,16]{0,1:T(8,128)S(1)}, f32[512,16]{0,1:T(8,128)}, u32[]{:S(2)}) copy-start(f32[512,16]{0,1:T(8,128)} %param.8) | copy-start | bytes 98308
  0.6 6.7 %copy-start.2 = (bf16[128,512]{1,0:T(8,128)(2,1)S(1)}, bf16[128,512]{1,0:T(8,128)(2,1)}, u32[]{:S(2)}) copy-start(bf16[128,512]{1,0:T(8,128)(2,1)} %x_ref.1) | copy-start | bytes 393220
  0.7 17.1 %collective-permute-start.4 = (bf16[32,8192]{1,0:T(8,128)(2,1)}, bf16[32,8192]{1,0:T(8,128)(2,1)S(1)}, u32[]{:S(2)}, u32[]{:S(2)}) collective-permute-start(bf16[32,8192]{1,0:T(8,128)(2,1)} %own_ref.1), channel_id=1, source_target_pairs={{1,2},{2,1},{0,0},{3,3},{5,6},{6,5},{4,4},{7,7},{9,10},{10,9},{8,8... | collective-permute-start | bytes 1572872 | tf_op jit(solution)/shard_map/ppermute | solution.py:279
  2.5 17.9 %collective-permute-start.6 = (bf16[32,8192]{1,0:T(8,128)(2,1)}, bf16[32,8192]{1,0:T(8,128)(2,1)S(1)}, u32[]{:S(2)}, u32[]{:S(2)}) collective-permute-start(bf16[32,8192]{1,0:T(8,128)(2,1)} %own_ref.1), channel_id=1, source_target_pairs={{0,1},{1,0},{2,3},{3,2},{4,5},{5,4},{6,7},{7,6},{8,9},{9,8},{10,11... | collective-permute-start | bytes 1572872 | tf_op jit(solution)/shard_map/ppermute | solution.py:275
  7.4 6.0 %copy-start.4 = (f32[512,16]{0,1:T(8,128)S(1)}, f32[512,16]{0,1:T(8,128)}, u32[]{:S(2)}) copy-start(f32[512,16]{0,1:T(8,128)} %param.7) | copy-start | bytes 98308
  7.4 6.0 %copy-start.5 = (f32[512]{0:T(512)S(1)}, f32[512]{0:T(512)}, u32[]{:S(2)}) copy-start(f32[512]{0:T(512)} %param.9) | copy-start | bytes 6148
  7.4 9.6 %copy-start = (bf16[512,8192]{1,0:T(8,128)(2,1)S(1)}, bf16[512,8192]{1,0:T(8,128)(2,1)}, u32[]{:S(2)}) copy-start(bf16[512,8192]{1,0:T(8,128)(2,1)} %weight_ref.9) | copy-start | bytes 25165828
  8.0 1.3 %collective-permute-start = (f32[32,512]{1,0:T(8,128)S(1)}, f32[32,512]{1,0:T(8,128)S(1)}, u32[]{:S(2)}, u32[]{:S(2)}) collective-permute-start(f32[32,512]{1,0:T(8,128)S(1)} %get-tuple-element.34.own_ref), channel_id=1, source_target_pairs={{0,4},{4,0},{8,12},{12,8},{16,20},{20,16},{24,28},{28,24},{1,5},{5... | collective-permute-start | bytes 196616 | tf_op jit(solution)/shard_map/ppermute | solution.py:256
  9.4 4.0 %collective-permute-start.1 = (bf16[32,512]{1,0:T(8,128)(2,1)S(1)}, bf16[32,512]{1,0:T(8,128)(2,1)S(1)}, u32[]{:S(2)}, u32[]{:S(2)}) collective-permute-start(bf16[32,512]{1,0:T(8,128)(2,1)S(1)} %shard_map.104), channel_id=1, source_target_pairs={{0,8},{4,20},{8,0},{12,28},{16,24},{20,4},{24,16},{28,12},{1,9},{5... | collective-permute-start | bytes 98312 | tf_op jit(solution)/shard_map/ppermute | solution.py:262
  10.9 4.8 %collective-permute-start.3 = (bf16[32,512]{1,0:T(8,128)(2,1)S(1)}, bf16[32,512]{1,0:T(8,128)(2,1)S(1)}, u32[]{:S(2)}, u32[]{:S(2)}) collective-permute-start(bf16[32,512]{1,0:T(8,128)(2,1)S(1)} %shard_map.104), channel_id=1, source_target_pairs={{0,24},{4,28},{8,16},{12,20},{16,8},{20,12},{24,0},{28,4},{1,25},{... | collective-permute-start | bytes 98312 | tf_op jit(solution)/shard_map/ppermute | solution.py:263
  13.3 2.4 %collective-permute-start.2 = (bf16[32,512]{1,0:T(8,128)(2,1)S(1)}, bf16[32,512]{1,0:T(8,128)(2,1)S(1)}, u32[]{:S(2)}, u32[]{:S(2)}) collective-permute-start(bf16[32,512]{1,0:T(8,128)(2,1)S(1)} %collective-permute-done.1.refs_0_), channel_id=1, source_target_pairs={{0,4},{4,0},{8,12},{12,8},{16,20},{20,16},{24,28},{28,24},{1,5},{5... | collective-permute-start | bytes 98312 | tf_op jit(solution)/shard_map/ppermute | solution.py:256
  17.8 7.0 %copy-start.1 = (bf16[32,8192]{1,0:T(8,128)(2,1)S(1)}, bf16[32,8192]{1,0:T(8,128)(2,1)}, u32[]{:S(2)}) copy-start(bf16[32,8192]{1,0:T(8,128)(2,1)} %own_ref.1) | copy-start | bytes 1572868
  18.5 9.3 %collective-permute-start.5 = (bf16[32,4096]{1,0:T(8,128)(2,1)S(1)}, bf16[32,4096]{1,0:T(8,128)(2,1)S(1)}, u32[]{:S(2)}, u32[]{:S(2)}) collective-permute-start(bf16[32,4096]{1,0:T(8,128)(2,1)S(1)} %shard_map.107), channel_id=1, source_target_pairs={{0,1},{1,0},{2,3},{3,2},{4,5},{5,4},{6,7},{7,6},{8,9},{9,8},{10,11... | collective-permute-start | bytes 786440 | tf_op jit(solution)/shard_map/ppermute | solution.py:275
  20.5 8.1 %collective-permute-start.8 = (bf16[32,4096]{1,0:T(8,128)(2,1)S(1)}, bf16[32,4096]{1,0:T(8,128)(2,1)S(1)}, u32[]{:S(2)}, u32[]{:S(2)}) collective-permute-start(bf16[32,4096]{1,0:T(8,128)(2,1)S(1)} %get-tuple-element.60), channel_id=1, source_target_pairs={{1,2},{2,1},{0,0},{3,3},{5,6},{6,5},{4,4},{7,7},{9,10},{10,9},{8,8... | collective-permute-start | bytes 786440 | tf_op jit(solution)/shard_map/ppermute | solution.py:279
  21.2 13.1 %collective-permute-start.10 = (bf16[32,4096]{1,0:T(8,128)(2,1)S(1)}, bf16[32,4096]{1,0:T(8,128)(2,1)S(1)}, u32[]{:S(2)}, u32[]{:S(2)}) collective-permute-start(bf16[32,4096]{1,0:T(8,128)(2,1)S(1)} %shard_map.109), channel_id=1, source_target_pairs={{0,1},{1,0},{2,3},{3,2},{4,5},{5,4},{6,7},{7,6},{8,9},{9,8},{10,11... | collective-permute-start | bytes 786440 | tf_op jit(solution)/shard_map/ppermute | solution.py:275
  24.1 10.3 %collective-permute-start.12 = (bf16[32,4096]{1,0:T(8,128)(2,1)S(1)}, bf16[32,4096]{1,0:T(8,128)(2,1)S(1)}, u32[]{:S(2)}, u32[]{:S(2)}) collective-permute-start(bf16[32,4096]{1,0:T(8,128)(2,1)S(1)} %get-tuple-element.59), channel_id=1, source_target_pairs={{1,2},{2,1},{0,0},{3,3},{5,6},{6,5},{4,4},{7,7},{9,10},{10,9},{8,8... | collective-permute-start | bytes 786440 | tf_op jit(solution)/shard_map/ppermute | solution.py:279
  27.9 13.7 %collective-permute-start.7 = (bf16[32,4096]{1,0:T(8,128)(2,1)S(1)}, bf16[32,4096]{1,0:T(8,128)(2,1)S(1)}, u32[]{:S(2)}, u32[]{:S(2)}) collective-permute-start(bf16[32,4096]{1,0:T(8,128)(2,1)S(1)} %shard_map.111), channel_id=1, source_target_pairs={{1,2},{2,1},{0,0},{3,3},{5,6},{6,5},{4,4},{7,7},{9,10},{10,9},{8,8... | collective-permute-start | bytes 786440 | tf_op jit(solution)/shard_map/ppermute | solution.py:279
  28.6 11.6 %collective-permute-start.9 = (bf16[32,4096]{1,0:T(8,128)(2,1)S(1)}, bf16[32,4096]{1,0:T(8,128)(2,1)S(1)}, u32[]{:S(2)}, u32[]{:S(2)}) collective-permute-start(bf16[32,4096]{1,0:T(8,128)(2,1)S(1)} %shard_map.112), channel_id=1, source_target_pairs={{0,1},{1,0},{2,3},{3,2},{4,5},{5,4},{6,7},{7,6},{8,9},{9,8},{10,11... | collective-permute-start | bytes 786440 | tf_op jit(solution)/shard_map/ppermute | solution.py:275
  34.4 8.6 %collective-permute-start.13 = (bf16[32,4096]{1,0:T(8,128)(2,1)S(1)}, bf16[32,4096]{1,0:T(8,128)(2,1)S(1)}, u32[]{:S(2)}, u32[]{:S(2)}) collective-permute-start(bf16[32,4096]{1,0:T(8,128)(2,1)S(1)} %shard_map.118), channel_id=1, source_target_pairs={{0,1},{1,0},{2,3},{3,2},{4,5},{5,4},{6,7},{7,6},{8,9},{9,8},{10,11... | collective-permute-start | bytes 786440 | tf_op jit(solution)/shard_map/ppermute | solution.py:275
  37.8 6.7 %collective-permute-start.11 = (bf16[32,4096]{1,0:T(8,128)(2,1)S(1)}, bf16[32,4096]{1,0:T(8,128)(2,1)S(1)}, u32[]{:S(2)}, u32[]{:S(2)}) collective-permute-start(bf16[32,4096]{1,0:T(8,128)(2,1)S(1)} %shard_map.116), channel_id=1, source_target_pairs={{1,2},{2,1},{0,0},{3,3},{5,6},{6,5},{4,4},{7,7},{9,10},{10,9},{8,8... | collective-permute-start | bytes 786440 | tf_op jit(solution)/shard_map/ppermute | solution.py:279
  44.7 13.5 %collective-permute-start.14 = (bf16[32,8192]{1,0:T(8,128)(2,1)S(1)}, bf16[32,8192]{1,0:T(8,128)(2,1)S(1)}, u32[]{:S(2)}, u32[]{:S(2)}) collective-permute-start(bf16[32,8192]{1,0:T(8,128)(2,1)S(1)} %shard_map.117), channel_id=1, source_target_pairs={{0,1},{1,0},{2,3},{3,2},{4,5},{5,4},{6,7},{7,6},{8,9},{9,8},{10,11... | collective-permute-start | bytes 1572872 | tf_op jit(solution)/shard_map/ppermute | solution.py:275
  46.8 11.4 %collective-permute-start.15 = (bf16[32,8192]{1,0:T(8,128)(2,1)S(1)}, bf16[32,8192]{1,0:T(8,128)(2,1)S(1)}, u32[]{:S(2)}, u32[]{:S(2)}) collective-permute-start(bf16[32,8192]{1,0:T(8,128)(2,1)S(1)} %shard_map.119), channel_id=1, source_target_pairs={{1,2},{2,1},{0,0},{3,3},{5,6},{6,5},{4,4},{7,7},{9,10},{10,9},{8,8... | collective-permute-start | bytes 1572872 | tf_op jit(solution)/shard_map/ppermute | solution.py:279
  48.6 1.4 %collective-permute-start.16 = (f32[56,512]{1,0:T(8,128)S(1)}, f32[56,512]{1,0:T(8,128)S(1)}, u32[]{:S(2)}, u32[]{:S(2)}) collective-permute-start(f32[56,512]{1,0:T(8,128)S(1)} %get-tuple-element.54.own_ref), channel_id=1, source_target_pairs={{0,4},{4,0},{8,12},{12,8},{16,20},{20,16},{24,28},{28,24},{1,5},{5... | collective-permute-start | bytes 344072 | tf_op jit(solution)/shard_map/ppermute | solution.py:256
  50.1 4.8 %collective-permute-start.17 = (bf16[64,512]{1,0:T(8,128)(2,1)S(1)}, bf16[64,512]{1,0:T(8,128)(2,1)S(1)}, u32[]{:S(2)}, u32[]{:S(2)}) collective-permute-start(bf16[64,512]{1,0:T(8,128)(2,1)S(1)} %shard_map.124.pair_ref), channel_id=1, source_target_pairs={{0,8},{4,20},{8,0},{12,28},{16,24},{20,4},{24,16},{28,12},{1,9},{5... | collective-permute-start | bytes 196616 | tf_op jit(solution)/shard_map/ppermute | solution.py:262
  51.7 5.2 %collective-permute-start.19 = (bf16[64,512]{1,0:T(8,128)(2,1)S(1)}, bf16[64,512]{1,0:T(8,128)(2,1)S(1)}, u32[]{:S(2)}, u32[]{:S(2)}) collective-permute-start(bf16[64,512]{1,0:T(8,128)(2,1)S(1)} %shard_map.124.pair_ref), channel_id=1, source_target_pairs={{0,24},{4,28},{8,16},{12,20},{16,8},{20,12},{24,0},{28,4},{1,25},{... | collective-permute-start | bytes 196616 | tf_op jit(solution)/shard_map/ppermute | solution.py:263
  54.8 2.0 %collective-permute-start.18 = (bf16[64,512]{1,0:T(8,128)(2,1)S(1)}, bf16[64,512]{1,0:T(8,128)(2,1)S(1)}, u32[]{:S(2)}, u32[]{:S(2)}) collective-permute-start(bf16[64,512]{1,0:T(8,128)(2,1)S(1)} %collective-permute-done.17.refs_0_), channel_id=1, source_target_pairs={{0,4},{4,0},{8,12},{12,8},{16,20},{20,16},{24,28},{28,24},{1,5},{5... | collective-permute-start | bytes 196616 | tf_op jit(solution)/shard_map/ppermute | solution.py:256

commit v4 on v3

--- a/solution.py
+++ b/solution.py
@@ -13,7 +13,7 @@
 STEP = 8
 LOCAL_FLOPS = 1_000_000_000
 CLEAR_FLOPS = 4_000_000_000
-HALVES = 2
+PARTS_OF_WIDTH = (5, 3)
 
 
 def call(body, outs, scratch, args, flops=1024, place=pltpu.VMEM):
@@ -398,9 +398,11 @@
 
 def line_of_four(out_grad, out_weight, merged, x_f, states_of, grads_of):
     rows, width = out_grad.shape
-    cut = width // HALVES
-    spans = [slice(at * cut, (at + 1) * cut) for at in range(HALVES)]
-    piece = [jax.ShapeDtypeStruct((rows, cut), BF16)]
+    unit = width // sum(PARTS_OF_WIDTH)
+    bounds = [sum(PARTS_OF_WIDTH[:at]) * unit for at in range(len(PARTS_OF_WIDTH) + 1)]
+    spans = [slice(*pair) for pair in zip(bounds, bounds[1:])]
+    cuts = [span.stop - span.start for span in spans]
+    piece = [[jax.ShapeDtypeStruct((rows, cut), BF16)] for cut in cuts]
     whole = [jax.ShapeDtypeStruct((rows, width), BF16)]
     pairs_of = lambda ones, twos: [ref for pair in zip(ones, twos) for ref in pair]
 
@@ -409,13 +411,13 @@
 
     shares = []
     second = []
-    for span in spans:
+    for at, span in enumerate(spans):
         (share,) = call(
-            functools.partial(share_body, span), [jax.ShapeDtypeStruct((merged.shape[0], cut), BF16)], [],
+            functools.partial(share_body, span), [jax.ShapeDtypeStruct((merged.shape[0], cuts[at]), BF16)], [],
             [merged, out_weight],
         )
         shares.append(share)
-        (part,) = call(functools.partial(send_body, span, True), piece, [], [share, across])
+        (part,) = call(functools.partial(send_body, span, True), piece[at], [], [share, across])
         second.append(outer(part))
         merged = lax.optimization_barrier((merged, part))[0]
     beside = lax.optimization_barrier((beside, part))[0]
@@ -425,25 +427,25 @@
     second[0] = lax.optimization_barrier((second[0], g_near))[0]
     third = []
     to_far = []
-    for at in range(HALVES):
-        (sent,) = call(functools.partial(add_body, True), piece, [], [shares[at], second[at]])
+    for at in range(len(spans)):
+        (sent,) = call(functools.partial(add_body, True), piece[at], [], [shares[at], second[at]])
         to_far.append(inner(sent))
         far = lax.optimization_barrier((across_far[at], sent))[0]
-        (sent,) = call(functools.partial(send_body, slice(None), False), piece, [], [shares[at], far])
+        (sent,) = call(functools.partial(send_body, slice(None), False), piece[at], [], [shares[at], far])
         third.append(outer(sent))
-        if at + 1 < HALVES:
+        if at + 1 < len(spans):
             states = states_of(lax.optimization_barrier((x_f, sent))[0])
             second[at + 1] = lax.optimization_barrier((second[at + 1], *states))[0]
     g_far = []
     ready = []
     for at, span in enumerate(spans):
         g_far = call(
-            functools.partial(far_body, span), g_rows, [pltpu.VMEM((2 * rows, cut), BF16)],
+            functools.partial(far_body, span), g_rows, [pltpu.VMEM((2 * rows, cuts[at]), BF16)],
             [second[at], third[at], across, across_far[at], out_weight, *g_far],
         )
         if at == 0:
             got = lax.optimization_barrier((to_far[0], *g_far))[0]
-            ready = call(functools.partial(last_body, [slice(None)]), piece, [], [shares[0], got])
+            ready = call(functools.partial(last_body, [slice(None)]), piece[0], [], [shares[0], got])
             third[-1] = lax.optimization_barrier((third[-1], *ready))[0]
     ready = call(functools.partial(last_body, spans), whole, [], [*ready, shares[-1], to_far[-1]])[0]
     (near,) = call(functools.partial(add_whole_body, spans), whole, [], pairs_of(shares, third))

time: 59.4 us -> 59.3 us (level)
  starting transfers between devices: 31.3 us -> 30.2 us
  waiting for transfers between devices: 11.8 us -> 12.8 us
    ppermute x6, starting transfers between devices: 19.9 us -> 18.8 us  [outer(): return lax.ppermute(array, 'tp', [(0, 1), (1, 0), (2, 3), (3, 2)])]
    ppermute x6, waiting for transfers between devices: 3.41 us -> 4.43 us  [outer(): return lax.ppermute(array, 'tp', [(0, 1), (1, 0), (2, 3), (3, 2)])]
where the time goes in v4:
time: 59.3 us; the launch traced here: 59.1 us
  starting transfers between devices  30.2 us (51%)
  Pallas kernels  15 us (25%)
  waiting for transfers between devices  12.8 us (22%)
  between operations  0.96 us (2%)
    ppermute x6, starting transfers between devices, outer(): return lax.ppermute(array, 'tp', [(0, 1), (1, 0), (2, 3), (3, 2)])  18.8 us
    pallas_call x25, Pallas kernels, call(): pl.pallas_call(body, out_shape=outs, in_specs=[whole] * len(args), out_sp...  15 us
    ppermute x6, starting transfers between devices, inner(): return lax.ppermute(array, 'tp', [(1, 2), (2, 1), (0, 0), (3, 3)])  5.2 us
    ppermute x6, waiting for transfers between devices, outer(): return lax.ppermute(array, 'tp', [(0, 1), (1, 0), (2, 3), (3, 2)])  4.43 us
    ppermute x2, starting transfers between devices, from_pairs(): lax.ppermute(array, 'ctx', [(i, i ^ (4 if i % 2 else 2)) for i in range(b...  3.16 us
    ppermute x2, waiting for transfers between devices, from_pairs(): corner = lax.ppermute(array, 'ctx', [(i, i ^ 6) for i in range(blocks)])  3.14 us
    ppermute x2, starting transfers between devices, from_pairs(): corner = lax.ppermute(array, 'ctx', [(i, i ^ 6) for i in range(blocks)])  2.93 us
    ppermute x2, waiting for transfers between devices, from_pairs(): lax.ppermute(array, 'ctx', [(i, i ^ (4 if i % 2 else 2)) for i in range(b...  2.64 us
  transfers between devices with their start and end apart: 20, of which 9 were waited for; matrix products, arithmetic and copies ran while one was open for 0% of the time, Pallas kernels for 24%

profile of v4, /device:TPU:0, one launch (start us, length us, event | category | flops | bytes accessed | tf_op | source)
XLA Modules:
  0.0 59.1 jit_solution(18372915084488642061)
XLA Ops:
  0.7 1.8 %collective-permute-start.4 = (bf16[32,8192]{1,0:T(8,128)(2,1)}, bf16[32,8192]{1,0:T(8,128)(2,1)S(1)}, u32[]{:S(2)}, u32[]{:S(2)}) collective-permute-start(bf16[32,8192]{1,0:T(8,128)(2,1)} %own_ref.1), channel_id=1, source_target_pairs={{1,2},{2,1},{0,0},{3,3},{5,6},{6,5},{4,4},{7,7},{9,10},{10,9},{8,8... | collective-permute-start | bytes 1572872 | tf_op jit(solution)/shard_map/ppermute | solution.py:279
  2.5 4.9 %collective-permute-start.6 = (bf16[32,8192]{1,0:T(8,128)(2,1)}, bf16[32,8192]{1,0:T(8,128)(2,1)S(1)}, u32[]{:S(2)}, u32[]{:S(2)}) collective-permute-start(bf16[32,8192]{1,0:T(8,128)(2,1)} %own_ref.1), channel_id=1, source_target_pairs={{0,1},{1,0},{2,3},{3,2},{4,5},{5,4},{6,7},{7,6},{8,9},{9,8},{10,11... | collective-permute-start | bytes 1572872 | tf_op jit(solution)/shard_map/ppermute | solution.py:275
  8.1 1.2 %collective-permute-done.other_ref = f32[32,512]{1,0:T(8,128)S(1)} collective-permute-done((f32[32,512]{1,0:T(8,128)S(1)}, f32[32,512]{1,0:T(8,128)S(1)}, u32[]{:S(2)}, u32[]{:S(2)}) %collective-permute-start) | collective-permute-done | bytes 65568 | tf_op jit(solution)/shard_map/ppermute | solution.py:256
  9.4 1.6 %collective-permute-start.1 = (bf16[32,512]{1,0:T(8,128)(2,1)S(1)}, bf16[32,512]{1,0:T(8,128)(2,1)S(1)}, u32[]{:S(2)}, u32[]{:S(2)}) collective-permute-start(bf16[32,512]{1,0:T(8,128)(2,1)S(1)} %shard_map.104), channel_id=1, source_target_pairs={{0,8},{4,20},{8,0},{12,28},{16,24},{20,4},{24,16},{28,12},{1,9},{5... | collective-permute-start | bytes 98312 | tf_op jit(solution)/shard_map/ppermute | solution.py:262
  10.9 1.5 %collective-permute-start.3 = (bf16[32,512]{1,0:T(8,128)(2,1)S(1)}, bf16[32,512]{1,0:T(8,128)(2,1)S(1)}, u32[]{:S(2)}, u32[]{:S(2)}) collective-permute-start(bf16[32,512]{1,0:T(8,128)(2,1)S(1)} %shard_map.104), channel_id=1, source_target_pairs={{0,24},{4,28},{8,16},{12,20},{16,8},{20,12},{24,0},{28,4},{1,25},{... | collective-permute-start | bytes 98312 | tf_op jit(solution)/shard_map/ppermute | solution.py:263
  12.4 0.9 %collective-permute-done.1.refs_0_ = bf16[32,512]{1,0:T(8,128)(2,1)S(1)} collective-permute-done((bf16[32,512]{1,0:T(8,128)(2,1)S(1)}, bf16[32,512]{1,0:T(8,128)(2,1)S(1)}, u32[]{:S(2)}, u32[]{:S(2)}) %collective-permute-start.1) | collective-permute-done | bytes 32800 | tf_op jit(solution)/shard_map/ppermute | solution.py:262
  13.4 2.4 %collective-permute-done.3.refs_2_ = bf16[32,512]{1,0:T(8,128)(2,1)S(1)} collective-permute-done((bf16[32,512]{1,0:T(8,128)(2,1)S(1)}, bf16[32,512]{1,0:T(8,128)(2,1)S(1)}, u32[]{:S(2)}, u32[]{:S(2)}) %collective-permute-start.3) | collective-permute-done | bytes 32800 | tf_op jit(solution)/shard_map/ppermute | solution.py:263
  15.7 1.2 %shard_map.105 = (bf16[128,512]{1,0:T(8,128)(2,1)S(1)}, f32[32,512]{1,0:T(8,128)S(1)}) custom-call(f32[128,512]{1,0:T(8,128)S(1)} %get-tuple-element.41.x_f, f32[56,512]{1,0:T(8,128)S(1)} %shard_map.103.table_ref, f32[32,512]{1,0:T(8,128)S(1)} %collective-permute-done.other_ref, bf16[32,512]{1,0:T(8,128)(2,1)S(1)} %collective-permute-done.1.refs_0_, ...), custom_call_target="tpu_custom_call" | custom-call | flops 1024 | bytes 1024 | tf_op jit(solution)/shard_map/pallas_call | solution.py:21
  17.0 0.9 %shard_map.106.share_ref.refs_0_ = bf16[128,5120]{1,0:T(8,128)(2,1)S(1)} custom-call(bf16[128,512]{1,0:T(8,128)(2,1)S(1)} %get-tuple-element.36.merged_ref, bf16[512,8192]{1,0:T(8,128)(2,1)S(1)} %copy-done), custom_call_target="tpu_custom_call" | custom-call | flops 1024 | bytes 1024 | tf_op jit(solution)/shard_map/pallas_call | solution.py:21
  18.5 1.8 %collective-permute-start.5 = (bf16[32,5120]{1,0:T(8,128)(2,1)S(1)}, bf16[32,5120]{1,0:T(8,128)(2,1)S(1)}, u32[]{:S(2)}, u32[]{:S(2)}) collective-permute-start(bf16[32,5120]{1,0:T(8,128)(2,1)S(1)} %shard_map.107), channel_id=1, source_target_pairs={{0,1},{1,0},{2,3},{3,2},{4,5},{5,4},{6,7},{7,6},{8,9},{9,8},{10,11... | collective-permute-start | bytes 983048 | tf_op jit(solution)/shard_map/ppermute | solution.py:275
  20.3 0.7 %collective-permute-start.8 = (bf16[32,5120]{1,0:T(8,128)(2,1)S(1)}, bf16[32,5120]{1,0:T(8,128)(2,1)S(1)}, u32[]{:S(2)}, u32[]{:S(2)}) collective-permute-start(bf16[32,5120]{1,0:T(8,128)(2,1)S(1)} %slice.6), channel_id=1, source_target_pairs={{1,2},{2,1},{0,0},{3,3},{5,6},{6,5},{4,4},{7,7},{9,10},{10,9},{8,8... | collective-permute-start | bytes 983048 | tf_op jit(solution)/shard_map/ppermute | solution.py:279
  21.0 2.9 %collective-permute-start.10 = (bf16[32,3072]{1,0:T(8,128)(2,1)S(1)}, bf16[32,3072]{1,0:T(8,128)(2,1)S(1)}, u32[]{:S(2)}, u32[]{:S(2)}) collective-permute-start(bf16[32,3072]{1,0:T(8,128)(2,1)S(1)} %shard_map.109), channel_id=1, source_target_pairs={{0,1},{1,0},{2,3},{3,2},{4,5},{5,4},{6,7},{7,6},{8,9},{9,8},{10,11... | collective-permute-start | bytes 589832 | tf_op jit(solution)/shard_map/ppermute | solution.py:275
  23.9 0.7 %collective-permute-start.12 = (bf16[32,3072]{1,0:T(8,128)(2,1)S(1)}, bf16[32,3072]{1,0:T(8,128)(2,1)S(1)}, u32[]{:S(2)}, u32[]{:S(2)}) collective-permute-start(bf16[32,3072]{1,0:T(8,128)(2,1)S(1)} %slice.7), channel_id=1, source_target_pairs={{1,2},{2,1},{0,0},{3,3},{5,6},{6,5},{4,4},{7,7},{9,10},{10,9},{8,8... | collective-permute-start | bytes 589832 | tf_op jit(solution)/shard_map/ppermute | solution.py:279
  24.6 2.6 %shard_map.110.refs_0_ = f32[64,512]{1,0:T(8,128)S(1)} custom-call(bf16[32,8192]{1,0:T(8,128)(2,1)S(1)} %copy-done.1, bf16[32,8192]{1,0:T(8,128)(2,1)S(1)} %collective-permute-done.6.beside_ref, bf16[512,8192]{1,0:T(8,128)(2,1)S(1)} %copy-done), custom_call_target="tpu_custom_call" | custom-call | flops 1024 | bytes 1024 | tf_op jit(solution)/shard_map/pallas_call | solution.py:21
  27.3 2.0 %collective-permute-done.5.got_ref.second_ref = bf16[32,5120]{1,0:T(8,128)(2,1)S(1)} collective-permute-done((bf16[32,5120]{1,0:T(8,128)(2,1)S(1)}, bf16[32,5120]{1,0:T(8,128)(2,1)S(1)}, u32[]{:S(2)}, u32[]{:S(2)}) %collective-permute-start.5) | collective-permute-done | bytes 327712 | tf_op jit(solution)/shard_map/ppermute | solution.py:275
  29.4 4.0 %collective-permute-start.9 = (bf16[32,5120]{1,0:T(8,128)(2,1)S(1)}, bf16[32,5120]{1,0:T(8,128)(2,1)S(1)}, u32[]{:S(2)}, u32[]{:S(2)}) collective-permute-start(bf16[32,5120]{1,0:T(8,128)(2,1)S(1)} %shard_map.112), channel_id=1, source_target_pairs={{0,1},{1,0},{2,3},{3,2},{4,5},{5,4},{6,7},{7,6},{8,9},{9,8},{10,11... | collective-permute-start | bytes 983048 | tf_op jit(solution)/shard_map/ppermute | solution.py:275
  34.0 0.9 %shard_map.115 = (f32[2048,512]{1,0:T(8,128)S(1)}, f32[2048,512]{1,0:T(8,128)S(1)}) custom-call(f32[128,512]{1,0:T(8,128)S(1)} %get-tuple-element.41.x_f, f32[56,512]{1,0:T(8,128)S(1)} %shard_map.103.table_ref, f32[32,512]{1,0:T(8,128)S(1)} %get-tuple-element.42.start_ref), custom_call_target="tpu_custom_call" | custom-call | flops 1024 | bytes 1024 | tf_op jit(solution)/shard_map/pallas_call | solution.py:21
  35.1 2.5 %collective-permute-start.13 = (bf16[32,3072]{1,0:T(8,128)(2,1)S(1)}, bf16[32,3072]{1,0:T(8,128)(2,1)S(1)}, u32[]{:S(2)}, u32[]{:S(2)}) collective-permute-start(bf16[32,3072]{1,0:T(8,128)(2,1)S(1)} %shard_map.118), channel_id=1, source_target_pairs={{0,1},{1,0},{2,3},{3,2},{4,5},{5,4},{6,7},{7,6},{8,9},{9,8},{10,11... | collective-permute-start | bytes 589832 | tf_op jit(solution)/shard_map/ppermute | solution.py:275
  38.3 2.2 %collective-permute-done.9.third_ref.refs_1_ = bf16[32,5120]{1,0:T(8,128)(2,1)S(1)} collective-permute-done((bf16[32,5120]{1,0:T(8,128)(2,1)S(1)}, bf16[32,5120]{1,0:T(8,128)(2,1)S(1)}, u32[]{:S(2)}, u32[]{:S(2)}) %collective-permute-start.9) | collective-permute-done | bytes 327712 | tf_op jit(solution)/shard_map/ppermute | solution.py:275
  40.5 1.7 %shard_map.113.refs_0_ = f32[64,512]{1,0:T(8,128)S(1)} custom-call(bf16[32,5120]{1,0:T(8,128)(2,1)S(1)} %collective-permute-done.5.got_ref.second_ref, bf16[32,5120]{1,0:T(8,128)(2,1)S(1)} %collective-permute-done.9.third_ref.refs_1_, bf16[32,8192]{1,0:T(8,128)(2,1)S(1)} %collective-permute-done.4.passing_ref.across_ref, ...), custom_call_target="tpu_custom_call" | custom-call | flops 1024 | bytes 1024 | tf_op jit(solution)/shard_map/pallas_call | solution.py:21
  42.6 1.1 %shard_map.120.refs_1_ = f32[64,512]{1,0:T(8,128)S(1)} custom-call(bf16[32,3072]{1,0:T(8,128)(2,1)S(1)} %collective-permute-done.10.got_ref.second_ref, bf16[32,3072]{1,0:T(8,128)(2,1)S(1)} %collective-permute-done.13.refs_3_.third_ref, bf16[32,8192]{1,0:T(8,128)(2,1)S(1)} %collective-permute-done.4.passing_ref.across_ref, ...), custom_call_target="tpu_custom_call" | custom-call | flops 1024 | bytes 1024 | tf_op jit(solution)/shard_map/pallas_call | solution.py:21
  44.0 2.8 %collective-permute-start.14 = (bf16[32,8192]{1,0:T(8,128)(2,1)S(1)}, bf16[32,8192]{1,0:T(8,128)(2,1)S(1)}, u32[]{:S(2)}, u32[]{:S(2)}) collective-permute-start(bf16[32,8192]{1,0:T(8,128)(2,1)S(1)} %shard_map.117), channel_id=1, source_target_pairs={{0,1},{1,0},{2,3},{3,2},{4,5},{5,4},{6,7},{7,6},{8,9},{9,8},{10,11... | collective-permute-start | bytes 1572872 | tf_op jit(solution)/shard_map/ppermute | solution.py:275
  46.7 0.7 %collective-permute-start.15 = (bf16[32,8192]{1,0:T(8,128)(2,1)S(1)}, bf16[32,8192]{1,0:T(8,128)(2,1)S(1)}, u32[]{:S(2)}, u32[]{:S(2)}) collective-permute-start(bf16[32,8192]{1,0:T(8,128)(2,1)S(1)} %shard_map.119), channel_id=1, source_target_pairs={{1,2},{2,1},{0,0},{3,3},{5,6},{6,5},{4,4},{7,7},{9,10},{10,9},{8,8... | collective-permute-start | bytes 1572872 | tf_op jit(solution)/shard_map/ppermute | solution.py:279
  47.4 1.2 %shard_map.122 = (f32[128,512]{1,0:T(8,128)S(1)}, f32[56,512]{1,0:T(8,128)S(1)}) custom-call(f32[128,512]{1,0:T(8,128)S(1)} %get-tuple-element.41.x_f, f32[56,512]{1,0:T(8,128)S(1)} %shard_map.103.table_ref, f32[2048,512]{1,0:T(8,128)S(1)} %get-tuple-element.43.h_ref, f32[2048,512]{1,0:T(8,128)S(1)} %get-tuple-element.44.q_ref, ...), custom_call_target="tpu_custom_call" | custom-call | flops 1024 | bytes 1024 | tf_op jit(solution)/shard_map/pallas_call | solution.py:21
  48.7 1.3 %collective-permute-done.16.other_ref = f32[56,512]{1,0:T(8,128)S(1)} collective-permute-done((f32[56,512]{1,0:T(8,128)S(1)}, f32[56,512]{1,0:T(8,128)S(1)}, u32[]{:S(2)}, u32[]{:S(2)}) %collective-permute-start.16) | collective-permute-done | bytes 114720 | tf_op jit(solution)/shard_map/ppermute | solution.py:256
  50.0 1.6 %collective-permute-start.17 = (bf16[64,512]{1,0:T(8,128)(2,1)S(1)}, bf16[64,512]{1,0:T(8,128)(2,1)S(1)}, u32[]{:S(2)}, u32[]{:S(2)}) collective-permute-start(bf16[64,512]{1,0:T(8,128)(2,1)S(1)} %shard_map.124.pair_ref), channel_id=1, source_target_pairs={{0,8},{4,20},{8,0},{12,28},{16,24},{20,4},{24,16},{28,12},{1,9},{5... | collective-permute-start | bytes 196616 | tf_op jit(solution)/shard_map/ppermute | solution.py:262
  51.6 1.4 %collective-permute-start.19 = (bf16[64,512]{1,0:T(8,128)(2,1)S(1)}, bf16[64,512]{1,0:T(8,128)(2,1)S(1)}, u32[]{:S(2)}, u32[]{:S(2)}) collective-permute-start(bf16[64,512]{1,0:T(8,128)(2,1)S(1)} %shard_map.124.pair_ref), channel_id=1, source_target_pairs={{0,24},{4,28},{8,16},{12,20},{16,8},{20,12},{24,0},{28,4},{1,25},{... | collective-permute-start | bytes 196616 | tf_op jit(solution)/shard_map/ppermute | solution.py:263
  53.1 1.7 %collective-permute-done.17.refs_0_ = bf16[64,512]{1,0:T(8,128)(2,1)S(1)} collective-permute-done((bf16[64,512]{1,0:T(8,128)(2,1)S(1)}, bf16[64,512]{1,0:T(8,128)(2,1)S(1)}, u32[]{:S(2)}, u32[]{:S(2)}) %collective-permute-start.17) | collective-permute-done | bytes 65568 | tf_op jit(solution)/shard_map/ppermute | solution.py:262
  54.8 1.2 %shard_map.123 = (f32[128,512]{1,0:T(8,128)S(1)}, f32[128,512]{1,0:T(8,128)S(1)}) custom-call(f32[128,512]{1,0:T(8,128)S(1)} %get-tuple-element.51.g_f, f32[56,512]{1,0:T(8,128)S(1)} %shard_map.103.table_ref), custom_call_target="tpu_custom_call" | custom-call | flops 1000000000 | bytes 1024 | tf_op jit(solution)/shard_map/pallas_call | solution.py:21
  56.0 0.8 %collective-permute-done.19.refs_2_ = bf16[64,512]{1,0:T(8,128)(2,1)S(1)} collective-permute-done((bf16[64,512]{1,0:T(8,128)(2,1)S(1)}, bf16[64,512]{1,0:T(8,128)(2,1)S(1)}, u32[]{:S(2)}, u32[]{:S(2)}) %collective-permute-start.19) | collective-permute-done | bytes 65568 | tf_op jit(solution)/shard_map/ppermute | solution.py:263
  56.8 1.3 %shard_map.125 = (bf16[128,512]{1,0:T(8,128)(2,1)}, f32[16,512]{1,0:T(8,128)}, f32[16,512]{1,0:T(8,128)}, f32[1,512]{1,0:T(1,128)}) custom-call(f32[128,512]{1,0:T(8,128)S(1)} %get-tuple-element.52.own_f, f32[128,512]{1,0:T(8,128)S(1)} %get-tuple-element.53.powers_ref, f32[56,512]{1,0:T(8,128)S(1)} %shard_map.103.table_ref, ...), custom_call_target="tpu_custom_call" | custom-call | flops 1024 | bytes 1024 | tf_op jit(solution)/shard_map/pallas_call | solution.py:21
  58.1 1.0 %shard_map.121 = bf16[32,8192]{1,0:T(8,128)(2,1)} custom-call(bf16[128,5120]{1,0:T(8,128)(2,1)S(1)} %shard_map.106.share_ref.refs_0_, bf16[128,3072]{1,0:T(8,128)(2,1)S(1)} %shard_map.108.share_ref.refs_1_.refs_2_, bf16[32,8192]{1,0:T(8,128)(2,1)S(1)} %collective-permute-done.14.refs_2_, bf16[32,8192]{1,0:T(8,128)(2,1)S(1)} %collective-permute-done.15.refs_3_), custom_call_target="tpu_custom_call" | custom-call | flops 1024 | bytes 1024 | tf_op jit(solution)/shard_map/pallas_call | solution.py:21
  (47 shorter events, 3.7 us)
Async XLA Ops:
  0.6 6.7 %copy-start.3 = (f32[512,16]{0,1:T(8,128)S(1)}, f32[512,16]{0,1:T(8,128)}, u32[]{:S(2)}) copy-start(f32[512,16]{0,1:T(8,128)} %param.8) | copy-start | bytes 98308
  0.6 6.7 %copy-start.2 = (bf16[128,512]{1,0:T(8,128)(2,1)S(1)}, bf16[128,512]{1,0:T(8,128)(2,1)}, u32[]{:S(2)}) copy-start(bf16[128,512]{1,0:T(8,128)(2,1)} %x_ref.1) | copy-start | bytes 393220
  0.7 17.2 %collective-permute-start.4 = (bf16[32,8192]{1,0:T(8,128)(2,1)}, bf16[32,8192]{1,0:T(8,128)(2,1)S(1)}, u32[]{:S(2)}, u32[]{:S(2)}) collective-permute-start(bf16[32,8192]{1,0:T(8,128)(2,1)} %own_ref.1), channel_id=1, source_target_pairs={{1,2},{2,1},{0,0},{3,3},{5,6},{6,5},{4,4},{7,7},{9,10},{10,9},{8,8... | collective-permute-start | bytes 1572872 | tf_op jit(solution)/shard_map/ppermute | solution.py:279
  2.5 17.8 %collective-permute-start.6 = (bf16[32,8192]{1,0:T(8,128)(2,1)}, bf16[32,8192]{1,0:T(8,128)(2,1)S(1)}, u32[]{:S(2)}, u32[]{:S(2)}) collective-permute-start(bf16[32,8192]{1,0:T(8,128)(2,1)} %own_ref.1), channel_id=1, source_target_pairs={{0,1},{1,0},{2,3},{3,2},{4,5},{5,4},{6,7},{7,6},{8,9},{9,8},{10,11... | collective-permute-start | bytes 1572872 | tf_op jit(solution)/shard_map/ppermute | solution.py:275
  7.4 6.0 %copy-start.4 = (f32[512,16]{0,1:T(8,128)S(1)}, f32[512,16]{0,1:T(8,128)}, u32[]{:S(2)}) copy-start(f32[512,16]{0,1:T(8,128)} %param.7) | copy-start | bytes 98308
  7.4 6.0 %copy-start.5 = (f32[512]{0:T(512)S(1)}, f32[512]{0:T(512)}, u32[]{:S(2)}) copy-start(f32[512]{0:T(512)} %param.9) | copy-start | bytes 6148
  7.4 9.6 %copy-start = (bf16[512,8192]{1,0:T(8,128)(2,1)S(1)}, bf16[512,8192]{1,0:T(8,128)(2,1)}, u32[]{:S(2)}) copy-start(bf16[512,8192]{1,0:T(8,128)(2,1)} %weight_ref.9) | copy-start | bytes 25165828
  8.0 1.3 %collective-permute-start = (f32[32,512]{1,0:T(8,128)S(1)}, f32[32,512]{1,0:T(8,128)S(1)}, u32[]{:S(2)}, u32[]{:S(2)}) collective-permute-start(f32[32,512]{1,0:T(8,128)S(1)} %get-tuple-element.34.own_ref), channel_id=1, source_target_pairs={{0,4},{4,0},{8,12},{12,8},{16,20},{20,16},{24,28},{28,24},{1,5},{5... | collective-permute-start | bytes 196616 | tf_op jit(solution)/shard_map/ppermute | solution.py:256
  9.4 4.0 %collective-permute-start.1 = (bf16[32,512]{1,0:T(8,128)(2,1)S(1)}, bf16[32,512]{1,0:T(8,128)(2,1)S(1)}, u32[]{:S(2)}, u32[]{:S(2)}) collective-permute-start(bf16[32,512]{1,0:T(8,128)(2,1)S(1)} %shard_map.104), channel_id=1, source_target_pairs={{0,8},{4,20},{8,0},{12,28},{16,24},{20,4},{24,16},{28,12},{1,9},{5... | collective-permute-start | bytes 98312 | tf_op jit(solution)/shard_map/ppermute | solution.py:262
  10.9 4.8 %collective-permute-start.3 = (bf16[32,512]{1,0:T(8,128)(2,1)S(1)}, bf16[32,512]{1,0:T(8,128)(2,1)S(1)}, u32[]{:S(2)}, u32[]{:S(2)}) collective-permute-start(bf16[32,512]{1,0:T(8,128)(2,1)S(1)} %shard_map.104), channel_id=1, source_target_pairs={{0,24},{4,28},{8,16},{12,20},{16,8},{20,12},{24,0},{28,4},{1,25},{... | collective-permute-start | bytes 98312 | tf_op jit(solution)/shard_map/ppermute | solution.py:263
  13.3 2.4 %collective-permute-start.2 = (bf16[32,512]{1,0:T(8,128)(2,1)S(1)}, bf16[32,512]{1,0:T(8,128)(2,1)S(1)}, u32[]{:S(2)}, u32[]{:S(2)}) collective-permute-start(bf16[32,512]{1,0:T(8,128)(2,1)S(1)} %collective-permute-done.1.refs_0_), channel_id=1, source_target_pairs={{0,4},{4,0},{8,12},{12,8},{16,20},{20,16},{24,28},{28,24},{1,5},{5... | collective-permute-start | bytes 98312 | tf_op jit(solution)/shard_map/ppermute | solution.py:256
  17.9 6.7 %copy-start.1 = (bf16[32,8192]{1,0:T(8,128)(2,1)S(1)}, bf16[32,8192]{1,0:T(8,128)(2,1)}, u32[]{:S(2)}) copy-start(bf16[32,8192]{1,0:T(8,128)(2,1)} %own_ref.1) | copy-start | bytes 1572868
  18.5 10.7 %collective-permute-start.5 = (bf16[32,5120]{1,0:T(8,128)(2,1)S(1)}, bf16[32,5120]{1,0:T(8,128)(2,1)S(1)}, u32[]{:S(2)}, u32[]{:S(2)}) collective-permute-start(bf16[32,5120]{1,0:T(8,128)(2,1)S(1)} %shard_map.107), channel_id=1, source_target_pairs={{0,1},{1,0},{2,3},{3,2},{4,5},{5,4},{6,7},{7,6},{8,9},{9,8},{10,11... | collective-permute-start | bytes 983048 | tf_op jit(solution)/shard_map/ppermute | solution.py:275
  20.3 9.0 %collective-permute-start.8 = (bf16[32,5120]{1,0:T(8,128)(2,1)S(1)}, bf16[32,5120]{1,0:T(8,128)(2,1)S(1)}, u32[]{:S(2)}, u32[]{:S(2)}) collective-permute-start(bf16[32,5120]{1,0:T(8,128)(2,1)S(1)} %slice.6), channel_id=1, source_target_pairs={{1,2},{2,1},{0,0},{3,3},{5,6},{6,5},{4,4},{7,7},{9,10},{10,9},{8,8... | collective-permute-start | bytes 983048 | tf_op jit(solution)/shard_map/ppermute | solution.py:279
  21.0 13.9 %collective-permute-start.10 = (bf16[32,3072]{1,0:T(8,128)(2,1)S(1)}, bf16[32,3072]{1,0:T(8,128)(2,1)S(1)}, u32[]{:S(2)}, u32[]{:S(2)}) collective-permute-start(bf16[32,3072]{1,0:T(8,128)(2,1)S(1)} %shard_map.109), channel_id=1, source_target_pairs={{0,1},{1,0},{2,3},{3,2},{4,5},{5,4},{6,7},{7,6},{8,9},{9,8},{10,11... | collective-permute-start | bytes 589832 | tf_op jit(solution)/shard_map/ppermute | solution.py:275
  23.9 11.1 %collective-permute-start.12 = (bf16[32,3072]{1,0:T(8,128)(2,1)S(1)}, bf16[32,3072]{1,0:T(8,128)(2,1)S(1)}, u32[]{:S(2)}, u32[]{:S(2)}) collective-permute-start(bf16[32,3072]{1,0:T(8,128)(2,1)S(1)} %slice.7), channel_id=1, source_target_pairs={{1,2},{2,1},{0,0},{3,3},{5,6},{6,5},{4,4},{7,7},{9,10},{10,9},{8,8... | collective-permute-start | bytes 589832 | tf_op jit(solution)/shard_map/ppermute | solution.py:279
  29.4 11.1 %collective-permute-start.9 = (bf16[32,5120]{1,0:T(8,128)(2,1)S(1)}, bf16[32,5120]{1,0:T(8,128)(2,1)S(1)}, u32[]{:S(2)}, u32[]{:S(2)}) collective-permute-start(bf16[32,5120]{1,0:T(8,128)(2,1)S(1)} %shard_map.112), channel_id=1, source_target_pairs={{0,1},{1,0},{2,3},{3,2},{4,5},{5,4},{6,7},{7,6},{8,9},{9,8},{10,11... | collective-permute-start | bytes 983048 | tf_op jit(solution)/shard_map/ppermute | solution.py:275
  33.3 8.9 %collective-permute-start.7 = (bf16[32,5120]{1,0:T(8,128)(2,1)S(1)}, bf16[32,5120]{1,0:T(8,128)(2,1)S(1)}, u32[]{:S(2)}, u32[]{:S(2)}) collective-permute-start(bf16[32,5120]{1,0:T(8,128)(2,1)S(1)} %shard_map.111), channel_id=1, source_target_pairs={{1,2},{2,1},{0,0},{3,3},{5,6},{6,5},{4,4},{7,7},{9,10},{10,9},{8,8... | collective-permute-start | bytes 983048 | tf_op jit(solution)/shard_map/ppermute | solution.py:279
  35.1 7.5 %collective-permute-start.13 = (bf16[32,3072]{1,0:T(8,128)(2,1)S(1)}, bf16[32,3072]{1,0:T(8,128)(2,1)S(1)}, u32[]{:S(2)}, u32[]{:S(2)}) collective-permute-start(bf16[32,3072]{1,0:T(8,128)(2,1)S(1)} %shard_map.118), channel_id=1, source_target_pairs={{0,1},{1,0},{2,3},{3,2},{4,5},{5,4},{6,7},{7,6},{8,9},{9,8},{10,11... | collective-permute-start | bytes 589832 | tf_op jit(solution)/shard_map/ppermute | solution.py:275
  37.6 6.2 %collective-permute-start.11 = (bf16[32,3072]{1,0:T(8,128)(2,1)S(1)}, bf16[32,3072]{1,0:T(8,128)(2,1)S(1)}, u32[]{:S(2)}, u32[]{:S(2)}) collective-permute-start(bf16[32,3072]{1,0:T(8,128)(2,1)S(1)} %shard_map.116), channel_id=1, source_target_pairs={{1,2},{2,1},{0,0},{3,3},{5,6},{6,5},{4,4},{7,7},{9,10},{10,9},{8,8... | collective-permute-start | bytes 589832 | tf_op jit(solution)/shard_map/ppermute | solution.py:279
  44.0 14.2 %collective-permute-start.14 = (bf16[32,8192]{1,0:T(8,128)(2,1)S(1)}, bf16[32,8192]{1,0:T(8,128)(2,1)S(1)}, u32[]{:S(2)}, u32[]{:S(2)}) collective-permute-start(bf16[32,8192]{1,0:T(8,128)(2,1)S(1)} %shard_map.117), channel_id=1, source_target_pairs={{0,1},{1,0},{2,3},{3,2},{4,5},{5,4},{6,7},{7,6},{8,9},{9,8},{10,11... | collective-permute-start | bytes 1572872 | tf_op jit(solution)/shard_map/ppermute | solution.py:275
  46.7 11.4 %collective-permute-start.15 = (bf16[32,8192]{1,0:T(8,128)(2,1)S(1)}, bf16[32,8192]{1,0:T(8,128)(2,1)S(1)}, u32[]{:S(2)}, u32[]{:S(2)}) collective-permute-start(bf16[32,8192]{1,0:T(8,128)(2,1)S(1)} %shard_map.119), channel_id=1, source_target_pairs={{1,2},{2,1},{0,0},{3,3},{5,6},{6,5},{4,4},{7,7},{9,10},{10,9},{8,8... | collective-permute-start | bytes 1572872 | tf_op jit(solution)/shard_map/ppermute | solution.py:279
  48.6 1.4 %collective-permute-start.16 = (f32[56,512]{1,0:T(8,128)S(1)}, f32[56,512]{1,0:T(8,128)S(1)}, u32[]{:S(2)}, u32[]{:S(2)}) collective-permute-start(f32[56,512]{1,0:T(8,128)S(1)} %get-tuple-element.54.own_ref), channel_id=1, source_target_pairs={{0,4},{4,0},{8,12},{12,8},{16,20},{20,16},{24,28},{28,24},{1,5},{5... | collective-permute-start | bytes 344072 | tf_op jit(solution)/shard_map/ppermute | solution.py:256
  50.0 4.8 %collective-permute-start.17 = (bf16[64,512]{1,0:T(8,128)(2,1)S(1)}, bf16[64,512]{1,0:T(8,128)(2,1)S(1)}, u32[]{:S(2)}, u32[]{:S(2)}) collective-permute-start(bf16[64,512]{1,0:T(8,128)(2,1)S(1)} %shard_map.124.pair_ref), channel_id=1, source_target_pairs={{0,8},{4,20},{8,0},{12,28},{16,24},{20,4},{24,16},{28,12},{1,9},{5... | collective-permute-start | bytes 196616 | tf_op jit(solution)/shard_map/ppermute | solution.py:262
  51.6 5.2 %collective-permute-start.19 = (bf16[64,512]{1,0:T(8,128)(2,1)S(1)}, bf16[64,512]{1,0:T(8,128)(2,1)S(1)}, u32[]{:S(2)}, u32[]{:S(2)}) collective-permute-start(bf16[64,512]{1,0:T(8,128)(2,1)S(1)} %shard_map.124.pair_ref), channel_id=1, source_target_pairs={{0,24},{4,28},{8,16},{12,20},{16,8},{20,12},{24,0},{28,4},{1,25},{... | collective-permute-start | bytes 196616 | tf_op jit(solution)/shard_map/ppermute | solution.py:263
  54.8 2.0 %collective-permute-start.18 = (bf16[64,512]{1,0:T(8,128)(2,1)S(1)}, bf16[64,512]{1,0:T(8,128)(2,1)S(1)}, u32[]{:S(2)}, u32[]{:S(2)}) collective-permute-start(bf16[64,512]{1,0:T(8,128)(2,1)S(1)} %collective-permute-done.17.refs_0_), channel_id=1, source_target_pairs={{0,4},{4,0},{8,12},{12,8},{16,20},{20,16},{24,28},{28,24},{1,5},{5... | collective-permute-start | bytes 196616 | tf_op jit(solution)/shard_map/ppermute | solution.py:256
